TPU v7x, 256 devices: a whole 4x4x8 slice. The times are simulated.
256 devices in a mesh: kvp: 64 (over z, x, core), tp: 4 (over y).
Axes of the slice: x: 4, y: 4, z: 8, core: 2. Of those that a mesh axis runs over, the one named last changes fastest.
Arguments:
- query: bfloat16 [64, 16384], P('kvp', 'tp'), may hold values from -24 to 24
- draft_kv: bfloat16 [64, 2, 1024], P('kvp', None, 'tp'), may hold values from -8 to 8
- key_cache: bfloat16 [8, 8192, 1024], P(None, 'kvp', 'tp'), may hold values from -8 to 8
- value_cache: bfloat16 [8, 8192, 1024], P(None, 'kvp', 'tp'), may hold values from -24 to 24
- prompt_of: int32 [32], replicated, may hold values from 0 to 7, as said below
- prefix_len: int32 [8], replicated, may hold values from 2048 to 8192, as said below
- out_weight: bfloat16 [16384, 16384], P('tp', 'kvp'), may hold values from -1 to 1
- stream: bfloat16 [64, 16384], P('tp', 'kvp'), may hold values from -6 to 6
- norm_gain: bfloat16 [16384], P('kvp'), may hold values from 0.099609375 to 1.8984375
- gate_up: bfloat16 [2, 26624, 16384], P(None, ('kvp', 'tp')), may hold values from -0.046875 to 0.046875
- down_weight: bfloat16 [26624, 16384], P(('kvp', 'tp')), may hold values from -0.0390625 to 0.0390625
Outputs:
- layer_out: bfloat16 [64, 16384], P('tp', 'kvp')
Inputs may be any that keep to these rules, and one draw needn't show every extreme that they name: `prompt_of`: each prompt id appears for exactly 4 samples. `prefix_len`: some prompt has the full length 8192.
All inputs are finite; a program needn't handle non-finite values.
Results may differ from a plain program's by a relative error of at most 0.01.
Values may be sent and summed in bfloat16 or wider, within the bound.
No kernel may reach another device: no remote copies, remote signals or barrier semaphores. Data moves between devices by JAX's collectives and lax.ppermute only.
A program may use at most 128 MiB of HBM per device.

v0:
```python
import jax
import jax.numpy as jnp
from jax import lax
from jax.sharding import PartitionSpec as P

D = 16384
H = 128
KVH = 8
HD = 128


floor_score = -1e30


def on_device(
    query,
    draft_kv,
    key_cache,
    value_cache,
    prompt_of,
    prefix_len,
    out_weight,
    stream,
    norm_gain,
    gate_up,
    down_weight,
):
    queries_all, draft_all = (
        lax.all_gather(query, "kvp", axis=0, tiled=True),
        lax.all_gather(draft_kv, "kvp", axis=0, tiled=True),
    )
    tokens = queries_all.shape[0]
    groups = H // KVH
    local_heads = key_cache.shape[2] // HD
    prompts = key_cache.shape[0]
    cache_len = key_cache.shape[1]
    row_count = prompt_of.shape[0]
    score_scale = HD ** (-0.5)
    queries = queries_all.reshape(tokens, local_heads, groups, HD)
    token_ids = jnp.arange(tokens, dtype=jnp.int32)
    token_row = token_ids % row_count
    token_step = token_ids // row_count
    row_match = (token_row[:, None] == jnp.arange(row_count, dtype=jnp.int32)[None, :]).astype(
        jnp.int32
    )
    token_prompt = jnp.sum(row_match * prompt_of[None, :], 1)
    prompt_match = (token_prompt[:, None] == jnp.arange(prompts, dtype=jnp.int32)[None, :]).astype(
        jnp.int32
    )
    token_len = jnp.sum(prompt_match * prefix_len[None, :], 1)
    position = lax.axis_index("kvp") * cache_len + jnp.arange(cache_len, dtype=jnp.int32)
    cache_keys = key_cache[token_prompt].reshape(tokens, cache_len, local_heads, HD)
    cache_values = value_cache[token_prompt].reshape(tokens, cache_len, local_heads, HD)
    scores = (
        jnp.einsum("tkgd,tckd->tkgc", queries, cache_keys, preferred_element_type=jnp.float32)
        * score_scale
    )
    visible = (position[None, :] < token_len[:, None])[:, None, None, :]
    draft_keys = draft_all[:, 0].reshape(tokens, local_heads, HD)
    draft_values = draft_all[:, 1].reshape(tokens, local_heads, HD)
    draft_scores = (
        jnp.einsum("tkgd,ukd->tkgu", queries, draft_keys, preferred_element_type=jnp.float32)
        * score_scale
    )
    device_zero = lax.axis_index("kvp") == 0
    own_draft = (
        (token_row[:, None] == token_row[None, :])
        & (token_step[None, :] <= token_step[:, None])
        & device_zero
    )
    own_draft = own_draft[:, None, None, :]
    local_max = jnp.maximum(
        jnp.max(jnp.where(visible, scores, floor_score), -1),
        jnp.max(jnp.where(own_draft, draft_scores, floor_score), -1),
    )
    shifted = jnp.where(visible, jnp.exp(scores - local_max[..., None]), 0.0)
    draft_weights = jnp.where(own_draft, jnp.exp(draft_scores - local_max[..., None]), 0.0)
    totals = jnp.sum(shifted, -1) + jnp.sum(draft_weights, -1)
    weighted = jnp.einsum(
        "tkgc,tckd->tkgd",
        shifted.astype(jnp.bfloat16),
        cache_values,
        preferred_element_type=jnp.float32,
    )
    weighted = weighted + jnp.einsum(
        "tkgu,ukd->tkgd",
        draft_weights.astype(jnp.bfloat16),
        draft_values,
        preferred_element_type=jnp.float32,
    )
    weighted = weighted.reshape(tokens, local_heads * groups * HD)
    local_max = local_max.reshape(tokens, local_heads * groups)
    totals = totals.reshape(tokens, local_heads * groups)
    global_max = lax.pmax(local_max, "kvp")
    factor = jnp.exp(local_max - global_max)
    summed, total_sum = (
        lax.psum_scatter(
            weighted * jnp.repeat(factor, HD, axis=1), "kvp", scatter_dimension=0, tiled=True
        ),
        lax.psum_scatter(totals * factor, "kvp", scatter_dimension=0, tiled=True),
    )
    attn = (summed / jnp.repeat(total_sum, HD, axis=1)).astype(jnp.bfloat16)
    partial_value = jnp.dot(
        lax.all_gather(attn, "kvp", axis=0, tiled=True),
        out_weight,
        preferred_element_type=jnp.float32,
    )
    projected = lax.psum_scatter(partial_value, "tp", scatter_dimension=0, tiled=True)
    middle = stream.astype(jnp.float32) + projected
    square_sum = lax.psum(jnp.sum(middle * middle, 1), "kvp")
    normed = (
        middle * lax.rsqrt(square_sum / D + 1e-05)[:, None] * norm_gain.astype(jnp.float32)
    ).astype(jnp.bfloat16)
    normed_cols = lax.all_gather(normed, "kvp", axis=1, tiled=True)
    shard_rows = lax.all_gather(normed_cols, "tp", axis=0, tiled=True)
    gate_value = lax.dot_general(
        shard_rows, gate_up[0], (((1,), (1,)), ((), ())), preferred_element_type=jnp.float32
    )
    up_value = lax.dot_general(
        shard_rows, gate_up[1], (((1,), (1,)), ((), ())), preferred_element_type=jnp.float32
    )
    hidden = (jax.nn.silu(gate_value) * up_value).astype(jnp.bfloat16)
    partial_out = jnp.dot(hidden, down_weight, preferred_element_type=jnp.float32)
    reduced = lax.psum_scatter(partial_out, "kvp", scatter_dimension=1, tiled=True)
    reduced = lax.psum_scatter(reduced, "tp", scatter_dimension=0, tiled=True)
    return (middle + reduced).astype(jnp.bfloat16)


def solution(mesh):
    in_specs = (
        P("kvp", "tp"),
        P("kvp", None, "tp"),
        P(None, "kvp", "tp"),
        P(None, "kvp", "tp"),
        P(),
        P(),
        P("tp", "kvp"),
        P("tp", "kvp"),
        P("kvp"),
        P(None, ("kvp", "tp"), None),
        P(("kvp", "tp"), None),
    )
    out_specs = P("tp", "kvp")
    return jax.shard_map(
        on_device, mesh=mesh, in_specs=in_specs, out_specs=out_specs, check_vma=False
    )
```

profile of v0, /device:TPU:8, one launch (start us, length us, event | category | flops | bytes accessed | tf_op | source)
XLA Modules:
  0.0 1109.5 jit_solution(296417602780646372)
XLA Ops:
  6.5 0.0 copy-start
  6.5 0.9 select_reduce_fusion.2
  7.4 0.9 select_reduce_fusion.3
  8.3 0.0 copy-start.8
  8.3 58.6 %all-gather = bf16[64,1,4096]{2,1,0:T(2,128)(2,1)} all-gather(bf16[1,1,4096]{2,1,0:T(2,128)(2,1)} %bitcast.94), channel_id=1, replica_groups=mesh['kvp'=64,'tp'=4] {'kvp'}, dimensions={0}, use_global_device_ids=true | all-gather | bytes 532480 | tf_op jit(solution)/shard_map/all_gather | solution.py:29
  67.0 5.1 reduce.1
  72.1 1.9 copy.98
  74.0 0.1 broadcast_compare_fusion
  74.1 0.0 copy-start.5
  74.1 3.8 gather_fusion
  77.9 5.6 select_reduce_fusion.1
  83.5 0.1 copy.82
  83.6 42.4 %all_gather.16 = bf16[64,2,256]{2,1,0:T(2,128)(2,1)S(1)} all-gather(bf16[1,2,256]{2,1,0:T(2,128)(2,1)S(1)} %copy-done.9), channel_id=1, replica_groups=mesh['kvp'=64,'tp'=4] {'kvp'}, dimensions={0}, use_global_device_ids=true | all-gather | bytes 66560 | tf_op jit(solution)/shard_map/all_gather | solution.py:30
  126.0 0.9 slice_reduce_fusion
  126.8 0.1 and_and_fusion
  126.9 0.0 copy-start.3
  126.9 2.7 select_reduce_fusion
  129.6 0.1 copy.83
  129.7 1.9 bitcast_reduce_fusion
  131.6 0.7 copy.88
  132.3 2.3 fusion.29
  134.6 248.9 %pmax.7 = f32[64,32]{0,1:T(8,128)S(1)} all-reduce(f32[64,32]{0,1:T(8,128)S(1)} %bitcast.91), channel_id=1, replica_groups=mesh['kvp'=64,'tp'=4] {'kvp'}, use_global_device_ids=true, to_apply=%region_4.5 | all-reduce | flops 2048 | bytes 16384 | tf_op jit(solution)/shard_map/pmax | solution.py:94
  383.5 0.7 add.86
  384.2 0.6 bitcast_multiply_fusion.1
  384.8 0.1 copy.87
  384.9 2.6 copy.85
  387.5 3.9 gather_fusion.1
  391.4 1.3 convolution_bitcast_fusion
  392.7 3.8 fusion.12
  396.5 0.3 broadcast_in_dim.70
  396.8 0.0 copy-start.4
  396.8 0.0 copy-start.10
  396.8 2.6 bitcast_multiply_fusion
  399.5 0.0 all-reduce.4.cloned.1.call-update
  399.5 0.0 reduce-scatter.5.cloned.1.call-start
  399.6 0.0 copy-done.11
  399.6 0.6 dynamic-slice
  400.1 246.3 %all-reduce.1 = f32[64,32]{0,1:T(8,128)S(1)} all-reduce(f32[64,32]{0,1:T(8,128)S(1)} %copy-done.7), channel_id=3, replica_groups=mesh['kvp'=64,'tp'=4] {'kvp'}, use_global_device_ids=true, to_apply=%region_8.9.clone | all-reduce | flops 2048 | bytes 16384
  646.5 0.8 dynamic-slice_reduce_fusion
  647.3 0.0 all-reduce.4.cloned.1.call-done
  647.3 0.1 broadcast_in_dim.71
  647.4 1.6 convert_bitcast_fusion
  649.0 47.2 %all-gather.1 = bf16[64,1,4096]{2,1,0:T(2,128)(2,1)S(1)} all-gather(bf16[1,1,4096]{2,1,0:T(2,128)(2,1)S(1)} %convert_bitcast_fusion), channel_id=1, replica_groups=mesh['kvp'=64,'tp'=4] {'kvp'}, dimensions={0}, use_global_device_ids=true | all-gather | bytes 532480 | tf_op jit(solution)/shard_map/all_gather | solution.py:104
  696.1 3.0 fusion.30
  699.1 0.0 reduce-scatter.5.cloned.1.call-update
  699.1 0.0 all-gather.4.cloned.1.call-start
  699.2 19.7 %reduce-scatter.5.cloned.1.call-done = f32[16,256]{1,0:T(8,128)} async-done(((f32[64,256]{1,0:T(8,128)}), f32[16,256]{1,0:T(8,128)}) %reduce-scatter.5.cloned.1.call-update) | async-done | bytes 16400 | tf_op jit(solution)/shard_map/reduce_scatter | solution.py:108
  718.9 0.0 copy-done.4
  718.9 0.8 multiply_reduce_fusion
  719.7 127.2 %psum.7 = f32[16]{0:T(128)S(1)} all-reduce(f32[16]{0:T(128)S(1)} %multiply_reduce_fusion), channel_id=1, replica_groups=mesh['kvp'=64,'tp'=4] {'kvp'}, use_global_device_ids=true, to_apply=%region_11.12 | all-reduce | flops 16 | bytes 128 | tf_op jit(solution)/shard_map/psum | solution.py:110
  847.0 0.8 multiply_convert_fusion
  847.7 44.5 %all_gather.18 = bf16[16,16384]{1,0:T(8,128)(2,1)} all-gather(bf16[16,256]{1,0:T(8,128)(2,1)S(1)} %multiply_convert_fusion), channel_id=1, replica_groups=mesh['kvp'=64,'tp'=4] {'kvp'}, dimensions={1}, use_global_device_ids=true | all-gather | bytes 532480 | tf_op jit(solution)/shard_map/all_gather | solution.py:114
  892.2 0.0 all-gather.4.cloned.1.call-update
  892.2 0.3 reduce-scatter.7.cloned.1.call-start
  892.5 31.1 %all-gather.4.cloned.1.call-done = bf16[64,16384]{1,0:T(8,128)(2,1)} async-done(((bf16[16,16384]{1,0:T(8,128)(2,1)}), bf16[64,16384]{1,0:T(8,128)(2,1)}) %all-gather.4.cloned.1.call-update) | async-done | bytes 2097168 | tf_op jit(solution)/shard_map/all_gather | solution.py:115
  923.6 3.9 fusion.8
  927.5 7.3 fusion.26
  934.8 0.0 reduce-scatter.7.cloned.1.call-update
  934.8 0.0 reduce-scatter.9.cloned.1.call-start
  934.9 145.0 %reduce-scatter.7.cloned.1.call-done = f32[64,256]{1,0:T(8,128)} async-done(((f32[64,16384]{1,0:T(8,128)}), f32[64,256]{1,0:T(8,128)}) %reduce-scatter.7.cloned.1.call-update) | async-done | bytes 65552 | tf_op jit(solution)/shard_map/reduce_scatter | solution.py:124
  1079.8 0.0 reduce-scatter.9.cloned.1.call-update
  1079.8 21.8 %reduce-scatter.9.cloned.1.call-done = f32[16,256]{1,0:T(8,128)} async-done(((f32[64,256]{1,0:T(8,128)}), f32[16,256]{1,0:T(8,128)}) %reduce-scatter.9.cloned.1.call-update) | async-done | bytes 16400 | tf_op jit(solution)/shard_map/reduce_scatter | solution.py:125
  1101.7 0.0 copy-done.1
  1101.7 1.3 add_convert_fusion
  (24 shorter events, 0.1 us)
Async XLA Ops:
  6.5 921.0 %copy-start = (bf16[104,16384]{1,0:T(8,128)(2,1)S(1)}, bf16[104,16384]{1,0:T(8,128)(2,1)}, u32[]{:S(2)}) copy-start(bf16[104,16384]{1,0:T(8,128)(2,1)} %param.21) | copy-start | bytes 10223620
  6.5 640.8 %all-reduce.4.cloned.1.call-start = ((), (), s32[]{:S(2)}) async-start(), calls=%async_computation.7 | async-start | bytes 2097152
  8.3 69.6 %copy-start.8 = (s32[1024]{0:T(1024)}, s32[1024]{0:T(1024)S(1)}, u32[]{:S(2)}) copy-start(s32[1024]{0:T(1024)S(1)} %pad_clamp_fusion) | copy-start | bytes 12292
  74.1 3.8 copy-start.5
  77.9 5.7 copy-start.9
  126.9 2.7 copy-start.3
  387.5 3.9 copy-start.2
  387.5 5.2 copy-start.6
  396.5 3.1 copy-start.11
  396.5 3.7 copy-start.7
  396.8 322.1 %copy-start.4 = (bf16[16,256]{1,0:T(8,128)(2,1)S(1)}, bf16[16,256]{1,0:T(8,128)(2,1)}, u32[]{:S(2)}) copy-start(bf16[16,256]{1,0:T(8,128)(2,1)} %param.18) | copy-start | bytes 24580
  396.8 322.9 %copy-start.10 = (bf16[256]{0:T(256)(128)(2,1)S(1)}, bf16[256]{0:T(256)(128)(2,1)}, u32[]{:S(2)}) copy-start(bf16[256]{0:T(256)(128)(2,1)} %param.19) | copy-start | bytes 1540
  399.5 319.4 %reduce-scatter.5.cloned.1.call-start = ((), (), s32[]{:S(2)}) async-start(), calls=%async_computation.3 | async-start | bytes 81920 | tf_op jit(solution)/shard_map/reduce_scatter | solution.py:108
  699.1 224.4 %all-gather.4.cloned.1.call-start = ((), (), s32[]{:S(2)}) async-start(), calls=%async_computation.4 | async-start | bytes 2621440 | tf_op jit(solution)/shard_map/all_gather | solution.py:115
  892.2 187.6 %reduce-scatter.7.cloned.1.call-start = ((), (), s32[]{:S(2)}) async-start(), calls=%async_computation.5 | async-start | bytes 4259840 | tf_op jit(solution)/shard_map/reduce_scatter | solution.py:124
  934.8 166.9 %copy-start.1 = (f32[16,256]{1,0:T(8,128)S(1)}, f32[16,256]{1,0:T(8,128)}, u32[]{:S(2)}) copy-start(f32[16,256]{1,0:T(8,128)} %reduce-scatter.5.cloned.1.call-done) | copy-start | bytes 49156
  934.8 166.9 %reduce-scatter.9.cloned.1.call-start = ((), (), s32[]{:S(2)}) async-start(), calls=%async_computation.6 | async-start | bytes 81920 | tf_op jit(solution)/shard_map/reduce_scatter | solution.py:125
Sparse Core Ops, SparseCore 0:
  399.6 182.1 all-reduce.3
  699.3 19.5 reduce-scatter.4
  892.3 31.1 all-gather.3
  934.9 144.8 reduce-scatter.6
  1082.3 19.3 reduce-scatter.8
where the time goes:
time: 1110 us
  blocking collectives  815 us (73%)
  waiting for transfers between devices  218 us (20%)
  matrix products  27.6 us (2%)
  other arithmetic  19.8 us (2%)
  local copies, waits for them, and re-layouts  15.9 us (1%)
  between operations  13.3 us (1%)
    pmax x1, blocking collectives, on_device(): global_max = lax.pmax(local_max, 'kvp')  249 us
    unnamed x1, blocking collectives  246 us
    reduce_scatter x1, waiting for transfers between devices, on_device(): lax.psum_scatter(partial_out, 'kvp', scatter_dimension=1, tiled=True)  145 us
    psum x1, blocking collectives, on_device(): square_sum = lax.psum(jnp.sum(middle * middle, 1), 'kvp')  127 us
    all_gather x1, blocking collectives, on_device(): lax.all_gather(query, 'kvp', axis=0, tiled=True)  58.6 us
    all_gather x1, blocking collectives, on_device(): lax.all_gather(attn, 'kvp', axis=0, tiled=True)  47.2 us
    all_gather x1, blocking collectives, on_device(): normed_cols = lax.all_gather(normed, 'kvp', axis=1, tiled=True)  44.5 us
    all_gather x1, blocking collectives, on_device(): lax.all_gather(draft_kv, 'kvp', axis=0, tiled=True)  42.4 us
  transfers between devices with their start and end apart: 5, of which 4 were waited for; matrix products, arithmetic and copies ran while one was open for 0% of the time, Pallas kernels for 0%

commit v1 on v0

v1 whole, which is shorter than its diff:
```python
import jax
import jax.numpy as jnp
from jax import lax
from jax.experimental import pallas as pl
from jax.experimental.pallas import tpu as pltpu
from jax.sharding import PartitionSpec as P

D = 16384
HD = 128
NZ, NX, NC, NY = 8, 4, 2, 4
PEERS = NZ * NX
HEADS = 32
GROUP = 16
PROMPTS = 8
TOKS = 64
HALF = 32
SHARD = 128
COLS = 256
EPS = 1e-05
SCALE = HD ** (-0.5)
FLOOR = -1e30
VMEM_LIMIT = 56 * 1024 * 1024

bf16 = jnp.bfloat16
f32 = jnp.float32


def kvp_index(z, x, c):
    return (z * NX + x) * NC + c


def all_index(z, x, c, y):
    return kvp_index(z, x, c) * NY + y


G_XZ = [[kvp_index(z, x, c) for z in range(NZ) for x in range(NX)] for c in range(NC)]
G_Z = [[kvp_index(z, x, c) for z in range(NZ)] for x in range(NX) for c in range(NC)]
G_XY = [
    [all_index(z, x, c, y) for x in range(NX) for y in range(NY)]
    for z in range(NZ)
    for c in range(NC)
]
CORE_PAIRS = [(i, i ^ 1) for i in range(NZ * NX * NC)]


def swap_cores(array):
    return lax.ppermute(array, "kvp", CORE_PAIRS)


def swap_plane(array):
    return lax.all_to_all(array, "kvp", 0, 0, axis_index_groups=G_XZ, tiled=True)


def nt_dot(a, b):
    return lax.dot_general(a, b, (((1,), (1,)), ((), ())), preferred_element_type=f32)


def nn_dot(a, b):
    return jnp.dot(a, b, preferred_element_type=f32)


def lane_ids(shape):
    return lax.broadcasted_iota(jnp.int32, shape, len(shape) - 1)


def row_ids(shape):
    return lax.broadcasted_iota(jnp.int32, shape, len(shape) - 2)


def stats_tile(rows, top, total):
    lanes = lane_ids((rows, HD))
    high = total.astype(bf16).astype(f32)
    low = total - high
    return jnp.where(
        lanes == 0, top, jnp.where(lanes == 1, high, jnp.where(lanes == 2, low, 0.0))
    )


def attention_kernel(
    prompt_ref, len_ref, own_ref, oth_ref, k_ref, v_ref, keep_ref, send_ref, order_ref, gath, count
):
    kvp = lax.axis_index("kvp")
    core = lax.rem(kvp, 2)
    for p in range(PROMPTS):
        count[p] = 0
    for s in range(HALF):
        p = prompt_ref[s]
        seen = jnp.minimum(count[p], 3)
        count[p] = seen + 1
        order_ref[p * 8 + seen] = s
        order_ref[p * 8 + 4 + seen] = s + HALF
    gath[0:PEERS] = own_ref[...]
    gath[PEERS : 2 * PEERS] = oth_ref[...]
    to_row = row_ids((256, 256))
    from_row = lane_ids((256, 256))
    regroup = (
        (to_row // GROUP == from_row % GROUP) & (to_row % GROUP == from_row // GROUP)
    ).astype(bf16)
    position = kvp * SHARD + lane_ids((SHARD, SHARD))
    for pair in range(4):
        out_ref = keep_ref if pair < 2 else send_ref
        for kv in range(2):
            parts = []
            for q_ in range(2):
                p = lax.rem(pair * 2 + q_ + 4 * core, PROMPTS)
                tiles = []
                for j in range(8):
                    t = order_ref[p * 8 + j]
                    row = t // 2 + PEERS * lax.rem(t + core, 2)
                    tiles.append(gath[row, kv * GROUP : (kv + 1) * GROUP, :])
                queries = jnp.concatenate(tiles, axis=0)
                keys = k_ref[p, :, kv * HD : (kv + 1) * HD]
                values = v_ref[p, :, kv * HD : (kv + 1) * HD]
                scores = nt_dot(queries, keys) * SCALE
                visible = position < len_ref[p]
                top = jnp.max(jnp.where(visible, scores, FLOOR), axis=1, keepdims=True)
                top = top.astype(bf16).astype(f32)
                weights = jnp.where(visible, jnp.exp(scores - top), 0.0)
                total = jnp.sum(weights, axis=1, keepdims=True)
                summed = nn_dot(weights.astype(bf16), values)
                parts.append(
                    jnp.concatenate(
                        [summed.astype(bf16), stats_tile(SHARD, top, total).astype(bf16)], axis=1
                    )
                )
            both = nn_dot(regroup, jnp.concatenate(parts, axis=0)).astype(bf16)
            first = (pair % 2) * 16
            for g in range(GROUP):
                out_ref[kv * GROUP + g, first : first + 16, :] = both[g * 16 : (g + 1) * 16, :]


def merge_kernel(a_ref, b_ref, out_ref):
    def step(h, carry):
        a = a_ref[h].astype(f32)
        b = b_ref[h].astype(f32)
        top_a, top_b = a[:, HD : HD + 1], b[:, HD : HD + 1]
        top = jnp.maximum(top_a, top_b)
        fa, fb = jnp.exp(top_a - top), jnp.exp(top_b - top)
        total = fa * (a[:, HD + 1 : HD + 2] + a[:, HD + 2 : HD + 3]) + fb * (
            b[:, HD + 1 : HD + 2] + b[:, HD + 2 : HD + 3]
        )
        out_ref[h, :, :HD] = (fa * a[:, :HD] + fb * b[:, :HD]).astype(bf16)
        out_ref[h, :, HD:] = stats_tile(HALF, top, total).astype(bf16)
        return carry

    lax.fori_loop(0, HEADS, step, 0, unroll=True)


def combine_kernel(order_ref, part_ref, own_ref, oth_ref, out_ref, gath):
    kvp = lax.axis_index("kvp")
    core = lax.rem(kvp, 2)
    head = kvp // 2
    kv = head // GROUP
    gath[0:PEERS] = own_ref[...]
    gath[PEERS : 2 * PEERS] = oth_ref[...]
    first = pl.multiple_of(kv * GROUP, GROUP)
    query_tiles, draft_tiles = [], []
    for s in range(HALF):
        t = order_ref[HALF * core + s]
        row = t // 2 + PEERS * lax.rem(t + core, 2)
        query_tiles.append(gath[row, pl.ds(first, GROUP), :])
        draft_tiles.append(gath[row, HEADS : HEADS + GROUP, :])
    shape = (HALF, HALF * GROUP)
    slot = row_ids(shape)
    other = lane_ids(shape) // GROUP
    inner = lane_ids(shape) % GROUP
    pick = ((slot == other) & (inner == head % GROUP)).astype(bf16)
    queries = nn_dot(pick, jnp.concatenate(query_tiles, axis=0)).astype(bf16)
    drafts = jnp.concatenate(draft_tiles, axis=0)
    scores = nt_dot(queries, drafts) * SCALE
    visible = (
        (slot // 8 == other // 8)
        & (slot % 4 == other % 4)
        & ((other // 4) % 2 <= (slot // 4) % 2)
        & (inner == kv)
    )
    top = jnp.max(jnp.where(visible, scores, FLOOR), axis=1, keepdims=True)
    for i in range(PEERS):
        top = jnp.maximum(top, part_ref[i, :, HD : HD + 1].astype(f32))
    weights = jnp.where(visible, jnp.exp(scores - top), 0.0)
    total = jnp.sum(weights, axis=1, keepdims=True)
    summed = nn_dot(pltpu.roll(weights, 2, 1).astype(bf16), drafts)
    for i in range(PEERS):
        part = part_ref[i].astype(f32)
        factor = jnp.exp(part[:, HD : HD + 1] - top)
        total = total + factor * (part[:, HD + 1 : HD + 2] + part[:, HD + 2 : HD + 3])
        summed = summed + factor * part[:, :HD]
    attn = (summed / total).astype(bf16)
    for i in range(PEERS):
        out_ref[i] = attn


def project_kernel(order_ref, own_ref, oth_ref, w_ref, stream_ref, out_ref, by_slot, by_token):
    kvp = lax.axis_index("kvp")
    core = lax.rem(kvp, 2)
    tp = lax.axis_index("tp")
    acc = jnp.zeros((TOKS, COLS), f32)
    for i in range(HEADS // 2):
        lhs = jnp.concatenate(
            [
                jnp.concatenate([own_ref[2 * i], own_ref[2 * i + 1]], axis=1),
                jnp.concatenate([oth_ref[2 * i], oth_ref[2 * i + 1]], axis=1),
            ],
            axis=0,
        )
        acc = acc + nn_dot(lhs, w_ref[2 * i * HD : (2 * i + 2) * HD, :])
    by_slot[...] = acc
    for r in range(TOKS):
        t = order_ref[lax.rem(r + HALF * core, TOKS)]
        by_token[pl.ds(t, 1), :] = by_slot[r : r + 1, :]
    mine = pl.ds(pl.multiple_of(tp * 16, 16), 16)
    by_token[mine, :] = by_token[mine, :] + stream_ref[...].astype(f32)
    for i in range(NY):
        out_ref[i] = by_token[...]


def norm_kernel(parts_ref, gain_ref, msg_ref, mid_ref, whole):
    tp = lax.axis_index("tp")
    middle = (parts_ref[0] + parts_ref[1]) + (parts_ref[2] + parts_ref[3])
    whole[...] = middle
    mid_ref[...] = whole[pl.ds(pl.multiple_of(tp * 16, 16), 16), :]
    scaled = (middle * gain_ref[...].astype(f32)).astype(bf16)
    squares = jnp.sum(middle * middle, axis=1, keepdims=True)
    high = squares.astype(bf16).astype(f32)
    low = squares - high
    lanes = lane_ids((16, HD))
    stats = jnp.zeros((16, HD), f32)
    for j in range(4):
        stats = jnp.where(lanes == 2 * j, high[16 * j : 16 * j + 16], stats)
        stats = jnp.where(lanes == 2 * j + 1, low[16 * j : 16 * j + 16], stats)
    block = jnp.concatenate(
        [scaled[16 * j : 16 * j + 16] for j in range(4)] + [stats.astype(bf16)], axis=1
    )
    for i in range(PEERS):
        msg_ref[i] = block


def feed_kernel(own_ref, oth_ref, gu_ref, down_ref, send_ref, keep_ref):
    core = lax.rem(lax.axis_index("kvp"), 2)
    gate = jnp.zeros((TOKS, 104), f32)
    up = jnp.zeros((TOKS, 104), f32)
    stats = jnp.zeros((16, HD), f32)
    for i in range(PEERS):
        for src_ref, side in ((own_ref, core), (oth_ref, 1 - core)):
            rows = jnp.concatenate(
                [src_ref[i, :, COLS * j : COLS * (j + 1)] for j in range(4)], axis=0
            )
            cols = pl.ds(pl.multiple_of((2 * i + side) * COLS, COLS), COLS)
            gate = gate + nt_dot(rows, gu_ref[0, :, cols])
            up = up + nt_dot(rows, gu_ref[1, :, cols])
            stats = stats + src_ref[i, :, 4 * COLS :].astype(f32)
    squares = jnp.concatenate(
        [stats[:, 2 * j : 2 * j + 1] + stats[:, 2 * j + 1 : 2 * j + 2] for j in range(4)], axis=0
    )
    rscale = lax.rsqrt(squares / D + EPS)
    gate = gate * rscale
    up = up * rscale
    hidden = (gate / (1.0 + jnp.exp(-gate)) * up).astype(bf16)
    for out_ref, side in ((send_ref, 1 - core), (keep_ref, core)):
        for z in range(NZ):
            for x in range(NX):
                cols = pl.ds(pl.multiple_of((2 * (z * NX + x) + side) * COLS, COLS), COLS)
                part = nn_dot(hidden, down_ref[:, cols]).astype(out_ref.dtype)
                for y in range(NY):
                    out_ref[x * NY + y, z * 16 : (z + 1) * 16, :] = part[16 * y : 16 * y + 16]


VMEM = pl.BlockSpec(memory_space=pltpu.VMEM)
SMEM = pl.BlockSpec(memory_space=pltpu.SMEM)
PARAMS = pltpu.CompilerParams(vmem_limit_bytes=VMEM_LIMIT)


def call(kernel, name, in_specs, out_shape, out_specs, scratch=()):
    return pl.pallas_call(
        kernel,
        name=name,
        in_specs=in_specs,
        out_shape=out_shape,
        out_specs=out_specs,
        scratch_shapes=list(scratch),
        compiler_params=PARAMS,
    )


def on_device(
    query,
    draft_kv,
    key_cache,
    value_cache,
    prompt_of,
    prefix_len,
    out_weight,
    stream,
    norm_gain,
    gate_up,
    down_weight,
):
    shape = jax.ShapeDtypeStruct
    block = jnp.concatenate(
        [query.reshape(HEADS, HD), draft_kv.reshape(4, HD), jnp.zeros((12, HD), bf16)], axis=0
    )
    own = swap_plane(jnp.broadcast_to(block[None], (PEERS, 48, HD)))
    oth = swap_cores(own)
    keep, send, order = call(
        attention_kernel,
        "attention",
        [SMEM, SMEM, VMEM, VMEM, VMEM, VMEM],
        [
            shape((HEADS, HALF, 2 * HD), bf16),
            shape((HEADS, HALF, 2 * HD), bf16),
            shape((TOKS,), jnp.int32),
        ],
        [VMEM, VMEM, SMEM],
        [pltpu.VMEM((2 * PEERS, 48, HD), bf16), pltpu.SMEM((PROMPTS,), jnp.int32)],
    )(prompt_of, prefix_len, own, oth, key_cache, value_cache)
    merged = call(
        merge_kernel, "merge", [VMEM, VMEM], shape((HEADS, HALF, 2 * HD), bf16), VMEM
    )(keep, swap_cores(send))
    attn = call(
        combine_kernel,
        "combine",
        [SMEM, VMEM, VMEM, VMEM],
        shape((PEERS, HALF, HD), bf16),
        VMEM,
        [pltpu.VMEM((2 * PEERS, 48, HD), bf16)],
    )(order, swap_plane(merged), own, oth)
    attn_own = swap_plane(attn)
    attn_oth = swap_cores(attn_own)
    partial = call(
        project_kernel,
        "project",
        [SMEM, VMEM, VMEM, VMEM, VMEM],
        shape((NY, TOKS, COLS), f32),
        VMEM,
        [pltpu.VMEM((TOKS, COLS), f32), pltpu.VMEM((TOKS, COLS), f32)],
    )(order, attn_own, attn_oth, out_weight, stream)
    partial = lax.all_to_all(partial, "tp", 0, 0, tiled=True)
    msg, middle = call(
        norm_kernel,
        "norm",
        [VMEM, VMEM],
        [shape((PEERS, 16, 4 * COLS + HD), bf16), shape((16, COLS), f32)],
        [VMEM, VMEM],
        [pltpu.VMEM((TOKS, COLS), f32)],
    )(partial, norm_gain.reshape(1, COLS))
    normed_own = swap_plane(msg)
    normed_oth = swap_cores(normed_own)
    send, keep = call(
        feed_kernel,
        "feed",
        [VMEM, VMEM, VMEM, VMEM],
        [shape((NX * NY, NZ * 16, COLS), bf16), shape((NX * NY, NZ * 16, COLS), f32)],
        [VMEM, VMEM],
    )(normed_own, normed_oth, gate_up, down_weight)
    summed = (keep + swap_cores(send).astype(f32)).astype(bf16)
    summed = lax.all_to_all(summed, ("kvp", "tp"), 0, 0, axis_index_groups=G_XY, tiled=True)
    summed = jnp.sum(summed.astype(f32), axis=0).astype(bf16).reshape(NZ, 16, COLS)
    summed = lax.all_to_all(summed, "kvp", 0, 0, axis_index_groups=G_Z, tiled=True)
    return (middle + jnp.sum(summed.astype(f32), axis=0)).astype(bf16)


def solution(mesh):
    in_specs = (
        P("kvp", "tp"),
        P("kvp", None, "tp"),
        P(None, "kvp", "tp"),
        P(None, "kvp", "tp"),
        P(),
        P(),
        P("tp", "kvp"),
        P("tp", "kvp"),
        P("kvp"),
        P(None, ("kvp", "tp"), None),
        P(("kvp", "tp"), None),
    )
    out_specs = P("tp", "kvp")
    return jax.shard_map(
        on_device, mesh=mesh, in_specs=in_specs, out_specs=out_specs, check_vma=False
    )
```

time: 1110 us -> 198 us (0.18)
  blocking collectives: 815 us -> 134 us
  waiting for transfers between devices: 218 us -> 15.8 us
  Pallas kernels: 0 us -> 33.2 us
  matrix products: 27.6 us -> 0 us
  other arithmetic: 19.8 us -> 3.56 us
  between operations: 13.3 us -> 0.07 us
    pmax x1 -> x0, blocking collectives: 249 us -> none  [on_device(): global_max = lax.pmax(local_max, 'kvp')]
    unnamed x1 -> x0, blocking collectives: 246 us -> none
    all_gather x4 -> x0, blocking collectives: 193 us -> none  [the longest x1 58.6 us: on_device(): lax.all_gather(query, 'kvp', axis=0, tiled=True)]
    reduce_scatter x3 -> x0, waiting for transfers between devices: 186 us -> none  [the longest x1 145 us: on_device(): lax.psum_scatter(partial_out, 'kvp', scatter_dimension=1, tiled=True)]
    all_to_all x0 -> x6, blocking collectives: none -> 134 us  [the longest x4 103 us: swap_plane(): lax.all_to_all(array, 'kvp', 0, 0, axis_index_groups=G_XZ, tiled=True)]
    psum x1 -> x0, blocking collectives: 127 us -> none  [on_device(): square_sum = lax.psum(jnp.sum(middle * middle, 1), 'kvp')]
    pallas_call x0 -> x6, Pallas kernels: none -> 33.2 us  [the longest x1 9.47 us: on_device(): call(feed_kernel, 'feed', [VMEM, VMEM, VMEM, VMEM], [shape((NX * NY, NZ *...]
    all_gather x1 -> x0, waiting for transfers between devices: 31.1 us -> none  [on_device(): shard_rows = lax.all_gather(normed_cols, 'tp', axis=0, tiled=True)]
  transfers between devices with their start and end apart: 5 -> 6, of which waited for: 4 -> 6; matrix products, arithmetic and copies ran while one was open for 0% -> 0% of each run, Pallas kernels for 0% -> 0%
where the time goes in v1:
time: 198 us; the launch traced here: 197 us
  blocking collectives  134 us (68%)
  Pallas kernels  33.2 us (17%)
  waiting for transfers between devices  15.8 us (8%)
  local copies, waits for them, and re-layouts  5.4 us (3%)
  starting transfers between devices  5.29 us (3%)
  other arithmetic  3.56 us (2%)
    all_to_all x4, blocking collectives, swap_plane(): lax.all_to_all(array, 'kvp', 0, 0, axis_index_groups=G_XZ, tiled=True)  103 us
    all_to_all x1, blocking collectives, on_device(): lax.all_to_all(summed, ('kvp', 'tp'), 0, 0, axis_index_groups=G_XY, tiled...  20.5 us
    ppermute x5, waiting for transfers between devices, swap_cores(): return lax.ppermute(array, 'kvp', CORE_PAIRS)  10.8 us
    all_to_all x1, blocking collectives, on_device(): lax.all_to_all(summed, 'kvp', 0, 0, axis_index_groups=G_Z, tiled=True)  10.8 us
    pallas_call x1, Pallas kernels, on_device(): call(feed_kernel, 'feed', [VMEM, VMEM, VMEM, VMEM], [shape((NX * NY, NZ *...  9.47 us
    pallas_call x1, Pallas kernels, on_device(): call(merge_kernel, 'merge', [VMEM, VMEM], shape((HEADS, HALF, 2 * HD), bf...  8.21 us
    pallas_call x1, Pallas kernels, on_device(): call(attention_kernel, 'attention', [SMEM, SMEM, VMEM, VMEM, VMEM, VMEM],...  6.44 us
    all_to_all x1, waiting for transfers between devices, on_device(): partial = lax.all_to_all(partial, 'tp', 0, 0, tiled=True)  4.94 us
  transfers between devices with their start and end apart: 6, of which 6 were waited for; matrix products, arithmetic and copies ran while one was open for 0% of the time, Pallas kernels for 0%

profile of v1, /device:TPU:8, one launch (start us, length us, event | category | flops | bytes accessed | tf_op | source)
XLA Modules:
  0.0 197.1 jit_solution(17161283421981702066)
XLA Ops:
  0.0 0.7 reshape.14
  0.7 0.1 pad.2.clone
  0.8 0.8 reduce.1
  1.5 0.1 maximum_maximum_fusion
  1.6 0.1 broadcast_in_dim.10
  1.7 26.5 %all_to_all.35.own_ref = bf16[32,48,128]{2,1,0:T(8,128)(2,1)S(1)} all-to-all(bf16[32,48,128]{2,1,0:T(8,128)(2,1)S(1)} %broadcast_in_dim.10), channel_id=1, replica_groups={{0,8,16,24,32,40,48,56,64,72,80,88,96,104,112,120,128,136,144,152,160,1..., dimensions={0} | all-to-all | bytes 786432 | tf_op jit(solution)/shard_map/all_to_all | solution.py:51
  28.1 0.0 copy-start.1
  28.1 0.0 collective-permute-start
  28.1 1.7 collective-permute-done.oth_ref
  29.9 0.0 copy-done.1
  29.9 0.0 copy-start.2
  29.9 0.7 copy-done.2
  30.6 6.4 %attention.1 = (bf16[32,32,256]{2,1,0:T(8,128)(2,1)}, bf16[32,32,256]{2,1,0:T(8,128)(2,1)}, s32[64]{0:T(128)}) custom-call(s32[32]{0:T(128)} %prompt_ref.1, s32[8]{0:T(128)} %len_ref.1, bf16[32,48,128]{2,1,0:T(8,128)(2,1)} %copy-done.1, bf16[32,48,128]{2,1,0:T(8,128)(2,1)} %copy-done.2, bf16[8,128,256]{2,1,0:T(8,128)(2,1)} %k_ref.1, bf16[8,128,256]{2,1,0:T(8,128)(2,1)} %v_ref.1), custom_call_target="tpu_custom_call" | custom-call | tf_op jit(solution)/shard_map/attention/pallas_call | solution.py:304
  37.1 0.2 collective-permute-start.1
  37.3 2.0 %collective-permute-done.1.b_ref = bf16[32,32,256]{2,1,0:T(8,128)(2,1)S(1)} collective-permute-done((bf16[32,32,256]{2,1,0:T(8,128)(2,1)}, bf16[32,32,256]{2,1,0:T(8,128)(2,1)S(1)}, u32[]{:S(2)}, u32[]{:S(2)}) %collective-permute-start.1) | collective-permute-done | bytes 524320 | tf_op jit(solution)/shard_map/ppermute | solution.py:47
  39.3 0.0 copy-start.6
  39.3 0.8 copy-done.6
  40.1 8.2 %merge.1 = bf16[32,32,256]{2,1,0:T(8,128)(2,1)} custom-call(bf16[32,32,256]{2,1,0:T(8,128)(2,1)} %get-tuple-element.13.a_ref, bf16[32,32,256]{2,1,0:T(8,128)(2,1)} %copy-done.6), custom_call_target="tpu_custom_call" | custom-call | tf_op jit(solution)/shard_map/merge/pallas_call | solution.py:316
  48.3 22.9 %all_to_all.36.part_ref = bf16[32,32,256]{2,1,0:T(8,128)(2,1)} all-to-all(bf16[32,32,256]{2,1,0:T(8,128)(2,1)} %merge.1), channel_id=1, replica_groups={{0,8,16,24,32,40,48,56,64,72,80,88,96,104,112,120,128,136,144,152,160,1..., dimensions={0} | all-to-all | bytes 1048576 | tf_op jit(solution)/shard_map/all_to_all | solution.py:51
  71.2 3.9 %combine.1 = bf16[32,32,128]{2,1,0:T(8,128)(2,1)} custom-call(s32[64]{0:T(128)} %get-tuple-element.12.order_ref, bf16[32,32,256]{2,1,0:T(8,128)(2,1)} %all_to_all.36.part_ref, bf16[32,48,128]{2,1,0:T(8,128)(2,1)} %copy-done.1, bf16[32,48,128]{2,1,0:T(8,128)(2,1)} %copy-done.2), custom_call_target="tpu_custom_call" | custom-call | tf_op jit(solution)/shard_map/combine/pallas_call | solution.py:319
  75.1 0.0 copy-start.9
  75.1 17.2 %all_to_all.37.own_ref = bf16[32,32,128]{2,1,0:T(8,128)(2,1)S(1)} all-to-all(bf16[32,32,128]{2,1,0:T(8,128)(2,1)} %combine.1), channel_id=1, replica_groups={{0,8,16,24,32,40,48,56,64,72,80,88,96,104,112,120,128,136,144,152,160,1..., dimensions={0} | all-to-all | bytes 524288 | tf_op jit(solution)/shard_map/all_to_all | solution.py:51
  92.2 0.0 copy-start.4
  92.2 0.0 collective-permute-start.2
  92.2 1.5 collective-permute-done.2.oth_ref
  93.8 0.0 copy-done.4
  93.8 0.0 copy-start.7
  93.8 0.7 copy-done.7
  94.5 3.1 %project.1 = f32[4,64,256]{2,1,0:T(8,128)} custom-call(s32[64]{0:T(128)} %get-tuple-element.12.order_ref, bf16[32,32,128]{2,1,0:T(8,128)(2,1)} %copy-done.4, bf16[32,32,128]{2,1,0:T(8,128)(2,1)} %copy-done.7, bf16[4096,256]{1,0:T(8,128)(2,1)} %w_ref.1, bf16[16,256]{1,0:T(8,128)(2,1)} %stream_ref.1), custom_call_target="tpu_custom_call" | custom-call | tf_op jit(solution)/shard_map/project/pallas_call | solution.py:329
  97.6 4.9 %all-to-all-start.3 = ((f32[4,64,256]{2,1,0:T(8,128)}), f32[4,64,256]{2,1,0:T(8,128)S(1)}, u32[]{:S(2)}, u32[]{:S(2)}) async-start(f32[4,64,256]{2,1,0:T(8,128)} %project.1), calls=%async_computation.3 | async-start | bytes 524288 | tf_op jit(solution)/shard_map/all_to_all | solution.py:337
  102.5 0.0 copy-done.9
  102.5 0.6 reshape.15.gain_ref
  103.0 4.9 %all-to-all-done.3.parts_ref = f32[4,64,256]{2,1,0:T(8,128)S(1)} async-done(((f32[4,64,256]{2,1,0:T(8,128)}), f32[4,64,256]{2,1,0:T(8,128)S(1)}, u32[]{:S(2)}, u32[]{:S(2)}) %all-to-all-start.3) | async-done | bytes 262176 | tf_op jit(solution)/shard_map/all_to_all | solution.py:337
  108.0 0.0 copy-start.5
  108.0 0.7 copy-done.5
  108.7 2.1 %norm.1 = (bf16[32,16,1152]{2,1,0:T(8,128)(2,1)}, f32[16,256]{1,0:T(8,128)}) custom-call(f32[4,64,256]{2,1,0:T(8,128)} %copy-done.5, bf16[1,256]{1,0:T(2,128)(2,1)} %reshape.15.gain_ref), custom_call_target="tpu_custom_call" | custom-call | tf_op jit(solution)/shard_map/norm/pallas_call | solution.py:338
  110.8 36.1 %all_to_all.38.own_ref = bf16[32,16,1152]{2,1,0:T(8,128)(2,1)S(1)} all-to-all(bf16[32,16,1152]{2,1,0:T(8,128)(2,1)} %get-tuple-element.16), channel_id=1, replica_groups={{0,8,16,24,32,40,48,56,64,72,80,88,96,104,112,120,128,136,144,152,160,1..., dimensions={0} | all-to-all | bytes 2359296 | tf_op jit(solution)/shard_map/all_to_all | solution.py:51
  146.9 0.0 copy-start
  146.9 0.0 collective-permute-start.3
  146.9 2.8 %collective-permute-done.3.oth_ref = bf16[32,16,1152]{2,1,0:T(8,128)(2,1)S(1)} collective-permute-done((bf16[32,16,1152]{2,1,0:T(8,128)(2,1)S(1)}, bf16[32,16,1152]{2,1,0:T(8,128)(2,1)S(1)}, u32[]{:S(2)}, u32[]{:S(2)}) %collective-permute-start.3) | collective-permute-done | bytes 1179680 | tf_op jit(solution)/shard_map/ppermute | solution.py:47
  149.7 0.0 copy-done
  149.7 0.0 copy-start.3
  149.7 1.0 copy-done.3
  150.7 9.5 %feed.1 = (bf16[16,128,256]{2,1,0:T(8,128)(2,1)}, f32[16,128,256]{2,1,0:T(8,128)}) custom-call(bf16[32,16,1152]{2,1,0:T(8,128)(2,1)} %copy-done, bf16[32,16,1152]{2,1,0:T(8,128)(2,1)} %copy-done.3, bf16[2,104,16384]{2,1,0:T(8,128)(2,1)} %gu_ref.1, bf16[104,16384]{1,0:T(8,128)(2,1)} %down_ref.1), custom_call_target="tpu_custom_call" | custom-call | tf_op jit(solution)/shard_map/feed/pallas_call | solution.py:348
  160.2 0.1 collective-permute-start.4
  160.4 2.7 %collective-permute-done.4 = bf16[16,128,256]{2,1,0:T(8,128)(2,1)S(1)} collective-permute-done((bf16[16,128,256]{2,1,0:T(8,128)(2,1)}, bf16[16,128,256]{2,1,0:T(8,128)(2,1)S(1)}, u32[]{:S(2)}, u32[]{:S(2)}) %collective-permute-start.4) | collective-permute-done | bytes 1048608 | tf_op jit(solution)/shard_map/ppermute | solution.py:47
  163.1 2.0 add_convert_fusion
  165.0 0.0 copy-start.8
  165.1 20.5 %all_to_all.39 = bf16[16,128,256]{2,1,0:T(8,128)(2,1)S(1)} all-to-all(bf16[16,128,256]{2,1,0:T(8,128)(2,1)S(1)} %add_convert_fusion), channel_id=1, replica_groups={{0,1,2,3,8,9,10,11,16,17,18,19,24,25,26,27},{4,5,6,7,12,13,14,15,20,21,..., dimensions={0} | all-to-all | bytes 2097152 | tf_op jit(solution)/shard_map/all_to_all | solution.py:356
  185.6 0.1 reduce_sum.21
  185.7 10.8 %all_to_all.40 = bf16[8,16,256]{2,1,0:T(8,128)(2,1)S(1)} all-to-all(bf16[8,16,256]{2,1,0:T(8,128)(2,1)S(1)} %bitcast.2), channel_id=1, replica_groups={{0,32,64,96,128,160,192,224},{4,36,68,100,132,164,196,228},{8,40,72,104..., dimensions={0} | all-to-all | bytes 131072 | tf_op jit(solution)/shard_map/all_to_all | solution.py:358
  196.5 0.0 copy-done.8
  196.5 0.6 add_convert_fusion.1
  (2 shorter events, 0.0 us)
Async XLA Ops:
  28.1 1.7 copy-start.1
  28.1 1.7 collective-permute-start
  29.9 0.7 copy-start.2
  37.1 2.2 %collective-permute-start.1 = (bf16[32,32,256]{2,1,0:T(8,128)(2,1)}, bf16[32,32,256]{2,1,0:T(8,128)(2,1)S(1)}, u32[]{:S(2)}, u32[]{:S(2)}) collective-permute-start(bf16[32,32,256]{2,1,0:T(8,128)(2,1)} %get-tuple-element.14), channel_id=1, source_target_pairs={{0,4},{4,0},{8,12},{12,8},{16,20},{20,16},{24,28},{28,24},{32,36},... | collective-permute-start | bytes 1572872 | tf_op jit(solution)/shard_map/ppermute | solution.py:47
  39.3 0.8 copy-start.6
  75.1 27.4 %copy-start.9 = (bf16[256]{0:T(256)(128)(2,1)S(1)}, bf16[256]{0:T(256)(128)(2,1)}, u32[]{:S(2)}) copy-start(bf16[256]{0:T(256)(128)(2,1)} %param.19) | copy-start | bytes 1540
  92.2 1.5 copy-start.4
  92.2 1.5 collective-permute-start.2
  93.8 0.7 copy-start.7
  97.6 10.4 %all-to-all-start.3 = ((f32[4,64,256]{2,1,0:T(8,128)}), f32[4,64,256]{2,1,0:T(8,128)S(1)}, u32[]{:S(2)}, u32[]{:S(2)}) async-start(f32[4,64,256]{2,1,0:T(8,128)} %project.1), calls=%async_computation.3 | async-start | bytes 524288 | tf_op jit(solution)/shard_map/all_to_all | solution.py:337
  108.0 0.7 copy-start.5
  146.9 2.9 %copy-start = (bf16[32,16,1152]{2,1,0:T(8,128)(2,1)}, bf16[32,16,1152]{2,1,0:T(8,128)(2,1)S(1)}, u32[]{:S(2)}) copy-start(bf16[32,16,1152]{2,1,0:T(8,128)(2,1)S(1)} %all_to_all.38.own_ref) | copy-start | bytes 3538948
  146.9 2.8 %collective-permute-start.3 = (bf16[32,16,1152]{2,1,0:T(8,128)(2,1)S(1)}, bf16[32,16,1152]{2,1,0:T(8,128)(2,1)S(1)}, u32[]{:S(2)}, u32[]{:S(2)}) collective-permute-start(bf16[32,16,1152]{2,1,0:T(8,128)(2,1)S(1)} %all_to_all.38.own_ref), channel_id=1, source_target_pairs={{0,4},{4,0},{8,12},{12,8},{16,20},{20,16},{24,28},{28,24},{32,36},... | collective-permute-start | bytes 3538952 | tf_op jit(solution)/shard_map/ppermute | solution.py:47
  149.7 1.0 copy-start.3
  160.2 2.9 %collective-permute-start.4 = (bf16[16,128,256]{2,1,0:T(8,128)(2,1)}, bf16[16,128,256]{2,1,0:T(8,128)(2,1)S(1)}, u32[]{:S(2)}, u32[]{:S(2)}) collective-permute-start(bf16[16,128,256]{2,1,0:T(8,128)(2,1)} %get-tuple-element.18), channel_id=1, source_target_pairs={{0,4},{4,0},{8,12},{12,8},{16,20},{20,16},{24,28},{28,24},{32,36},... | collective-permute-start | bytes 3145736 | tf_op jit(solution)/shard_map/ppermute | solution.py:47
  165.0 31.4 %copy-start.8 = (f32[16,256]{1,0:T(8,128)S(1)}, f32[16,256]{1,0:T(8,128)}, u32[]{:S(2)}) copy-start(f32[16,256]{1,0:T(8,128)} %get-tuple-element.15) | copy-start | bytes 49156

commit v2 on v1

--- a/solution.py
+++ b/solution.py
@@ -19,7 +19,7 @@
 EPS = 1e-05
 SCALE = HD ** (-0.5)
 FLOOR = -1e30
-VMEM_LIMIT = 56 * 1024 * 1024
+VMEM_LIMIT = 24 * 1024 * 1024
 
 bf16 = jnp.bfloat16
 f32 = jnp.float32
@@ -77,7 +77,7 @@
 
 
 def attention_kernel(
-    prompt_ref, len_ref, own_ref, oth_ref, k_ref, v_ref, keep_ref, send_ref, order_ref, gath, count
+    prompt_ref, len_ref, own_ref, oth_ref, k_ref, v_ref, k2_ref, v2_ref, out_ref, order_ref, gath, count
 ):
     kvp = lax.axis_index("kvp")
     core = lax.rem(kvp, 2)
@@ -96,21 +96,23 @@
     regroup = (
         (to_row // GROUP == from_row % GROUP) & (to_row % GROUP == from_row // GROUP)
     ).astype(bf16)
-    position = kvp * SHARD + lane_ids((SHARD, SHARD))
-    for pair in range(4):
-        out_ref = keep_ref if pair < 2 else send_ref
+    here = kvp * SHARD + lane_ids((SHARD, SHARD))
+    there = (kvp + 1 - 2 * core) * SHARD + lane_ids((SHARD, SHARD))
+    position = jnp.concatenate([here, there], axis=1)
+    for pair in range(2):
         for kv in range(2):
+            cols = slice(kv * HD, (kv + 1) * HD)
             parts = []
             for q_ in range(2):
-                p = lax.rem(pair * 2 + q_ + 4 * core, PROMPTS)
+                p = pair * 2 + q_ + 4 * core
                 tiles = []
                 for j in range(8):
                     t = order_ref[p * 8 + j]
                     row = t // 2 + PEERS * lax.rem(t + core, 2)
                     tiles.append(gath[row, kv * GROUP : (kv + 1) * GROUP, :])
                 queries = jnp.concatenate(tiles, axis=0)
-                keys = k_ref[p, :, kv * HD : (kv + 1) * HD]
-                values = v_ref[p, :, kv * HD : (kv + 1) * HD]
+                keys = jnp.concatenate([k_ref[p, :, cols], k2_ref[p, :, cols]], axis=0)
+                values = jnp.concatenate([v_ref[p, :, cols], v2_ref[p, :, cols]], axis=0)
                 scores = nt_dot(queries, keys) * SCALE
                 visible = position < len_ref[p]
                 top = jnp.max(jnp.where(visible, scores, FLOOR), axis=1, keepdims=True)
@@ -124,26 +126,10 @@
                     )
                 )
             both = nn_dot(regroup, jnp.concatenate(parts, axis=0)).astype(bf16)
-            first = (pair % 2) * 16
             for g in range(GROUP):
-                out_ref[kv * GROUP + g, first : first + 16, :] = both[g * 16 : (g + 1) * 16, :]
-
-
-def merge_kernel(a_ref, b_ref, out_ref):
-    def step(h, carry):
-        a = a_ref[h].astype(f32)
-        b = b_ref[h].astype(f32)
-        top_a, top_b = a[:, HD : HD + 1], b[:, HD : HD + 1]
-        top = jnp.maximum(top_a, top_b)
-        fa, fb = jnp.exp(top_a - top), jnp.exp(top_b - top)
-        total = fa * (a[:, HD + 1 : HD + 2] + a[:, HD + 2 : HD + 3]) + fb * (
-            b[:, HD + 1 : HD + 2] + b[:, HD + 2 : HD + 3]
-        )
-        out_ref[h, :, :HD] = (fa * a[:, :HD] + fb * b[:, :HD]).astype(bf16)
-        out_ref[h, :, HD:] = stats_tile(HALF, top, total).astype(bf16)
-        return carry
-
-    lax.fori_loop(0, HEADS, step, 0, unroll=True)
+                out_ref[kv * GROUP + g, pair * 16 : pair * 16 + 16, :] = both[
+                    g * 16 : (g + 1) * 16, :
+                ]
 
 
 def combine_kernel(order_ref, part_ref, own_ref, oth_ref, out_ref, gath):
@@ -296,26 +282,20 @@
     down_weight,
 ):
     shape = jax.ShapeDtypeStruct
+    key_pair, value_pair = swap_cores(key_cache), swap_cores(value_cache)
     block = jnp.concatenate(
         [query.reshape(HEADS, HD), draft_kv.reshape(4, HD), jnp.zeros((12, HD), bf16)], axis=0
     )
     own = swap_plane(jnp.broadcast_to(block[None], (PEERS, 48, HD)))
     oth = swap_cores(own)
-    keep, send, order = call(
+    part, order = call(
         attention_kernel,
         "attention",
-        [SMEM, SMEM, VMEM, VMEM, VMEM, VMEM],
-        [
-            shape((HEADS, HALF, 2 * HD), bf16),
-            shape((HEADS, HALF, 2 * HD), bf16),
-            shape((TOKS,), jnp.int32),
-        ],
-        [VMEM, VMEM, SMEM],
+        [SMEM, SMEM, VMEM, VMEM, VMEM, VMEM, VMEM, VMEM],
+        [shape((HEADS, HALF, 2 * HD), bf16), shape((TOKS,), jnp.int32)],
+        [VMEM, SMEM],
         [pltpu.VMEM((2 * PEERS, 48, HD), bf16), pltpu.SMEM((PROMPTS,), jnp.int32)],
-    )(prompt_of, prefix_len, own, oth, key_cache, value_cache)
-    merged = call(
-        merge_kernel, "merge", [VMEM, VMEM], shape((HEADS, HALF, 2 * HD), bf16), VMEM
-    )(keep, swap_cores(send))
+    )(prompt_of, prefix_len, own, oth, key_cache, value_cache, key_pair, value_pair)
     attn = call(
         combine_kernel,
         "combine",
@@ -323,7 +303,7 @@
         shape((PEERS, HALF, HD), bf16),
         VMEM,
         [pltpu.VMEM((2 * PEERS, 48, HD), bf16)],
-    )(order, swap_plane(merged), own, oth)
+    )(order, swap_plane(part), own, oth)
     attn_own = swap_plane(attn)
     attn_oth = swap_cores(attn_own)
     partial = call(

time: 198 us -> 174 us (0.88)
  blocking collectives: 134 us -> 106 us
  Pallas kernels: 33.2 us -> 11.2 us
  waiting for transfers between devices: 15.8 us -> 29 us
  starting transfers between devices: 5.29 us -> 17.1 us
  local copies, waits for them, and re-layouts: 5.4 us -> 8.62 us
    all_to_all x4 -> x3, blocking collectives: 103 us -> 74.3 us  [swap_plane(): lax.all_to_all(array, 'kvp', 0, 0, axis_index_groups=G_XZ, tiled=True)]
    all_to_all x0 -> x1, waiting for transfers between devices: none -> 14.7 us  [swap_plane(): lax.all_to_all(array, 'kvp', 0, 0, axis_index_groups=G_XZ, tiled=True)]
    pallas_call x2 -> x1, Pallas kernels: 14.7 us -> 3.06 us  [on_device(): call(attention_kernel, 'attention', [SMEM, SMEM, VMEM, VMEM, VMEM, VMEM,...]
    all_to_all x0 -> x1, starting transfers between devices: none -> 11.3 us  [swap_plane(): lax.all_to_all(array, 'kvp', 0, 0, axis_index_groups=G_XZ, tiled=True)]
    pallas_call x1, Pallas kernels: 9.47 us -> 3.4 us  [on_device(): call(feed_kernel, 'feed', [VMEM, VMEM, VMEM, VMEM], [shape((NX * NY, NZ *...]
    unnamed x20, local copies, waits for them, and re-layouts: 4.01 us -> 7.05 us
    ppermute x5 -> x6, waiting for transfers between devices: 10.8 us -> 8.61 us  [swap_cores(): return lax.ppermute(array, 'kvp', CORE_PAIRS)]
  transfers between devices with their start and end apart: 6 -> 8, of which waited for: 6 -> 6; matrix products, arithmetic and copies ran while one was open for 0% -> 0% of each run, Pallas kernels for 0% -> 0%
where the time goes in v2:
time: 174 us; the launch traced here: 173 us
  blocking collectives  106 us (61%)
  waiting for transfers between devices  29 us (17%)
  starting transfers between devices  17.1 us (10%)
  Pallas kernels  11.2 us (6%)
  local copies, waits for them, and re-layouts  8.62 us (5%)
  other arithmetic  1.88 us (1%)
    all_to_all x3, blocking collectives, swap_plane(): lax.all_to_all(array, 'kvp', 0, 0, axis_index_groups=G_XZ, tiled=True)  74.3 us
    all_to_all x1, blocking collectives, on_device(): lax.all_to_all(summed, ('kvp', 'tp'), 0, 0, axis_index_groups=G_XY, tiled...  20.5 us
    all_to_all x1, waiting for transfers between devices, swap_plane(): lax.all_to_all(array, 'kvp', 0, 0, axis_index_groups=G_XZ, tiled=True)  14.7 us
    all_to_all x1, starting transfers between devices, swap_plane(): lax.all_to_all(array, 'kvp', 0, 0, axis_index_groups=G_XZ, tiled=True)  11.3 us
    all_to_all x1, blocking collectives, on_device(): lax.all_to_all(summed, 'kvp', 0, 0, axis_index_groups=G_Z, tiled=True)  10.8 us
    ppermute x6, waiting for transfers between devices, swap_cores(): return lax.ppermute(array, 'kvp', CORE_PAIRS)  8.61 us
    unnamed x20, local copies, waits for them, and re-layouts  7.05 us
    all_to_all x1, waiting for transfers between devices, on_device(): partial = lax.all_to_all(partial, 'tp', 0, 0, tiled=True)  5.61 us
  transfers between devices with their start and end apart: 8, of which 6 were waited for; matrix products, arithmetic and copies ran while one was open for 0% of the time, Pallas kernels for 0%

profile of v2, /device:TPU:8, one launch (start us, length us, event | category | flops | bytes accessed | tf_op | source)
XLA Modules:
  0.0 173.3 jit_solution(11711162324473741040)
XLA Ops:
  0.0 0.7 reshape.14
  0.7 0.1 pad.2.clone
  0.8 0.8 reduce.1
  1.5 0.1 maximum_maximum_fusion
  1.6 0.8 broadcast_in_dim.10
  2.4 11.3 %all-to-all-start = ((bf16[32,48,128]{2,1,0:T(8,128)(2,1)}), bf16[32,48,128]{2,1,0:T(8,128)(2,1)S(1)}, u32[]{:S(2)}, u32[]{:S(2)}) async-start(bf16[32,48,128]{2,1,0:T(8,128)(2,1)} %broadcast_in_dim.10), calls=%async_computation | async-start | bytes 786432 | tf_op jit(solution)/shard_map/all_to_all | solution.py:51
  13.7 0.1 collective-permute-start.1
  13.8 0.5 collective-permute-start.2
  14.3 14.7 %all-to-all-done.own_ref = bf16[32,48,128]{2,1,0:T(8,128)(2,1)S(1)} async-done(((bf16[32,48,128]{2,1,0:T(8,128)(2,1)}), bf16[32,48,128]{2,1,0:T(8,128)(2,1)S(1)}, u32[]{:S(2)}, u32[]{:S(2)}) %all-to-all-start) | async-done | bytes 393248 | tf_op jit(solution)/shard_map/all_to_all | solution.py:51
  29.1 0.0 collective-permute-start
  29.1 0.0 collective-permute-done.1.k2_ref
  29.1 0.0 collective-permute-done.2.v2_ref
  29.1 1.7 collective-permute-done.oth_ref
  30.8 0.0 copy-start.4
  30.8 1.0 copy-done.4
  31.9 0.0 copy-start.5
  31.9 1.0 copy-done.5
  32.9 0.0 copy-start.7
  32.9 0.7 copy-done.7
  33.6 0.0 copy-start.8
  33.6 0.7 copy-done.8
  34.2 3.1 %attention.1 = (bf16[32,32,256]{2,1,0:T(8,128)(2,1)S(1)}, s32[64]{0:T(128)S(1)}) custom-call(s32[32]{0:T(128)S(1)} %copy-done.7, s32[8]{0:T(128)S(1)} %copy-done.8, bf16[32,48,128]{2,1,0:T(8,128)(2,1)S(1)} %all-to-all-done.own_ref, bf16[32,48,128]{2,1,0:T(8,128)(2,1)S(1)} %collective-permute-done.oth_ref, bf16[8,128,256]{2,1,0:T(8,128)(2,1)S(1)} %copy-done.4, ...), custom_call_target="tpu_custom_call" | custom-call | tf_op jit(solution)/shard_map/attention/pallas_call | solution.py:291
  37.3 0.0 copy-start.2
  37.3 0.0 copy-start.6
  37.3 22.3 %all_to_all.35.part_ref = bf16[32,32,256]{2,1,0:T(8,128)(2,1)S(1)} all-to-all(bf16[32,32,256]{2,1,0:T(8,128)(2,1)S(1)} %get-tuple-element.12), channel_id=1, replica_groups={{0,8,16,24,32,40,48,56,64,72,80,88,96,104,112,120,128,136,144,152,160,1..., dimensions={0} | all-to-all | bytes 1048576 | tf_op jit(solution)/shard_map/all_to_all | solution.py:51
  59.6 2.5 %combine.1 = bf16[32,32,128]{2,1,0:T(8,128)(2,1)S(1)} custom-call(s32[64]{0:T(128)S(1)} %get-tuple-element.11.order_ref, bf16[32,32,256]{2,1,0:T(8,128)(2,1)S(1)} %all_to_all.35.part_ref, bf16[32,48,128]{2,1,0:T(8,128)(2,1)S(1)} %all-to-all-done.own_ref, bf16[32,48,128]{2,1,0:T(8,128)(2,1)S(1)} %collective-permute-done.oth_ref), custom_call_target="tpu_custom_call" | custom-call | tf_op jit(solution)/shard_map/combine/pallas_call | solution.py:299
  62.0 0.0 copy-start.9
  62.1 16.8 %all_to_all.36.own_ref = bf16[32,32,128]{2,1,0:T(8,128)(2,1)S(1)} all-to-all(bf16[32,32,128]{2,1,0:T(8,128)(2,1)S(1)} %combine.1), channel_id=1, replica_groups={{0,8,16,24,32,40,48,56,64,72,80,88,96,104,112,120,128,136,144,152,160,1..., dimensions={0} | all-to-all | bytes 524288 | tf_op jit(solution)/shard_map/all_to_all | solution.py:51
  78.9 0.0 collective-permute-start.3
  78.9 1.5 collective-permute-done.3.oth_ref
  80.4 0.0 copy-done.2
  80.4 0.0 copy-done.6
  80.4 0.0 copy-start.1
  80.4 1.2 project.1
  81.6 0.0 copy-start.3
  81.6 0.7 copy-done.3
  82.3 4.9 %all-to-all-start.3 = ((f32[4,64,256]{2,1,0:T(8,128)}), f32[4,64,256]{2,1,0:T(8,128)}, u32[]{:S(2)}, u32[]{:S(2)}) async-start(f32[4,64,256]{2,1,0:T(8,128)} %copy-done.3), calls=%async_computation.3 | async-start | bytes 524288 | tf_op jit(solution)/shard_map/all_to_all | solution.py:317
  87.2 0.0 copy-done.9
  87.2 5.6 %all-to-all-done.3.parts_ref = f32[4,64,256]{2,1,0:T(8,128)} async-done(((f32[4,64,256]{2,1,0:T(8,128)}), f32[4,64,256]{2,1,0:T(8,128)}, u32[]{:S(2)}, u32[]{:S(2)}) %all-to-all-start.3) | async-done | bytes 262176 | tf_op jit(solution)/shard_map/all_to_all | solution.py:317
  92.8 1.1 norm.1
  93.9 35.2 %all_to_all.37.own_ref = bf16[32,16,1152]{2,1,0:T(8,128)(2,1)S(1)} all-to-all(bf16[32,16,1152]{2,1,0:T(8,128)(2,1)S(1)} %get-tuple-element.14), channel_id=1, replica_groups={{0,8,16,24,32,40,48,56,64,72,80,88,96,104,112,120,128,136,144,152,160,1..., dimensions={0} | all-to-all | bytes 2359296 | tf_op jit(solution)/shard_map/all_to_all | solution.py:51
  129.1 0.0 collective-permute-start.4
  129.1 2.8 %collective-permute-done.4.oth_ref = bf16[32,16,1152]{2,1,0:T(8,128)(2,1)S(1)} collective-permute-done((bf16[32,16,1152]{2,1,0:T(8,128)(2,1)S(1)}, bf16[32,16,1152]{2,1,0:T(8,128)(2,1)S(1)}, u32[]{:S(2)}, u32[]{:S(2)}) %collective-permute-start.4) | collective-permute-done | bytes 1179680 | tf_op jit(solution)/shard_map/ppermute | solution.py:47
  131.9 0.0 copy-done.1
  131.9 0.0 copy-start
  131.9 2.9 %copy-done = bf16[2,104,16384]{2,1,0:T(8,128)(2,1)S(1)} copy-done((bf16[2,104,16384]{2,1,0:T(8,128)(2,1)S(1)}, bf16[2,104,16384]{2,1,0:T(8,128)(2,1)}, u32[]{:S(2)}) %copy-start) | copy-done | bytes 6815768
  134.9 3.4 %feed.1 = (bf16[16,128,256]{2,1,0:T(8,128)(2,1)S(1)}, f32[16,128,256]{2,1,0:T(8,128)S(1)}) custom-call(bf16[32,16,1152]{2,1,0:T(8,128)(2,1)S(1)} %all_to_all.37.own_ref, bf16[32,16,1152]{2,1,0:T(8,128)(2,1)S(1)} %collective-permute-done.4.oth_ref, bf16[2,104,16384]{2,1,0:T(8,128)(2,1)S(1)} %copy-done, bf16[104,16384]{1,0:T(8,128)(2,1)S(1)} %copy-done.1), custom_call_target="tpu_custom_call" | custom-call | tf_op jit(solution)/shard_map/feed/pallas_call | solution.py:328
  138.3 0.2 collective-permute-start.5
  138.5 2.5 %collective-permute-done.5 = bf16[16,128,256]{2,1,0:T(8,128)(2,1)S(1)} collective-permute-done((bf16[16,128,256]{2,1,0:T(8,128)(2,1)S(1)}, bf16[16,128,256]{2,1,0:T(8,128)(2,1)S(1)}, u32[]{:S(2)}, u32[]{:S(2)}) %collective-permute-start.5) | collective-permute-done | bytes 1048608 | tf_op jit(solution)/shard_map/ppermute | solution.py:47
  141.0 0.3 add_convert_fusion
  141.3 20.5 %all_to_all.38 = bf16[16,128,256]{2,1,0:T(8,128)(2,1)S(1)} all-to-all(bf16[16,128,256]{2,1,0:T(8,128)(2,1)S(1)} %add_convert_fusion), channel_id=1, replica_groups={{0,1,2,3,8,9,10,11,16,17,18,19,24,25,26,27},{4,5,6,7,12,13,14,15,20,21,..., dimensions={0} | all-to-all | bytes 2097152 | tf_op jit(solution)/shard_map/all_to_all | solution.py:336
  161.8 0.1 reduce_sum.21
  161.9 10.8 %all_to_all.39 = bf16[8,16,256]{2,1,0:T(8,128)(2,1)S(1)} all-to-all(bf16[8,16,256]{2,1,0:T(8,128)(2,1)S(1)} %bitcast.2), channel_id=1, replica_groups={{0,32,64,96,128,160,192,224},{4,36,68,100,132,164,196,228},{8,40,72,104..., dimensions={0} | all-to-all | bytes 131072 | tf_op jit(solution)/shard_map/all_to_all | solution.py:338
  172.7 0.6 add_convert_fusion.1
  (3 shorter events, 0.0 us)
Async XLA Ops:
  2.4 26.7 %all-to-all-start = ((bf16[32,48,128]{2,1,0:T(8,128)(2,1)}), bf16[32,48,128]{2,1,0:T(8,128)(2,1)S(1)}, u32[]{:S(2)}, u32[]{:S(2)}) async-start(bf16[32,48,128]{2,1,0:T(8,128)(2,1)} %broadcast_in_dim.10), calls=%async_computation | async-start | bytes 786432 | tf_op jit(solution)/shard_map/all_to_all | solution.py:51
  13.7 15.4 %collective-permute-start.1 = (bf16[8,128,256]{2,1,0:T(8,128)(2,1)}, bf16[8,128,256]{2,1,0:T(8,128)(2,1)S(1)}, u32[]{:S(2)}, u32[]{:S(2)}) collective-permute-start(bf16[8,128,256]{2,1,0:T(8,128)(2,1)} %k_ref.1), channel_id=1, source_target_pairs={{0,4},{4,0},{8,12},{12,8},{16,20},{20,16},{24,28},{28,24},{32,36},... | collective-permute-start | bytes 1572872 | tf_op jit(solution)/shard_map/ppermute | solution.py:47
  13.8 15.3 %collective-permute-start.2 = (bf16[8,128,256]{2,1,0:T(8,128)(2,1)}, bf16[8,128,256]{2,1,0:T(8,128)(2,1)S(1)}, u32[]{:S(2)}, u32[]{:S(2)}) collective-permute-start(bf16[8,128,256]{2,1,0:T(8,128)(2,1)} %v_ref.1), channel_id=1, source_target_pairs={{0,4},{4,0},{8,12},{12,8},{16,20},{20,16},{24,28},{28,24},{32,36},... | collective-permute-start | bytes 1572872 | tf_op jit(solution)/shard_map/ppermute | solution.py:47
  29.1 1.7 collective-permute-start
  30.8 1.0 copy-start.4
  31.9 1.0 copy-start.5
  32.9 0.7 copy-start.7
  33.6 0.7 copy-start.8
  37.3 43.1 %copy-start.2 = (bf16[4096,256]{1,0:T(8,128)(2,1)S(1)}, bf16[4096,256]{1,0:T(8,128)(2,1)}, u32[]{:S(2)}) copy-start(bf16[4096,256]{1,0:T(8,128)(2,1)} %w_ref.1) | copy-start | bytes 6291460
  37.3 43.1 %copy-start.6 = (bf16[16,256]{1,0:T(8,128)(2,1)S(1)}, bf16[16,256]{1,0:T(8,128)(2,1)}, u32[]{:S(2)}) copy-start(bf16[16,256]{1,0:T(8,128)(2,1)} %stream_ref.1) | copy-start | bytes 24580
  62.0 25.1 %copy-start.9 = (bf16[256]{0:T(256)(128)(2,1)S(1)}, bf16[256]{0:T(256)(128)(2,1)}, u32[]{:S(2)}) copy-start(bf16[256]{0:T(256)(128)(2,1)} %param.19) | copy-start | bytes 1540
  78.9 1.5 collective-permute-start.3
  80.4 51.5 %copy-start.1 = (bf16[104,16384]{1,0:T(8,128)(2,1)S(1)}, bf16[104,16384]{1,0:T(8,128)(2,1)}, u32[]{:S(2)}) copy-start(bf16[104,16384]{1,0:T(8,128)(2,1)} %down_ref.1) | copy-start | bytes 10223620
  81.6 0.7 copy-start.3
  82.3 10.5 %all-to-all-start.3 = ((f32[4,64,256]{2,1,0:T(8,128)}), f32[4,64,256]{2,1,0:T(8,128)}, u32[]{:S(2)}, u32[]{:S(2)}) async-start(f32[4,64,256]{2,1,0:T(8,128)} %copy-done.3), calls=%async_computation.3 | async-start | bytes 524288 | tf_op jit(solution)/shard_map/all_to_all | solution.py:317
  129.1 2.8 %collective-permute-start.4 = (bf16[32,16,1152]{2,1,0:T(8,128)(2,1)S(1)}, bf16[32,16,1152]{2,1,0:T(8,128)(2,1)S(1)}, u32[]{:S(2)}, u32[]{:S(2)}) collective-permute-start(bf16[32,16,1152]{2,1,0:T(8,128)(2,1)S(1)} %all_to_all.37.own_ref), channel_id=1, source_target_pairs={{0,4},{4,0},{8,12},{12,8},{16,20},{20,16},{24,28},{28,24},{32,36},... | collective-permute-start | bytes 3538952 | tf_op jit(solution)/shard_map/ppermute | solution.py:47
  131.9 2.9 %copy-start = (bf16[2,104,16384]{2,1,0:T(8,128)(2,1)S(1)}, bf16[2,104,16384]{2,1,0:T(8,128)(2,1)}, u32[]{:S(2)}) copy-start(bf16[2,104,16384]{2,1,0:T(8,128)(2,1)} %gu_ref.1) | copy-start | bytes 20447236
  138.3 2.7 %collective-permute-start.5 = (bf16[16,128,256]{2,1,0:T(8,128)(2,1)S(1)}, bf16[16,128,256]{2,1,0:T(8,128)(2,1)S(1)}, u32[]{:S(2)}, u32[]{:S(2)}) collective-permute-start(bf16[16,128,256]{2,1,0:T(8,128)(2,1)S(1)} %get-tuple-element.16), channel_id=1, source_target_pairs={{0,4},{4,0},{8,12},{12,8},{16,20},{20,16},{24,28},{28,24},{32,36},... | collective-permute-start | bytes 3145736 | tf_op jit(solution)/shard_map/ppermute | solution.py:47

commit v3 on v2

v3 whole, which is shorter than its diff:
```python
import jax
import jax.numpy as jnp
from jax import lax
from jax.experimental import pallas as pl
from jax.experimental.pallas import tpu as pltpu
from jax.sharding import PartitionSpec as P

D = 16384
HD = 128
NZ, NX, NC, NY = 8, 4, 2, 4
PEERS = NZ * NX
HEADS = 32
GROUP = 16
PROMPTS = 8
TOKS = 64
HALF = 32
SHARD = 128
COLS = 256
HIDDEN = 104
EPS = 1e-05
SCALE = HD ** (-0.5)
FLOOR = -1e30
VMEM_LIMIT = 24 * 1024 * 1024

bf16 = jnp.bfloat16
f32 = jnp.float32


def kvp_index(z, x, c):
    return (z * NX + x) * NC + c


def all_index(z, x, c, y):
    return kvp_index(z, x, c) * NY + y


G_XZ = [[kvp_index(z, x, c) for z in range(NZ) for x in range(NX)] for c in range(NC)]
G_Z = [[kvp_index(z, x, c) for z in range(NZ)] for x in range(NX) for c in range(NC)]
G_XY = [
    [all_index(z, x, c, y) for x in range(NX) for y in range(NY)]
    for z in range(NZ)
    for c in range(NC)
]
CORE_PAIRS = [(i, i ^ 1) for i in range(NZ * NX * NC)]


def swap_cores(array):
    return lax.ppermute(array, "kvp", CORE_PAIRS)


def swap_plane(array):
    return lax.all_to_all(array, "kvp", 0, 0, axis_index_groups=G_XZ, tiled=True)


def swap_face(array):
    return lax.all_to_all(array, ("kvp", "tp"), 0, 0, axis_index_groups=G_XY, tiled=True)


def nt_dot(a, b):
    return lax.dot_general(a, b, (((1,), (1,)), ((), ())), preferred_element_type=f32)


def nn_dot(a, b):
    return jnp.dot(a, b, preferred_element_type=f32)


def lane_ids(shape):
    return lax.broadcasted_iota(jnp.int32, shape, len(shape) - 1)


def row_ids(shape):
    return lax.broadcasted_iota(jnp.int32, shape, len(shape) - 2)


def prepare_kernel(
    prompt_ref, len_ref, query_ref, k_ref, v_ref, block_ref, k_out, v_out, order_ref, rows, count, sems
):
    k_copy = pltpu.make_async_copy(k_ref, k_out, sems.at[0])
    v_copy = pltpu.make_async_copy(v_ref, v_out, sems.at[1])
    k_copy.start()
    v_copy.start()
    query = query_ref[...].astype(f32)
    for h in range(HEADS):
        rows[h : h + 1, :] = query[:, h * HD : (h + 1) * HD]
    block = rows[...].astype(bf16)
    for i in range(PEERS):
        block_ref[i] = block
    for p in range(PROMPTS):
        count[p] = 0
        order_ref[TOKS + p] = len_ref[p]
    for s in range(HALF):
        p = prompt_ref[s]
        seen = jnp.minimum(count[p], 3)
        count[p] = seen + 1
        order_ref[p * 8 + seen] = s
        order_ref[p * 8 + 4 + seen] = s + HALF
    k_copy.wait()
    v_copy.wait()


def gather_row(order_ref, slot, core):
    t = order_ref[slot]
    return t // 2 + PEERS * lax.rem(t + core, 2)


def attention_kernel(
    order_ref,
    own_ref,
    oth_ref,
    k_ref,
    v_ref,
    k2_ref,
    v2_ref,
    draft_ref,
    draft2_ref,
    out_ref,
    gath,
    extra,
):
    kvp = lax.axis_index("kvp")
    core = lax.rem(kvp, 2)
    gath[0:PEERS] = own_ref[...]
    gath[PEERS : 2 * PEERS] = oth_ref[...]
    extra[...] = jnp.zeros((GROUP, HD), f32)
    for side, ref in enumerate((draft_ref, draft2_ref)):
        both = ref[0].astype(f32)
        for i in range(4):
            row = side * 4 + i
            extra[row : row + 1, :] = both[i // 2 : i // 2 + 1, (i % 2) * HD : (i % 2 + 1) * HD]
    extras = extra[...]
    to_row = row_ids((256, 256))
    from_row = lane_ids((256, 256))
    regroup = (
        (to_row // GROUP == from_row % GROUP) & (to_row % GROUP == from_row // GROUP)
    ).astype(bf16)
    by_group = (lane_ids((GROUP, SHARD)) % GROUP == row_ids((GROUP, SHARD))).astype(bf16)
    lanes = lane_ids((SHARD, SHARD))
    token = row_ids((SHARD, SHARD)) // GROUP
    here = kvp * SHARD + lanes
    there = (kvp + 1 - 2 * core) * SHARD + lanes
    position = jnp.concatenate([here, there], axis=1)
    for kv in range(2):
        cols = slice(kv * HD, (kv + 1) * HD)
        stats = jnp.zeros((GROUP, SHARD), f32)
        for pair in range(2):
            parts = []
            for q_ in range(2):
                i = pair * 2 + q_
                p = i + 4 * core
                queries = jnp.concatenate(
                    [
                        gath[gather_row(order_ref, p * 8 + j, core), kv * GROUP : (kv + 1) * GROUP, :]
                        for j in range(8)
                    ],
                    axis=0,
                )
                keys = jnp.concatenate([k_ref[p, :, cols], k2_ref[p, :, cols]], axis=0)
                values = jnp.concatenate([v_ref[p, :, cols], v2_ref[p, :, cols]], axis=0)
                scores = nt_dot(queries, keys) * SCALE
                visible = position < order_ref[TOKS + p]
                top = jnp.max(jnp.where(visible, scores, FLOOR), axis=1, keepdims=True)
                top = top.astype(bf16).astype(f32)
                weights = jnp.where(visible, jnp.exp(scores - top), 0.0)
                total = jnp.sum(weights, axis=1, keepdims=True)
                summed = nn_dot(weights.astype(bf16), values)
                parts.append(summed.astype(bf16))
                high = total.astype(bf16).astype(f32)
                low = total - high
                at = token + i * 8
                spread = jnp.where(
                    lanes == at,
                    top,
                    jnp.where(
                        lanes == at + HALF, high, jnp.where(lanes == at + 2 * HALF, low, 0.0)
                    ),
                )
                stats = stats + nn_dot(by_group, spread.astype(bf16))
            both = nn_dot(regroup, jnp.concatenate(parts, axis=0)).astype(bf16)
            for g in range(GROUP):
                out_ref[kv * GROUP + g, pair * 16 : pair * 16 + 16, :] = both[
                    g * 16 : (g + 1) * 16, :
                ]
        inner = row_ids((GROUP, HD))
        for g in range(GROUP):
            out_ref[kv * GROUP + g, HALF : HALF + 16, :] = jnp.where(
                inner == 8, stats[g : g + 1, :], extras
            ).astype(bf16)


def combine_kernel(order_ref, part_ref, gath, out_ref, stat, turn):
    kvp = lax.axis_index("kvp")
    core = lax.rem(kvp, 2)
    head = kvp // 2
    kv = head // GROUP
    first = pl.multiple_of(kv * GROUP, GROUP)
    query_tiles, draft_tiles = [], []
    slots = row_ids((HALF, HD))
    slot_token = jnp.zeros((HALF, HD), jnp.int32)
    for s in range(HALF):
        slot = HALF * core + s
        query_tiles.append(gath[gather_row(order_ref, slot, core), pl.ds(first, GROUP), :])
        slot_token = jnp.where(slots == s, order_ref[slot], slot_token)
    for i in range(PEERS):
        tile = part_ref[i, HALF : HALF + 16, :]
        draft_tiles.append(tile)
        stat[i : i + 1, :] = tile.astype(f32)[8:9, :]
    shape = (HALF, HALF * GROUP)
    outer = lane_ids(shape) // GROUP
    inner = lane_ids(shape) % GROUP
    pick = ((row_ids(shape) == outer) & (inner == head % GROUP)).astype(bf16)
    queries = nn_dot(pick, jnp.concatenate(query_tiles, axis=0)).astype(bf16)
    drafts = jnp.concatenate(draft_tiles, axis=0)
    scores = nt_dot(queries, drafts) * SCALE
    slot_token = jnp.concatenate([slot_token] * 4, axis=1)
    side = inner // 4
    key_token = 2 * outer + jnp.where(side == 0, core, 1 - core)
    visible = (
        (inner % 4 == kv)
        & (side < 2)
        & (slot_token % HALF == key_token % HALF)
        & (key_token // HALF <= slot_token // HALF)
    )
    stats = stat[...]
    top_row = jnp.max(stats, axis=0, keepdims=True)
    factors = jnp.exp(stats - top_row)
    totals = pltpu.roll(stats, HD - HALF, 1) + pltpu.roll(stats, HD - 2 * HALF, 1)
    turn[...] = jnp.zeros((HD, HD), f32)
    turn[0:PEERS, :] = factors
    turn[PEERS : PEERS + 1, :] = jnp.sum(factors * totals, axis=0, keepdims=True)
    turn[PEERS + 1 : PEERS + 2, :] = top_row
    turned = turn[...].T[0:HALF, :]
    total = turned[:, PEERS : PEERS + 1]
    top_cache = turned[:, PEERS + 1 : PEERS + 2]
    summed = jnp.zeros((HALF, HD), f32)
    for i in range(PEERS):
        summed = summed + turned[:, i : i + 1] * part_ref[i, 0:HALF, :].astype(f32)
    top_draft = jnp.max(jnp.where(visible, scores, FLOOR), axis=1, keepdims=True)
    top = jnp.maximum(top_cache, top_draft)
    weights = jnp.where(visible, jnp.exp(scores - top), 0.0)
    scale = jnp.exp(top_cache - top)
    total = scale * total + jnp.sum(weights, axis=1, keepdims=True)
    summed = scale * summed + nn_dot(pltpu.roll(weights, 2, 1).astype(bf16), drafts)
    attn = (summed / total).astype(bf16)
    for i in range(PEERS):
        out_ref[i] = attn


def project_kernel(order_ref, own_ref, oth_ref, w_ref, out_ref, by_slot, by_token):
    core = lax.rem(lax.axis_index("kvp"), 2)
    acc = jnp.zeros((TOKS, COLS), f32)
    for i in range(HEADS // 2):
        lhs = jnp.concatenate(
            [
                jnp.concatenate([own_ref[2 * i], own_ref[2 * i + 1]], axis=1),
                jnp.concatenate([oth_ref[2 * i], oth_ref[2 * i + 1]], axis=1),
            ],
            axis=0,
        )
        acc = acc + nn_dot(lhs, w_ref[2 * i * HD : (2 * i + 2) * HD, :])
    by_slot[...] = acc
    for r in range(TOKS):
        t = order_ref[lax.rem(r + HALF * core, TOKS)]
        by_token[pl.ds(t, 1), :] = by_slot[r : r + 1, :]
    for y in range(NY):
        out_ref[y] = by_token[16 * y : 16 * y + 16, :]


def norm_kernel(parts_ref, stream_ref, gain_ref, msg_ref, mid_ref):
    middle = (
        (parts_ref[0] + parts_ref[1]) + (parts_ref[2] + parts_ref[3])
    ) + stream_ref[...].astype(f32)
    mid_ref[...] = middle
    scaled = (middle * gain_ref[...].astype(f32).reshape(1, COLS)).astype(bf16)
    squares = jnp.sum(middle * middle, axis=1, keepdims=True)
    high = squares.astype(bf16).astype(f32)
    low = squares - high
    lanes = lane_ids((16, HD))
    stats = jnp.where(lanes == 0, high, jnp.where(lanes == 1, low, 0.0)).astype(bf16)
    block = jnp.concatenate([scaled, stats], axis=1)
    for i in range(NZ):
        msg_ref[i] = block


def spread_kernel(in_ref, out_ref):
    stats = jnp.zeros((16, HD), f32)
    for z in range(NZ):
        stats = stats + in_ref[z, :, COLS:].astype(f32)
    squares = stats[:, 0:1] + stats[:, 1:2]
    high = squares.astype(bf16).astype(f32)
    low = squares - high
    lanes = lane_ids((16, COLS))
    tile = jnp.where(lanes == 0, high, jnp.where(lanes == 1, low, 0.0)).astype(bf16)
    for i in range(NX * NY):
        for z in range(NZ):
            out_ref[i, z * 16 : (z + 1) * 16, :] = in_ref[z, :, :COLS]
        out_ref[i, NZ * 16 :, :] = tile


def feed_kernel(own_ref, oth_ref, gu_ref, down_ref, send_ref, keep_ref, weights, sems):
    core = lax.rem(lax.axis_index("kvp"), 2)
    width = D // NZ
    copies = [
        pltpu.make_async_copy(
            gu_ref.at[:, :, pl.ds(z * width, width)], weights.at[z], sems.at[z]
        )
        for z in range(NZ)
    ]
    for copy in copies:
        copy.start()
    gate = jnp.zeros((TOKS, HIDDEN), f32)
    up = jnp.zeros((TOKS, HIDDEN), f32)
    stats = [jnp.zeros((16, HD), f32) for _ in range(NY)]
    for x in range(NX):
        for y in range(NY):
            for src_ref in (own_ref, oth_ref):
                stats[y] = stats[y] + src_ref[x * NY + y, NZ * 16 :, :HD].astype(f32)
    for z in range(NZ):
        copies[z].wait()
        for x in range(NX):
            for src_ref, side in ((own_ref, core), (oth_ref, 1 - core)):
                rows = jnp.concatenate(
                    [src_ref[x * NY + y, z * 16 : (z + 1) * 16, :] for y in range(NY)], axis=0
                )
                cols = pl.ds(pl.multiple_of((2 * x + side) * COLS, COLS), COLS)
                gate = gate + nt_dot(rows, weights[z, 0, :, cols])
                up = up + nt_dot(rows, weights[z, 1, :, cols])
    squares = jnp.concatenate([s[:, 0:1] + s[:, 1:2] for s in stats], axis=0)
    rscale = lax.rsqrt(squares / D + EPS)
    gate = gate * rscale
    up = up * rscale
    hidden = (gate / (1.0 + jnp.exp(-gate)) * up).astype(bf16)
    for out_ref, side in ((send_ref, 1 - core), (keep_ref, core)):
        for z in range(NZ):
            for x in range(NX):
                cols = pl.ds(pl.multiple_of((2 * (z * NX + x) + side) * COLS, COLS), COLS)
                part = nn_dot(hidden, down_ref[:, cols]).astype(out_ref.dtype)
                for y in range(NY):
                    out_ref[x * NY + y, z * 16 : (z + 1) * 16, :] = part[16 * y : 16 * y + 16]


VMEM = pl.BlockSpec(memory_space=pltpu.VMEM)
SMEM = pl.BlockSpec(memory_space=pltpu.SMEM)
HBM = pl.BlockSpec(memory_space=pltpu.HBM)
PARAMS = pltpu.CompilerParams(vmem_limit_bytes=VMEM_LIMIT)


def call(kernel, name, in_specs, out_shape, out_specs, scratch=()):
    return pl.pallas_call(
        kernel,
        name=name,
        in_specs=in_specs,
        out_shape=out_shape,
        out_specs=out_specs,
        scratch_shapes=list(scratch),
        compiler_params=PARAMS,
    )


def in_hbm(array):
    return pltpu.with_memory_space_constraint(array, pltpu.HBM)


def on_device(
    query,
    draft_kv,
    key_cache,
    value_cache,
    prompt_of,
    prefix_len,
    out_weight,
    stream,
    norm_gain,
    gate_up,
    down_weight,
):
    shape = jax.ShapeDtypeStruct
    cache = shape((PROMPTS, SHARD, 2 * HD), bf16)
    key_pair, value_pair = swap_cores(key_cache), swap_cores(value_cache)
    draft_pair = swap_cores(draft_kv)
    block, keys, values, order = call(
        prepare_kernel,
        "prepare",
        [SMEM, SMEM, VMEM, HBM, HBM],
        [
            shape((PEERS, HEADS, HD), bf16),
            cache,
            cache,
            shape((TOKS + PROMPTS,), jnp.int32),
        ],
        [VMEM, VMEM, VMEM, SMEM],
        [
            pltpu.VMEM((HEADS, HD), f32),
            pltpu.SMEM((PROMPTS,), jnp.int32),
            pltpu.SemaphoreType.DMA((2,)),
        ],
    )(in_hbm(prompt_of), in_hbm(prefix_len), in_hbm(query), in_hbm(key_cache), in_hbm(value_cache))
    own = swap_plane(block)
    oth = swap_cores(own)
    part, gath = call(
        attention_kernel,
        "attention",
        [SMEM] + [VMEM] * 8,
        [shape((HEADS, 48, HD), bf16), shape((TOKS, HEADS, HD), bf16)],
        [VMEM, VMEM],
        [pltpu.VMEM((GROUP, HD), f32)],
    )(order, own, oth, keys, values, key_pair, value_pair, draft_kv, draft_pair)
    attn = call(
        combine_kernel,
        "combine",
        [SMEM, VMEM, VMEM],
        shape((PEERS, HALF, HD), bf16),
        VMEM,
        [pltpu.VMEM((PEERS, HD), f32), pltpu.VMEM((HD, HD), f32)],
    )(order, swap_plane(part), gath)
    attn_own = swap_plane(attn)
    attn_oth = swap_cores(attn_own)
    partial = call(
        project_kernel,
        "project",
        [SMEM, VMEM, VMEM, VMEM],
        shape((NY, 16, COLS), f32),
        VMEM,
        [pltpu.VMEM((TOKS, COLS), f32), pltpu.VMEM((TOKS, COLS), f32)],
    )(order, attn_own, attn_oth, out_weight)
    partial = lax.all_to_all(partial, "tp", 0, 0, tiled=True)
    msg, middle = call(
        norm_kernel,
        "norm",
        [VMEM, VMEM, VMEM],
        [shape((NZ, 16, COLS + HD), bf16), shape((16, COLS), f32)],
        [VMEM, VMEM],
    )(partial, in_hbm(stream), in_hbm(norm_gain))
    msg = lax.all_to_all(msg, "kvp", 0, 0, axis_index_groups=G_Z, tiled=True)
    msg = call(spread_kernel, "spread", [VMEM], shape((NX * NY, NZ * 16 + 16, COLS), bf16), VMEM)(
        msg
    )
    normed_own = swap_face(msg)
    normed_oth = swap_cores(normed_own)
    send, keep = call(
        feed_kernel,
        "feed",
        [VMEM, VMEM, HBM, VMEM],
        [shape((NX * NY, NZ * 16, COLS), bf16), shape((NX * NY, NZ * 16, COLS), f32)],
        [VMEM, VMEM],
        [
            pltpu.VMEM((NZ, 2, HIDDEN, D // NZ), bf16),
            pltpu.SemaphoreType.DMA((NZ,)),
        ],
    )(normed_own, normed_oth, in_hbm(gate_up), down_weight)
    summed = (keep + swap_cores(send).astype(f32)).astype(bf16)
    summed = swap_face(summed)
    summed = jnp.sum(summed.astype(f32), axis=0).astype(bf16).reshape(NZ, 16, COLS)
    summed = lax.all_to_all(summed, "kvp", 0, 0, axis_index_groups=G_Z, tiled=True)
    return (middle + jnp.sum(summed.astype(f32), axis=0)).astype(bf16)


def solution(mesh):
    in_specs = (
        P("kvp", "tp"),
        P("kvp", None, "tp"),
        P(None, "kvp", "tp"),
        P(None, "kvp", "tp"),
        P(),
        P(),
        P("tp", "kvp"),
        P("tp", "kvp"),
        P("kvp"),
        P(None, ("kvp", "tp"), None),
        P(("kvp", "tp"), None),
    )
    out_specs = P("tp", "kvp")
    return jax.shard_map(
        on_device, mesh=mesh, in_specs=in_specs, out_specs=out_specs, check_vma=False
    )
```

time: 174 us -> 157 us (0.902)
  waiting for transfers between devices: 29 us -> 20 us
  local copies, waits for them, and re-layouts: 8.62 us -> 0.68 us
  starting transfers between devices: 17.1 us -> 12.7 us
  Pallas kernels: 11.2 us -> 14 us
    all_to_all x1 -> x4, blocking collectives: 20.5 us -> 60.4 us  [the longest x2 40.1 us: swap_face(): lax.all_to_all(array, ('kvp', 'tp'), 0, 0, axis_index_groups=G_XY, tiled=...]
    all_to_all x3 -> x2, blocking collectives: 74.3 us -> 36.2 us  [swap_plane(): lax.all_to_all(array, 'kvp', 0, 0, axis_index_groups=G_XZ, tiled=True)]
    unnamed x20 -> x6, local copies, waits for them, and re-layouts: 7.05 us -> 0.68 us
    all_to_all x1 -> x0, waiting for transfers between devices: 5.61 us -> none  [on_device(): partial = lax.all_to_all(partial, 'tp', 0, 0, tiled=True)]
    all_to_all x1 -> x0, starting transfers between devices: 4.91 us -> none  [on_device(): partial = lax.all_to_all(partial, 'tp', 0, 0, tiled=True)]
    pallas_call x5 -> x7, Pallas kernels: 11.2 us -> 14 us  [the longest x1 4.76 us: on_device(): call(feed_kernel, 'feed', [VMEM, VMEM, HBM, VMEM], [shape((NX * NY, NZ *...]
    all_to_all x1, waiting for transfers between devices: 14.7 us -> 12.1 us  [swap_plane(): lax.all_to_all(array, 'kvp', 0, 0, axis_index_groups=G_XZ, tiled=True)]
    ppermute x6 -> x7, waiting for transfers between devices: 8.61 us -> 7.93 us  [swap_cores(): return lax.ppermute(array, 'kvp', CORE_PAIRS)]
  transfers between devices with their start and end apart: 8 -> 8, of which waited for: 6 -> 5; matrix products, arithmetic and copies ran while one was open for 0% -> 0% of each run, Pallas kernels for 0% -> 0%
where the time goes in v3:
time: 157 us; the launch traced here: 156 us
  blocking collectives  107 us (68%)
  waiting for transfers between devices  20 us (13%)
  Pallas kernels  14 us (9%)
  starting transfers between devices  12.7 us (8%)
    all_to_all x2, blocking collectives, swap_face(): lax.all_to_all(array, ('kvp', 'tp'), 0, 0, axis_index_groups=G_XY, tiled=...  40.1 us
    all_to_all x2, blocking collectives, swap_plane(): lax.all_to_all(array, 'kvp', 0, 0, axis_index_groups=G_XZ, tiled=True)  36.2 us
    all_to_all x1, waiting for transfers between devices, swap_plane(): lax.all_to_all(array, 'kvp', 0, 0, axis_index_groups=G_XZ, tiled=True)  12.1 us
    all_to_all x1, starting transfers between devices, swap_plane(): lax.all_to_all(array, 'kvp', 0, 0, axis_index_groups=G_XZ, tiled=True)  11.3 us
    all_to_all x1, blocking collectives, on_device(): msg = lax.all_to_all(msg, 'kvp', 0, 0, axis_index_groups=G_Z, tiled=True)  11.1 us
    all_to_all x1, blocking collectives, on_device(): lax.all_to_all(summed, 'kvp', 0, 0, axis_index_groups=G_Z, tiled=True)  10.8 us
    all_to_all x1, blocking collectives, on_device(): partial = lax.all_to_all(partial, 'tp', 0, 0, tiled=True)  9.14 us
    ppermute x7, waiting for transfers between devices, swap_cores(): return lax.ppermute(array, 'kvp', CORE_PAIRS)  7.93 us
  transfers between devices with their start and end apart: 8, of which 5 were waited for; matrix products, arithmetic and copies ran while one was open for 0% of the time, Pallas kernels for 0%

profile of v3, /device:TPU:8, one launch (start us, length us, event | category | flops | bytes accessed | tf_op | source)
XLA Modules:
  0.0 155.9 jit_solution(1286406390741983001)
XLA Ops:
  0.0 2.7 %prepare.1 = (bf16[32,32,128]{2,1,0:T(8,128)(2,1)}, bf16[8,128,256]{2,1,0:T(8,128)(2,1)S(1)}, bf16[8,128,256]{2,1,0:T(8,128)(2,1)S(1)}, s32[72]{0:T(128)S(1)}) custom-call(s32[32]{0:T(128)} %prompt_ref.1, s32[8]{0:T(128)} %len_ref.1, bf16[1,4096]{1,0:T(2,128)(2,1)} %query_ref.1, bf16[8,128,256]{2,1,0:T(8,128)(2,1)} %k_ref.1, bf16[8,128,256]{2,1,0:T(8,128)(2,1)} %v_ref.1), custom_call_target="tpu_custom_call" | custom-call | tf_op jit(solution)/shard_map/prepare/pallas_call | solution.py:380
  2.7 11.3 %all-to-all-start = ((bf16[32,32,128]{2,1,0:T(8,128)(2,1)}), bf16[32,32,128]{2,1,0:T(8,128)(2,1)S(1)}, u32[]{:S(2)}, u32[]{:S(2)}) async-start(bf16[32,32,128]{2,1,0:T(8,128)(2,1)} %get-tuple-element.16), calls=%async_computation | async-start | bytes 524288 | tf_op jit(solution)/shard_map/all_to_all | solution.py:52
  14.0 0.1 collective-permute-start.1
  14.1 0.5 collective-permute-start.2
  14.6 12.1 %all-to-all-done.own_ref = bf16[32,32,128]{2,1,0:T(8,128)(2,1)S(1)} async-done(((bf16[32,32,128]{2,1,0:T(8,128)(2,1)}), bf16[32,32,128]{2,1,0:T(8,128)(2,1)S(1)}, u32[]{:S(2)}, u32[]{:S(2)}) %all-to-all-start) | async-done | bytes 262176 | tf_op jit(solution)/shard_map/all_to_all | solution.py:52
  26.7 0.0 collective-permute-start
  26.7 0.5 collective-permute-start.3
  27.2 1.0 collective-permute-done.3.draft2_ref
  28.2 0.0 collective-permute-done.1.k2_ref
  28.2 0.0 collective-permute-done.2.v2_ref
  28.2 0.0 collective-permute-done.oth_ref
  28.2 0.0 copy-start.2
  28.3 0.7 copy-done.2
  28.9 0.0 copy-start.1
  28.9 3.0 %attention.1 = (bf16[32,48,128]{2,1,0:T(8,128)(2,1)S(1)}, bf16[64,32,128]{2,1,0:T(8,128)(2,1)S(1)}) custom-call(s32[72]{0:T(128)S(1)} %get-tuple-element.15.order_ref, bf16[32,32,128]{2,1,0:T(8,128)(2,1)S(1)} %all-to-all-done.own_ref, bf16[32,32,128]{2,1,0:T(8,128)(2,1)S(1)} %collective-permute-done.oth_ref, ...), custom_call_target="tpu_custom_call" | custom-call | tf_op jit(solution)/shard_map/attention/pallas_call | solution.py:399
  31.9 19.8 %all_to_all.40.part_ref = bf16[32,48,128]{2,1,0:T(8,128)(2,1)S(1)} all-to-all(bf16[32,48,128]{2,1,0:T(8,128)(2,1)S(1)} %get-tuple-element.19), channel_id=1, replica_groups={{0,8,16,24,32,40,48,56,64,72,80,88,96,104,112,120,128,136,144,152,160,1..., dimensions={0} | all-to-all | bytes 786432 | tf_op jit(solution)/shard_map/all_to_all | solution.py:52
  51.7 1.5 combine.1
  53.2 16.4 %all_to_all.41.own_ref = bf16[32,32,128]{2,1,0:T(8,128)(2,1)S(1)} all-to-all(bf16[32,32,128]{2,1,0:T(8,128)(2,1)S(1)} %combine.1), channel_id=1, replica_groups={{0,8,16,24,32,40,48,56,64,72,80,88,96,104,112,120,128,136,144,152,160,1..., dimensions={0} | all-to-all | bytes 524288 | tf_op jit(solution)/shard_map/all_to_all | solution.py:52
  69.6 0.0 collective-permute-start.4
  69.6 1.5 collective-permute-done.4.oth_ref
  71.1 0.0 copy-done.1
  71.1 1.2 project.1
  72.3 0.0 copy-start
  72.3 9.1 %all_to_all.42.parts_ref = f32[4,16,256]{2,1,0:T(8,128)S(1)} all-to-all(f32[4,16,256]{2,1,0:T(8,128)S(1)} %project.1), channel_id=1, replica_groups=mesh['kvp'=64,'tp'=4] {'tp'}, dimensions={0} | all-to-all | bytes 131072 | tf_op jit(solution)/shard_map/all_to_all | solution.py:425
  81.5 0.8 norm.1
  82.3 11.1 %all_to_all.43.in_ref = bf16[8,16,384]{2,1,0:T(8,128)(2,1)S(1)} all-to-all(bf16[8,16,384]{2,1,0:T(8,128)(2,1)S(1)} %get-tuple-element.22), channel_id=1, replica_groups={{0,32,64,96,128,160,192,224},{4,36,68,100,132,164,196,228},{8,40,72,104..., dimensions={0} | all-to-all | bytes 196608 | tf_op jit(solution)/shard_map/all_to_all | solution.py:433
  93.4 0.2 spread.1
  93.5 19.2 %all_to_all.44.own_ref = bf16[16,144,256]{2,1,0:T(8,128)(2,1)S(1)} all-to-all(bf16[16,144,256]{2,1,0:T(8,128)(2,1)S(1)} %spread.1), channel_id=1, replica_groups={{0,1,2,3,8,9,10,11,16,17,18,19,24,25,26,27},{4,5,6,7,12,13,14,15,20,21,..., dimensions={0} | all-to-all | bytes 2359296 | tf_op jit(solution)/shard_map/all_to_all | solution.py:56
  112.8 0.0 collective-permute-start.5
  112.8 2.8 %collective-permute-done.5.oth_ref = bf16[16,144,256]{2,1,0:T(8,128)(2,1)S(1)} collective-permute-done((bf16[16,144,256]{2,1,0:T(8,128)(2,1)S(1)}, bf16[16,144,256]{2,1,0:T(8,128)(2,1)S(1)}, u32[]{:S(2)}, u32[]{:S(2)}) %collective-permute-start.5) | collective-permute-done | bytes 1179680 | tf_op jit(solution)/shard_map/ppermute | solution.py:48
  115.6 0.0 copy-done
  115.6 4.8 %feed.1 = (bf16[16,128,256]{2,1,0:T(8,128)(2,1)S(1)}, f32[16,128,256]{2,1,0:T(8,128)S(1)}) custom-call(bf16[16,144,256]{2,1,0:T(8,128)(2,1)S(1)} %all_to_all.44.own_ref, bf16[16,144,256]{2,1,0:T(8,128)(2,1)S(1)} %collective-permute-done.5.oth_ref, bf16[2,104,16384]{2,1,0:T(8,128)(2,1)} %gu_ref.1, bf16[104,16384]{1,0:T(8,128)(2,1)S(1)} %copy-done), custom_call_target="tpu_custom_call" | custom-call | tf_op jit(solution)/shard_map/feed/pallas_call | solution.py:439
  120.4 0.2 collective-permute-start.6
  120.6 2.5 %collective-permute-done.6 = bf16[16,128,256]{2,1,0:T(8,128)(2,1)S(1)} collective-permute-done((bf16[16,128,256]{2,1,0:T(8,128)(2,1)S(1)}, bf16[16,128,256]{2,1,0:T(8,128)(2,1)S(1)}, u32[]{:S(2)}, u32[]{:S(2)}) %collective-permute-start.6) | collective-permute-done | bytes 1048608 | tf_op jit(solution)/shard_map/ppermute | solution.py:48
  123.1 0.4 add_convert_fusion
  123.5 20.9 %all_to_all.45 = bf16[16,128,256]{2,1,0:T(8,128)(2,1)S(1)} all-to-all(bf16[16,128,256]{2,1,0:T(8,128)(2,1)S(1)} %add_convert_fusion), channel_id=1, replica_groups={{0,1,2,3,8,9,10,11,16,17,18,19,24,25,26,27},{4,5,6,7,12,13,14,15,20,21,..., dimensions={0} | all-to-all | bytes 2097152 | tf_op jit(solution)/shard_map/all_to_all | solution.py:56
  144.4 0.1 reduce_sum.21
  144.5 10.8 %all_to_all.46 = bf16[8,16,256]{2,1,0:T(8,128)(2,1)S(1)} all-to-all(bf16[8,16,256]{2,1,0:T(8,128)(2,1)S(1)} %bitcast.1), channel_id=1, replica_groups={{0,32,64,96,128,160,192,224},{4,36,68,100,132,164,196,228},{8,40,72,104..., dimensions={0} | all-to-all | bytes 131072 | tf_op jit(solution)/shard_map/all_to_all | solution.py:453
  155.3 0.6 add_convert_fusion.1
  (1 shorter events, 0.0 us)
Async XLA Ops:
  2.7 24.0 %all-to-all-start = ((bf16[32,32,128]{2,1,0:T(8,128)(2,1)}), bf16[32,32,128]{2,1,0:T(8,128)(2,1)S(1)}, u32[]{:S(2)}, u32[]{:S(2)}) async-start(bf16[32,32,128]{2,1,0:T(8,128)(2,1)} %get-tuple-element.16), calls=%async_computation | async-start | bytes 524288 | tf_op jit(solution)/shard_map/all_to_all | solution.py:52
  14.0 14.2 %collective-permute-start.1 = (bf16[8,128,256]{2,1,0:T(8,128)(2,1)}, bf16[8,128,256]{2,1,0:T(8,128)(2,1)S(1)}, u32[]{:S(2)}, u32[]{:S(2)}) collective-permute-start(bf16[8,128,256]{2,1,0:T(8,128)(2,1)} %k_ref.1), channel_id=1, source_target_pairs={{0,4},{4,0},{8,12},{12,8},{16,20},{20,16},{24,28},{28,24},{32,36},... | collective-permute-start | bytes 1572872 | tf_op jit(solution)/shard_map/ppermute | solution.py:48
  14.1 14.1 %collective-permute-start.2 = (bf16[8,128,256]{2,1,0:T(8,128)(2,1)}, bf16[8,128,256]{2,1,0:T(8,128)(2,1)S(1)}, u32[]{:S(2)}, u32[]{:S(2)}) collective-permute-start(bf16[8,128,256]{2,1,0:T(8,128)(2,1)} %v_ref.1), channel_id=1, source_target_pairs={{0,4},{4,0},{8,12},{12,8},{16,20},{20,16},{24,28},{28,24},{32,36},... | collective-permute-start | bytes 1572872 | tf_op jit(solution)/shard_map/ppermute | solution.py:48
  26.7 1.6 collective-permute-start
  26.7 1.5 collective-permute-start.3
  28.2 0.7 copy-start.2
  28.9 42.2 %copy-start.1 = (bf16[4096,256]{1,0:T(8,128)(2,1)S(1)}, bf16[4096,256]{1,0:T(8,128)(2,1)}, u32[]{:S(2)}) copy-start(bf16[4096,256]{1,0:T(8,128)(2,1)} %w_ref.1) | copy-start | bytes 6291460
  69.6 1.5 collective-permute-start.4
  72.3 43.3 %copy-start = (bf16[104,16384]{1,0:T(8,128)(2,1)S(1)}, bf16[104,16384]{1,0:T(8,128)(2,1)}, u32[]{:S(2)}) copy-start(bf16[104,16384]{1,0:T(8,128)(2,1)} %down_ref.1) | copy-start | bytes 10223620
  112.8 2.8 %collective-permute-start.5 = (bf16[16,144,256]{2,1,0:T(8,128)(2,1)S(1)}, bf16[16,144,256]{2,1,0:T(8,128)(2,1)S(1)}, u32[]{:S(2)}, u32[]{:S(2)}) collective-permute-start(bf16[16,144,256]{2,1,0:T(8,128)(2,1)S(1)} %all_to_all.44.own_ref), channel_id=1, source_target_pairs={{0,4},{4,0},{8,12},{12,8},{16,20},{20,16},{24,28},{28,24},{32,36},... | collective-permute-start | bytes 3538952 | tf_op jit(solution)/shard_map/ppermute | solution.py:48
  120.4 2.7 %collective-permute-start.6 = (bf16[16,128,256]{2,1,0:T(8,128)(2,1)S(1)}, bf16[16,128,256]{2,1,0:T(8,128)(2,1)S(1)}, u32[]{:S(2)}, u32[]{:S(2)}) collective-permute-start(bf16[16,128,256]{2,1,0:T(8,128)(2,1)S(1)} %get-tuple-element.24), channel_id=1, source_target_pairs={{0,4},{4,0},{8,12},{12,8},{16,20},{20,16},{24,28},{28,24},{32,36},... | collective-permute-start | bytes 3145736 | tf_op jit(solution)/shard_map/ppermute | solution.py:48

commit v4 on v3

--- a/solution.py
+++ b/solution.py
@@ -17,10 +17,13 @@
 SHARD = 128
 COLS = 256
 HIDDEN = 104
+STAT_ROW = 4
+GAIN_ROW = 5
+ROWS_OUT = HALF + 8
 EPS = 1e-05
 SCALE = HD ** (-0.5)
 FLOOR = -1e30
-VMEM_LIMIT = 24 * 1024 * 1024
+VMEM_LIMIT = 18 * 1024 * 1024
 
 bf16 = jnp.bfloat16
 f32 = jnp.float32
@@ -41,6 +44,11 @@
     for z in range(NZ)
     for c in range(NC)
 ]
+G_YZ = [
+    [all_index(z, x, c, y) for z in range(NZ) for y in range(NY)]
+    for x in range(NX)
+    for c in range(NC)
+]
 CORE_PAIRS = [(i, i ^ 1) for i in range(NZ * NX * NC)]
 
 
@@ -73,7 +81,21 @@
 
 
 def prepare_kernel(
-    prompt_ref, len_ref, query_ref, k_ref, v_ref, block_ref, k_out, v_out, order_ref, rows, count, sems
+    prompt_ref,
+    len_ref,
+    query_ref,
+    draft_ref,
+    gain_ref,
+    k_ref,
+    v_ref,
+    block_ref,
+    k_out,
+    v_out,
+    extra_ref,
+    order_ref,
+    rows,
+    count,
+    sems,
 ):
     k_copy = pltpu.make_async_copy(k_ref, k_out, sems.at[0])
     v_copy = pltpu.make_async_copy(v_ref, v_out, sems.at[1])
@@ -85,6 +107,13 @@
     block = rows[...].astype(bf16)
     for i in range(PEERS):
         block_ref[i] = block
+    extra_ref[...] = jnp.zeros((2, 8, HD), f32)
+    gain = gain_ref[...].astype(f32).reshape(1, COLS)
+    draft = draft_ref[0].astype(f32)
+    for kv in range(2):
+        for i in range(2):
+            extra_ref[kv, i : i + 1, :] = draft[i : i + 1, kv * HD : (kv + 1) * HD]
+            extra_ref[kv, GAIN_ROW + i : GAIN_ROW + i + 1, :] = gain[:, i * HD : (i + 1) * HD]
     for p in range(PROMPTS):
         count[p] = 0
         order_ref[TOKS + p] = len_ref[p]
@@ -111,23 +140,16 @@
     v_ref,
     k2_ref,
     v2_ref,
-    draft_ref,
+    extra_ref,
     draft2_ref,
     out_ref,
     gath,
-    extra,
+    tail,
 ):
     kvp = lax.axis_index("kvp")
     core = lax.rem(kvp, 2)
     gath[0:PEERS] = own_ref[...]
     gath[PEERS : 2 * PEERS] = oth_ref[...]
-    extra[...] = jnp.zeros((GROUP, HD), f32)
-    for side, ref in enumerate((draft_ref, draft2_ref)):
-        both = ref[0].astype(f32)
-        for i in range(4):
-            row = side * 4 + i
-            extra[row : row + 1, :] = both[i // 2 : i // 2 + 1, (i % 2) * HD : (i % 2 + 1) * HD]
-    extras = extra[...]
     to_row = row_ids((256, 256))
     from_row = lane_ids((256, 256))
     regroup = (
@@ -180,14 +202,17 @@
                 out_ref[kv * GROUP + g, pair * 16 : pair * 16 + 16, :] = both[
                     g * 16 : (g + 1) * 16, :
                 ]
-        inner = row_ids((GROUP, HD))
+        inner = row_ids((8, HD))
+        tail[...] = extra_ref[kv]
+        tail[2:4, :] = draft2_ref[0].astype(f32)[:, cols]
+        extras = tail[...]
         for g in range(GROUP):
-            out_ref[kv * GROUP + g, HALF : HALF + 16, :] = jnp.where(
-                inner == 8, stats[g : g + 1, :], extras
+            out_ref[kv * GROUP + g, HALF:ROWS_OUT, :] = jnp.where(
+                inner == STAT_ROW, stats[g : g + 1, :], extras
             ).astype(bf16)
 
 
-def combine_kernel(order_ref, part_ref, gath, out_ref, stat, turn):
+def combine_kernel(order_ref, part_ref, gath, out_ref, gain_ref, stat, turn):
     kvp = lax.axis_index("kvp")
     core = lax.rem(kvp, 2)
     head = kvp // 2
@@ -201,22 +226,25 @@
         query_tiles.append(gath[gather_row(order_ref, slot, core), pl.ds(first, GROUP), :])
         slot_token = jnp.where(slots == s, order_ref[slot], slot_token)
     for i in range(PEERS):
-        tile = part_ref[i, HALF : HALF + 16, :]
+        tile = part_ref[i, HALF:ROWS_OUT, :].astype(f32)
         draft_tiles.append(tile)
-        stat[i : i + 1, :] = tile.astype(f32)[8:9, :]
+        stat[i : i + 1, :] = tile[STAT_ROW : STAT_ROW + 1, :]
+        for j in range(2):
+            gain_ref[i : i + 1, j * HD : (j + 1) * HD] = tile[GAIN_ROW + j : GAIN_ROW + j + 1, :]
     shape = (HALF, HALF * GROUP)
-    outer = lane_ids(shape) // GROUP
-    inner = lane_ids(shape) % GROUP
-    pick = ((row_ids(shape) == outer) & (inner == head % GROUP)).astype(bf16)
+    pick = (
+        (row_ids(shape) == lane_ids(shape) // GROUP) & (lane_ids(shape) % GROUP == head % GROUP)
+    ).astype(bf16)
     queries = nn_dot(pick, jnp.concatenate(query_tiles, axis=0)).astype(bf16)
-    drafts = jnp.concatenate(draft_tiles, axis=0)
+    drafts = jnp.concatenate(draft_tiles, axis=0).astype(bf16)
     scores = nt_dot(queries, drafts) * SCALE
-    slot_token = jnp.concatenate([slot_token] * 4, axis=1)
-    side = inner // 4
-    key_token = 2 * outer + jnp.where(side == 0, core, 1 - core)
+    shape = (HALF, PEERS * 8)
+    outer = lane_ids(shape) // 8
+    inner = lane_ids(shape) % 8
+    slot_token = jnp.concatenate([slot_token] * 2, axis=1)
+    key_token = 2 * outer + jnp.where(inner == 0, core, 1 - core)
     visible = (
-        (inner % 4 == kv)
-        & (side < 2)
+        ((inner == 0) | (inner == 2))
         & (slot_token % HALF == key_token % HALF)
         & (key_token // HALF <= slot_token // HALF)
     )
@@ -239,14 +267,15 @@
     weights = jnp.where(visible, jnp.exp(scores - top), 0.0)
     scale = jnp.exp(top_cache - top)
     total = scale * total + jnp.sum(weights, axis=1, keepdims=True)
-    summed = scale * summed + nn_dot(pltpu.roll(weights, 2, 1).astype(bf16), drafts)
+    summed = scale * summed + nn_dot(pltpu.roll(weights, 1, 1).astype(bf16), drafts)
     attn = (summed / total).astype(bf16)
     for i in range(PEERS):
         out_ref[i] = attn
 
 
-def project_kernel(order_ref, own_ref, oth_ref, w_ref, out_ref, by_slot, by_token):
+def project_kernel(order_ref, own_ref, oth_ref, w_ref, stream_ref, out_ref, by_slot, by_token):
     core = lax.rem(lax.axis_index("kvp"), 2)
+    tp = lax.axis_index("tp")
     acc = jnp.zeros((TOKS, COLS), f32)
     for i in range(HEADS // 2):
         lhs = jnp.concatenate(
@@ -261,81 +290,82 @@
     for r in range(TOKS):
         t = order_ref[lax.rem(r + HALF * core, TOKS)]
         by_token[pl.ds(t, 1), :] = by_slot[r : r + 1, :]
+    mine = pl.ds(pl.multiple_of(tp * 16, 16), 16)
+    by_token[mine, :] = by_token[mine, :] + stream_ref[...].astype(f32)
     for y in range(NY):
-        out_ref[y] = by_token[16 * y : 16 * y + 16, :]
-
-
-def norm_kernel(parts_ref, stream_ref, gain_ref, msg_ref, mid_ref):
-    middle = (
-        (parts_ref[0] + parts_ref[1]) + (parts_ref[2] + parts_ref[3])
-    ) + stream_ref[...].astype(f32)
-    mid_ref[...] = middle
-    scaled = (middle * gain_ref[...].astype(f32).reshape(1, COLS)).astype(bf16)
-    squares = jnp.sum(middle * middle, axis=1, keepdims=True)
-    high = squares.astype(bf16).astype(f32)
-    low = squares - high
-    lanes = lane_ids((16, HD))
-    stats = jnp.where(lanes == 0, high, jnp.where(lanes == 1, low, 0.0)).astype(bf16)
-    block = jnp.concatenate([scaled, stats], axis=1)
-    for i in range(NZ):
-        msg_ref[i] = block
-
-
-def spread_kernel(in_ref, out_ref):
-    stats = jnp.zeros((16, HD), f32)
+        rows = by_token[16 * y : 16 * y + 16, :].astype(bf16)
+        for z in range(NZ):
+            out_ref[z * NY + y] = rows
+
+
+def spread_kernel(in_ref, gain_ref, out_ref, mid_ref, whole):
+    mine = lax.axis_index("kvp") // NC
+    x = lax.rem(mine, NX)
+    squares = jnp.zeros((16, 1), f32)
     for z in range(NZ):
-        stats = stats + in_ref[z, :, COLS:].astype(f32)
-    squares = stats[:, 0:1] + stats[:, 1:2]
+        parts = [in_ref[z * NY + y].astype(f32) for y in range(NY)]
+        middle = (parts[0] + parts[1]) + (parts[2] + parts[3])
+        whole[z] = middle
+        squares = squares + jnp.sum(middle * middle, axis=1, keepdims=True)
+        scaled = (middle * gain_ref[pl.ds(z * NX + x, 1), :]).astype(bf16)
+        for i in range(NX * NY):
+            out_ref[i, z * 16 : (z + 1) * 16, :] = scaled
+    mid_ref[...] = whole[mine // NX]
     high = squares.astype(bf16).astype(f32)
     low = squares - high
     lanes = lane_ids((16, COLS))
     tile = jnp.where(lanes == 0, high, jnp.where(lanes == 1, low, 0.0)).astype(bf16)
     for i in range(NX * NY):
-        for z in range(NZ):
-            out_ref[i, z * 16 : (z + 1) * 16, :] = in_ref[z, :, :COLS]
         out_ref[i, NZ * 16 :, :] = tile
 
 
-def feed_kernel(own_ref, oth_ref, gu_ref, down_ref, send_ref, keep_ref, weights, sems):
+def sum_of_squares(src_ref):
+    columns = []
+    for y in range(NY):
+        stats = jnp.zeros((16, HD), f32)
+        for x in range(NX):
+            stats = stats + src_ref[x * NY + y, NZ * 16 :, :HD].astype(f32)
+        columns.append(stats[:, 0:1] + stats[:, 1:2])
+    return jnp.concatenate(columns, axis=0)
+
+
+def token_rows(src_ref, i):
+    z, x = i // NX, i % NX
+    return jnp.concatenate(
+        [src_ref[x * NY + y, z * 16 : (z + 1) * 16, :] for y in range(NY)], axis=0
+    )
+
+
+def gate_kernel(rows_ref, gu_ref, gu2_ref, sums_ref):
     core = lax.rem(lax.axis_index("kvp"), 2)
-    width = D // NZ
-    copies = [
-        pltpu.make_async_copy(
-            gu_ref.at[:, :, pl.ds(z * width, width)], weights.at[z], sems.at[z]
-        )
-        for z in range(NZ)
-    ]
-    for copy in copies:
-        copy.start()
-    gate = jnp.zeros((TOKS, HIDDEN), f32)
-    up = jnp.zeros((TOKS, HIDDEN), f32)
-    stats = [jnp.zeros((16, HD), f32) for _ in range(NY)]
-    for x in range(NX):
+    sums = [jnp.zeros((TOKS, HIDDEN), f32) for _ in range(4)]
+    sums_ref[4] = jnp.broadcast_to(sum_of_squares(rows_ref), (TOKS, HD))
+    for i in range(PEERS):
+        rows = token_rows(rows_ref, i)
+        cols = pl.ds(pl.multiple_of((2 * i + core) * COLS, COLS), COLS)
+        for j, ref in enumerate((gu_ref, gu2_ref)):
+            for k in range(2):
+                sums[2 * j + k] = sums[2 * j + k] + nt_dot(rows, ref[k, :, cols])
+    for j in range(4):
+        sums_ref[j, :, :HIDDEN] = sums[j]
+
+
+def down_kernel(own_ref, oth_ref, down_ref, down2_ref, out_ref):
+    core = lax.rem(lax.axis_index("kvp"), 2)
+    squares = own_ref[4][:, 0:1] + oth_ref[4][:, 0:1]
+    rscale = lax.rsqrt(squares / D + EPS)
+    hidden = []
+    for j in range(2):
+        gate = (own_ref[2 * j] + oth_ref[2 - 2 * j])[:, :HIDDEN] * rscale
+        up = (own_ref[2 * j + 1] + oth_ref[3 - 2 * j])[:, :HIDDEN] * rscale
+        hidden.append((gate / (1.0 + jnp.exp(-gate)) * up).astype(bf16))
+    for i in range(PEERS):
+        z, x = i // NX, i % NX
+        cols = pl.ds(pl.multiple_of((2 * i + core) * COLS, COLS), COLS)
+        part = nn_dot(hidden[0], down_ref[:, cols]) + nn_dot(hidden[1], down2_ref[:, cols])
+        part = part.astype(bf16)
         for y in range(NY):
-            for src_ref in (own_ref, oth_ref):
-                stats[y] = stats[y] + src_ref[x * NY + y, NZ * 16 :, :HD].astype(f32)
-    for z in range(NZ):
-        copies[z].wait()
-        for x in range(NX):
-            for src_ref, side in ((own_ref, core), (oth_ref, 1 - core)):
-                rows = jnp.concatenate(
-                    [src_ref[x * NY + y, z * 16 : (z + 1) * 16, :] for y in range(NY)], axis=0
-                )
-                cols = pl.ds(pl.multiple_of((2 * x + side) * COLS, COLS), COLS)
-                gate = gate + nt_dot(rows, weights[z, 0, :, cols])
-                up = up + nt_dot(rows, weights[z, 1, :, cols])
-    squares = jnp.concatenate([s[:, 0:1] + s[:, 1:2] for s in stats], axis=0)
-    rscale = lax.rsqrt(squares / D + EPS)
-    gate = gate * rscale
-    up = up * rscale
-    hidden = (gate / (1.0 + jnp.exp(-gate)) * up).astype(bf16)
-    for out_ref, side in ((send_ref, 1 - core), (keep_ref, core)):
-        for z in range(NZ):
-            for x in range(NX):
-                cols = pl.ds(pl.multiple_of((2 * (z * NX + x) + side) * COLS, COLS), COLS)
-                part = nn_dot(hidden, down_ref[:, cols]).astype(out_ref.dtype)
-                for y in range(NY):
-                    out_ref[x * NY + y, z * 16 : (z + 1) * 16, :] = part[16 * y : 16 * y + 16]
+            out_ref[x * NY + y, z * 16 : (z + 1) * 16, :] = part[16 * y : 16 * y + 16]
 
 
 VMEM = pl.BlockSpec(memory_space=pltpu.VMEM)
@@ -377,78 +407,92 @@
     cache = shape((PROMPTS, SHARD, 2 * HD), bf16)
     key_pair, value_pair = swap_cores(key_cache), swap_cores(value_cache)
     draft_pair = swap_cores(draft_kv)
-    block, keys, values, order = call(
+    block, keys, values, extra, order = call(
         prepare_kernel,
         "prepare",
-        [SMEM, SMEM, VMEM, HBM, HBM],
+        [SMEM, SMEM, VMEM, VMEM, VMEM, HBM, HBM],
         [
             shape((PEERS, HEADS, HD), bf16),
             cache,
             cache,
+            shape((2, 8, HD), f32),
             shape((TOKS + PROMPTS,), jnp.int32),
         ],
-        [VMEM, VMEM, VMEM, SMEM],
+        [VMEM, VMEM, VMEM, VMEM, SMEM],
         [
             pltpu.VMEM((HEADS, HD), f32),
             pltpu.SMEM((PROMPTS,), jnp.int32),
             pltpu.SemaphoreType.DMA((2,)),
         ],
-    )(in_hbm(prompt_of), in_hbm(prefix_len), in_hbm(query), in_hbm(key_cache), in_hbm(value_cache))
+    )(
+        in_hbm(prompt_of),
+        in_hbm(prefix_len),
+        in_hbm(query),
+        in_hbm(draft_kv),
+        in_hbm(norm_gain),
+        in_hbm(key_cache),
+        in_hbm(value_cache),
+    )
+    block, draft_pair, key_pair, value_pair = lax.optimization_barrier(
+        (block, draft_pair, key_pair, value_pair)
+    )
     own = swap_plane(block)
     oth = swap_cores(own)
     part, gath = call(
         attention_kernel,
         "attention",
         [SMEM] + [VMEM] * 8,
-        [shape((HEADS, 48, HD), bf16), shape((TOKS, HEADS, HD), bf16)],
+        [shape((HEADS, ROWS_OUT, HD), bf16), shape((TOKS, HEADS, HD), bf16)],
         [VMEM, VMEM],
-        [pltpu.VMEM((GROUP, HD), f32)],
-    )(order, own, oth, keys, values, key_pair, value_pair, draft_kv, draft_pair)
-    attn = call(
+        [pltpu.VMEM((8, HD), f32)],
+    )(order, own, oth, keys, values, key_pair, value_pair, extra, draft_pair)
+    part, gate_up_sent = lax.optimization_barrier((part, gate_up))
+    gate_up_pair = swap_cores(gate_up_sent)
+    attn, gains = call(
         combine_kernel,
         "combine",
         [SMEM, VMEM, VMEM],
-        shape((PEERS, HALF, HD), bf16),
-        VMEM,
+        [shape((PEERS, HALF, HD), bf16), shape((PEERS, COLS), f32)],
+        [VMEM, VMEM],
         [pltpu.VMEM((PEERS, HD), f32), pltpu.VMEM((HD, HD), f32)],
     )(order, swap_plane(part), gath)
+    attn, down_sent = lax.optimization_barrier((attn, down_weight))
+    down_pair = swap_cores(down_sent)
     attn_own = swap_plane(attn)
     attn_oth = swap_cores(attn_own)
     partial = call(
         project_kernel,
         "project",
-        [SMEM, VMEM, VMEM, VMEM],
-        shape((NY, 16, COLS), f32),
+        [SMEM, VMEM, VMEM, VMEM, VMEM],
+        shape((NZ * NY, 16, COLS), bf16),
         VMEM,
         [pltpu.VMEM((TOKS, COLS), f32), pltpu.VMEM((TOKS, COLS), f32)],
-    )(order, attn_own, attn_oth, out_weight)
-    partial = lax.all_to_all(partial, "tp", 0, 0, tiled=True)
+    )(order, attn_own, attn_oth, out_weight, in_hbm(stream))
+    partial = lax.all_to_all(partial, ("kvp", "tp"), 0, 0, axis_index_groups=G_YZ, tiled=True)
     msg, middle = call(
-        norm_kernel,
-        "norm",
-        [VMEM, VMEM, VMEM],
-        [shape((NZ, 16, COLS + HD), bf16), shape((16, COLS), f32)],
+        spread_kernel,
+        "spread",
         [VMEM, VMEM],
-    )(partial, in_hbm(stream), in_hbm(norm_gain))
-    msg = lax.all_to_all(msg, "kvp", 0, 0, axis_index_groups=G_Z, tiled=True)
-    msg = call(spread_kernel, "spread", [VMEM], shape((NX * NY, NZ * 16 + 16, COLS), bf16), VMEM)(
-        msg
-    )
-    normed_own = swap_face(msg)
-    normed_oth = swap_cores(normed_own)
-    send, keep = call(
-        feed_kernel,
-        "feed",
-        [VMEM, VMEM, HBM, VMEM],
-        [shape((NX * NY, NZ * 16, COLS), bf16), shape((NX * NY, NZ * 16, COLS), f32)],
+        [shape((NX * NY, NZ * 16 + 16, COLS), bf16), shape((16, COLS), f32)],
         [VMEM, VMEM],
-        [
-            pltpu.VMEM((NZ, 2, HIDDEN, D // NZ), bf16),
-            pltpu.SemaphoreType.DMA((NZ,)),
-        ],
-    )(normed_own, normed_oth, in_hbm(gate_up), down_weight)
-    summed = (keep + swap_cores(send).astype(f32)).astype(bf16)
-    summed = swap_face(summed)
+        [pltpu.VMEM((NZ, 16, COLS), f32)],
+    )(partial, gains)
+    normed = swap_face(msg)
+    sums = call(
+        gate_kernel,
+        "gate",
+        [VMEM] * 3,
+        shape((5, TOKS, HD), f32),
+        VMEM,
+    )(normed, gate_up, gate_up_pair)
+    partial = call(
+        down_kernel,
+        "down",
+        [VMEM] * 4,
+        shape((NX * NY, NZ * 16, COLS), bf16),
+        VMEM,
+    )(sums, swap_cores(sums), down_weight, down_pair)
+    summed = swap_face(partial)
     summed = jnp.sum(summed.astype(f32), axis=0).astype(bf16).reshape(NZ, 16, COLS)
     summed = lax.all_to_all(summed, "kvp", 0, 0, axis_index_groups=G_Z, tiled=True)
     return (middle + jnp.sum(summed.astype(f32), axis=0)).astype(bf16)

time: 157 us -> 150 us (0.955)
  blocking collectives: 107 us -> 131 us
  waiting for transfers between devices: 20 us -> 4.45 us
  starting transfers between devices: 12.7 us -> 1.02 us
  Pallas kernels: 14 us -> 12.3 us
    all_to_all x2 -> x3, blocking collectives: 36.2 us -> 60.6 us  [swap_plane(): lax.all_to_all(array, 'kvp', 0, 0, axis_index_groups=G_XZ, tiled=True)]
    all_to_all x1 -> x0, waiting for transfers between devices: 12.1 us -> none  [swap_plane(): lax.all_to_all(array, 'kvp', 0, 0, axis_index_groups=G_XZ, tiled=True)]
    all_to_all x1 -> x0, starting transfers between devices: 11.3 us -> none  [swap_plane(): lax.all_to_all(array, 'kvp', 0, 0, axis_index_groups=G_XZ, tiled=True)]
    ppermute x7 -> x8, waiting for transfers between devices: 7.93 us -> 4.45 us  [swap_cores(): return lax.ppermute(array, 'kvp', CORE_PAIRS)]
    all_to_all x2 -> x1, blocking collectives: 20.2 us -> 17.1 us  [on_device(): lax.all_to_all(partial, ('kvp', 'tp'), 0, 0, axis_index_groups=G_YZ, tile...]
    all_to_all x2, blocking collectives: 40.1 us -> 42.2 us  [swap_face(): lax.all_to_all(array, ('kvp', 'tp'), 0, 0, axis_index_groups=G_XY, tiled=...]
    pallas_call x7, Pallas kernels: 14 us -> 12.3 us  [the longest x1 2.97 us: on_device(): call(attention_kernel, 'attention', [SMEM] + [VMEM] * 8, [shape((HEADS, R...]
  transfers between devices with their start and end apart: 8 -> 8, of which waited for: 5 -> 3; matrix products, arithmetic and copies ran while one was open for 0% -> 0% of each run, Pallas kernels for 0% -> 6%
where the time goes in v4:
time: 150 us
  blocking collectives  131 us (87%)
  Pallas kernels  12.3 us (8%)
  waiting for transfers between devices  4.45 us (3%)
    all_to_all x3, blocking collectives, swap_plane(): lax.all_to_all(array, 'kvp', 0, 0, axis_index_groups=G_XZ, tiled=True)  60.6 us
    all_to_all x2, blocking collectives, swap_face(): lax.all_to_all(array, ('kvp', 'tp'), 0, 0, axis_index_groups=G_XY, tiled=...  42.2 us
    all_to_all x1, blocking collectives, on_device(): lax.all_to_all(partial, ('kvp', 'tp'), 0, 0, axis_index_groups=G_YZ, tile...  17.1 us
    all_to_all x1, blocking collectives, on_device(): lax.all_to_all(summed, 'kvp', 0, 0, axis_index_groups=G_Z, tiled=True)  11.1 us
    ppermute x8, waiting for transfers between devices, swap_cores(): return lax.ppermute(array, 'kvp', CORE_PAIRS)  4.45 us
  transfers between devices with their start and end apart: 8, of which 3 were waited for; matrix products, arithmetic and copies ran while one was open for 0% of the time, Pallas kernels for 6%

profile of v4, /device:TPU:8, one launch (start us, length us, event | category | flops | bytes accessed | tf_op | source)
XLA Modules:
  0.0 149.7 jit_solution(6786220463059407962)
XLA Ops:
  0.0 0.0 copy-start.1
  0.0 0.0 copy-start.2
  0.0 0.0 collective-permute-start.1
  0.0 0.5 collective-permute-start.2
  0.5 0.1 collective-permute-start
  0.6 2.9 %prepare.1 = (bf16[32,32,128]{2,1,0:T(8,128)(2,1)S(1)}, bf16[8,128,256]{2,1,0:T(8,128)(2,1)S(1)}, bf16[8,128,256]{2,1,0:T(8,128)(2,1)S(1)}, f32[2,8,128]{2,1,0:T(8,128)S(1)}, s32[72]{0:T(128)S(1)}) custom-call(s32[32]{0:T(128)} %prompt_ref.1, s32[8]{0:T(128)} %len_ref.1, bf16[1,4096]{1,0:T(2,128)(2,1)} %query_ref.1, bf16[1,2,256]{2,1,0:T(2,128)(2,1)} %draft_ref.1, ...), custom_call_target="tpu_custom_call" | custom-call | tf_op jit(solution)/shard_map/prepare/pallas_call | solution.py:410
  3.5 0.0 collective-permute-done.draft2_ref
  3.5 0.0 collective-permute-done.1.k2_ref
  3.5 0.0 collective-permute-done.2.v2_ref
  3.5 24.8 %all_to_all.35.own_ref = bf16[32,32,128]{2,1,0:T(8,128)(2,1)S(1)} all-to-all(bf16[32,32,128]{2,1,0:T(8,128)(2,1)S(1)} %get-tuple-element.26), channel_id=1, replica_groups={{0,8,16,24,32,40,48,56,64,72,80,88,96,104,112,120,128,136,144,152,160,1..., dimensions={0} | all-to-all | bytes 524288 | tf_op jit(solution)/shard_map/all_to_all | solution.py:60
  28.4 0.0 collective-permute-start.3
  28.4 1.5 %collective-permute-done.3.oth_ref = bf16[32,32,128]{2,1,0:T(8,128)(2,1)S(1)} collective-permute-done((bf16[32,32,128]{2,1,0:T(8,128)(2,1)S(1)}, bf16[32,32,128]{2,1,0:T(8,128)(2,1)S(1)}, u32[]{:S(2)}, u32[]{:S(2)}) %collective-permute-start.3) | collective-permute-done | bytes 262176 | tf_op jit(solution)/shard_map/ppermute | solution.py:56
  29.9 3.0 %attention.1 = (bf16[32,40,128]{2,1,0:T(8,128)(2,1)S(1)}, bf16[64,32,128]{2,1,0:T(8,128)(2,1)S(1)}) custom-call(s32[72]{0:T(128)S(1)} %get-tuple-element.24.order_ref, bf16[32,32,128]{2,1,0:T(8,128)(2,1)S(1)} %all_to_all.35.own_ref, bf16[32,32,128]{2,1,0:T(8,128)(2,1)S(1)} %collective-permute-done.3.oth_ref, ...), custom_call_target="tpu_custom_call" | custom-call | tf_op jit(solution)/shard_map/attention/pallas_call | solution.py:441
  32.9 0.2 collective-permute-start.5
  33.1 18.4 %all_to_all.36.part_ref = bf16[32,40,128]{2,1,0:T(8,128)(2,1)S(1)} all-to-all(bf16[32,40,128]{2,1,0:T(8,128)(2,1)S(1)} %get-tuple-element.34), channel_id=1, replica_groups={{0,8,16,24,32,40,48,56,64,72,80,88,96,104,112,120,128,136,144,152,160,1..., dimensions={0} | all-to-all | bytes 655360 | tf_op jit(solution)/shard_map/all_to_all | solution.py:60
  51.5 0.0 copy-start
  51.5 1.5 %combine.1 = (bf16[32,32,128]{2,1,0:T(8,128)(2,1)S(1)}, f32[32,256]{1,0:T(8,128)S(1)}) custom-call(s32[72]{0:T(128)S(1)} %get-tuple-element.24.order_ref, bf16[32,40,128]{2,1,0:T(8,128)(2,1)S(1)} %all_to_all.36.part_ref, bf16[64,32,128]{2,1,0:T(8,128)(2,1)S(1)} %get-tuple-element.35.gath), custom_call_target="tpu_custom_call" | custom-call | tf_op jit(solution)/shard_map/combine/pallas_call | solution.py:451
  53.0 0.0 copy-done.1
  53.0 0.1 collective-permute-start.7
  53.1 17.4 %all_to_all.37.own_ref = bf16[32,32,128]{2,1,0:T(8,128)(2,1)S(1)} all-to-all(bf16[32,32,128]{2,1,0:T(8,128)(2,1)S(1)} %get-tuple-element.37), channel_id=1, replica_groups={{0,8,16,24,32,40,48,56,64,72,80,88,96,104,112,120,128,136,144,152,160,1..., dimensions={0} | all-to-all | bytes 524288 | tf_op jit(solution)/shard_map/all_to_all | solution.py:60
  70.5 0.0 collective-permute-start.4
  70.5 1.5 %collective-permute-done.4.oth_ref = bf16[32,32,128]{2,1,0:T(8,128)(2,1)S(1)} collective-permute-done((bf16[32,32,128]{2,1,0:T(8,128)(2,1)S(1)}, bf16[32,32,128]{2,1,0:T(8,128)(2,1)S(1)}, u32[]{:S(2)}, u32[]{:S(2)}) %collective-permute-start.4) | collective-permute-done | bytes 262176 | tf_op jit(solution)/shard_map/ppermute | solution.py:56
  72.0 0.0 copy-done.2
  72.0 1.3 project.1
  73.4 17.1 %all_to_all.38.in_ref = bf16[32,16,256]{2,1,0:T(8,128)(2,1)S(1)} all-to-all(bf16[32,16,256]{2,1,0:T(8,128)(2,1)S(1)} %project.1), channel_id=1, replica_groups={{0,1,2,3,32,33,34,35,64,65,66,67,96,97,98,99,128,129,130,131,160,161,16..., dimensions={0} | all-to-all | bytes 524288 | tf_op jit(solution)/shard_map/all_to_all | solution.py:471
  90.4 0.2 spread.1
  90.6 21.3 %all_to_all.39.rows_ref = bf16[16,144,256]{2,1,0:T(8,128)(2,1)S(1)} all-to-all(bf16[16,144,256]{2,1,0:T(8,128)(2,1)S(1)} %get-tuple-element.40), channel_id=1, replica_groups={{0,1,2,3,8,9,10,11,16,17,18,19,24,25,26,27},{4,5,6,7,12,13,14,15,20,21,..., dimensions={0} | all-to-all | bytes 2359296 | tf_op jit(solution)/shard_map/all_to_all | solution.py:64
  111.9 0.0 collective-permute-done.5.gu2_ref
  111.9 0.0 copy-done
  111.9 2.7 %gate.1.own_ref = f32[5,64,128]{2,1,0:T(8,128)S(1)} custom-call(bf16[16,144,256]{2,1,0:T(8,128)(2,1)S(1)} %all_to_all.39.rows_ref, bf16[2,104,16384]{2,1,0:T(8,128)(2,1)S(1)} %copy-done, bf16[2,104,16384]{2,1,0:T(8,128)(2,1)S(1)} %collective-permute-done.5.gu2_ref), custom_call_target="tpu_custom_call" | custom-call | tf_op jit(solution)/shard_map/gate/pallas_call | solution.py:481
  114.6 0.1 collective-permute-start.6
  114.7 0.0 collective-permute-done.7.down2_ref
  114.7 1.4 collective-permute-done.6.oth_ref
  116.1 0.8 down.1
  116.9 20.9 %all_to_all.40 = bf16[16,128,256]{2,1,0:T(8,128)(2,1)S(1)} all-to-all(bf16[16,128,256]{2,1,0:T(8,128)(2,1)S(1)} %down.1), channel_id=1, replica_groups={{0,1,2,3,8,9,10,11,16,17,18,19,24,25,26,27},{4,5,6,7,12,13,14,15,20,21,..., dimensions={0} | all-to-all | bytes 2097152 | tf_op jit(solution)/shard_map/all_to_all | solution.py:64
  137.8 0.1 reduce_sum.21
  137.9 11.1 %all_to_all.41 = bf16[8,16,256]{2,1,0:T(8,128)(2,1)S(1)} all-to-all(bf16[8,16,256]{2,1,0:T(8,128)(2,1)S(1)} %bitcast.1), channel_id=1, replica_groups={{0,32,64,96,128,160,192,224},{4,36,68,100,132,164,196,228},{8,40,72,104..., dimensions={0} | all-to-all | bytes 131072 | tf_op jit(solution)/shard_map/all_to_all | solution.py:497
  149.1 0.6 add_convert_fusion
  (1 shorter events, 0.0 us)
Async XLA Ops:
  0.0 53.0 %copy-start.1 = (bf16[104,16384]{1,0:T(8,128)(2,1)S(1)}, bf16[104,16384]{1,0:T(8,128)(2,1)}, u32[]{:S(2)}) copy-start(bf16[104,16384]{1,0:T(8,128)(2,1)} %down_ref.1) | copy-start | bytes 10223620
  0.0 72.0 %copy-start.2 = (bf16[4096,256]{1,0:T(8,128)(2,1)S(1)}, bf16[4096,256]{1,0:T(8,128)(2,1)}, u32[]{:S(2)}) copy-start(bf16[4096,256]{1,0:T(8,128)(2,1)} %w_ref.1) | copy-start | bytes 6291460
  0.0 3.5 %collective-permute-start.1 = (bf16[8,128,256]{2,1,0:T(8,128)(2,1)}, bf16[8,128,256]{2,1,0:T(8,128)(2,1)S(1)}, u32[]{:S(2)}, u32[]{:S(2)}) collective-permute-start(bf16[8,128,256]{2,1,0:T(8,128)(2,1)} %k_ref.1), channel_id=1, source_target_pairs={{0,4},{4,0},{8,12},{12,8},{16,20},{20,16},{24,28},{28,24},{32,36},... | collective-permute-start | bytes 1572872 | tf_op jit(solution)/shard_map/ppermute | solution.py:56
  0.0 3.5 %collective-permute-start.2 = (bf16[8,128,256]{2,1,0:T(8,128)(2,1)}, bf16[8,128,256]{2,1,0:T(8,128)(2,1)S(1)}, u32[]{:S(2)}, u32[]{:S(2)}) collective-permute-start(bf16[8,128,256]{2,1,0:T(8,128)(2,1)} %v_ref.1), channel_id=1, source_target_pairs={{0,4},{4,0},{8,12},{12,8},{16,20},{20,16},{24,28},{28,24},{32,36},... | collective-permute-start | bytes 1572872 | tf_op jit(solution)/shard_map/ppermute | solution.py:56
  0.5 3.0 %collective-permute-start = (bf16[1,2,256]{2,1,0:T(2,128)(2,1)}, bf16[1,2,256]{2,1,0:T(2,128)(2,1)S(1)}, u32[]{:S(2)}, u32[]{:S(2)}) collective-permute-start(bf16[1,2,256]{2,1,0:T(2,128)(2,1)} %draft_ref.1), channel_id=1, source_target_pairs={{0,4},{4,0},{8,12},{12,8},{16,20},{20,16},{24,28},{28,24},{32,36},... | collective-permute-start | bytes 3080 | tf_op jit(solution)/shard_map/ppermute | solution.py:56
  28.4 1.5 %collective-permute-start.3 = (bf16[32,32,128]{2,1,0:T(8,128)(2,1)S(1)}, bf16[32,32,128]{2,1,0:T(8,128)(2,1)S(1)}, u32[]{:S(2)}, u32[]{:S(2)}) collective-permute-start(bf16[32,32,128]{2,1,0:T(8,128)(2,1)S(1)} %all_to_all.35.own_ref), channel_id=1, source_target_pairs={{0,4},{4,0},{8,12},{12,8},{16,20},{20,16},{24,28},{28,24},{32,36},... | collective-permute-start | bytes 786440 | tf_op jit(solution)/shard_map/ppermute | solution.py:56
  32.9 79.0 %collective-permute-start.5 = (bf16[2,104,16384]{2,1,0:T(8,128)(2,1)}, bf16[2,104,16384]{2,1,0:T(8,128)(2,1)S(1)}, u32[]{:S(2)}, u32[]{:S(2)}) collective-permute-start(bf16[2,104,16384]{2,1,0:T(8,128)(2,1)} %gu_ref.1), channel_id=1, source_target_pairs={{0,4},{4,0},{8,12},{12,8},{16,20},{20,16},{24,28},{28,24},{32,36},... | collective-permute-start | bytes 20447240 | tf_op jit(solution)/shard_map/ppermute | solution.py:56
  51.5 60.4 %copy-start = (bf16[2,104,16384]{2,1,0:T(8,128)(2,1)S(1)}, bf16[2,104,16384]{2,1,0:T(8,128)(2,1)}, u32[]{:S(2)}) copy-start(bf16[2,104,16384]{2,1,0:T(8,128)(2,1)} %gu_ref.1) | copy-start | bytes 20447236
  53.0 61.7 %collective-permute-start.7 = (bf16[104,16384]{1,0:T(8,128)(2,1)S(1)}, bf16[104,16384]{1,0:T(8,128)(2,1)S(1)}, u32[]{:S(2)}, u32[]{:S(2)}) collective-permute-start(bf16[104,16384]{1,0:T(8,128)(2,1)S(1)} %copy-done.1), channel_id=1, source_target_pairs={{0,4},{4,0},{8,12},{12,8},{16,20},{20,16},{24,28},{28,24},{32,36},... | collective-permute-start | bytes 10223624 | tf_op jit(solution)/shard_map/ppermute | solution.py:56
  70.5 1.5 %collective-permute-start.4 = (bf16[32,32,128]{2,1,0:T(8,128)(2,1)S(1)}, bf16[32,32,128]{2,1,0:T(8,128)(2,1)S(1)}, u32[]{:S(2)}, u32[]{:S(2)}) collective-permute-start(bf16[32,32,128]{2,1,0:T(8,128)(2,1)S(1)} %all_to_all.37.own_ref), channel_id=1, source_target_pairs={{0,4},{4,0},{8,12},{12,8},{16,20},{20,16},{24,28},{28,24},{32,36},... | collective-permute-start | bytes 786440 | tf_op jit(solution)/shard_map/ppermute | solution.py:56
  114.6 1.5 collective-permute-start.6

commit v5 on v4

--- a/solution.py
+++ b/solution.py
@@ -97,8 +97,9 @@
     count,
     sems,
 ):
-    k_copy = pltpu.make_async_copy(k_ref, k_out, sems.at[0])
-    v_copy = pltpu.make_async_copy(v_ref, v_out, sems.at[1])
+    half = pl.ds(lax.rem(lax.axis_index("kvp"), 2) * (PROMPTS // 2), PROMPTS // 2)
+    k_copy = pltpu.make_async_copy(k_ref.at[half], k_out, sems.at[0])
+    v_copy = pltpu.make_async_copy(v_ref.at[half], v_out, sems.at[1])
     k_copy.start()
     v_copy.start()
     query = query_ref[...].astype(f32)
@@ -143,6 +144,9 @@
     extra_ref,
     draft2_ref,
     out_ref,
+    query_ref,
+    slot_ref,
+    lane_ref,
     gath,
     tail,
 ):
@@ -161,6 +165,16 @@
     here = kvp * SHARD + lanes
     there = (kvp + 1 - 2 * core) * SHARD + lanes
     position = jnp.concatenate([here, there], axis=1)
+    slots = row_ids((HALF, HD))
+    slot_token = jnp.zeros((HALF, HD), jnp.int32)
+    for s in range(HALF):
+        slot_token = jnp.where(slots == s, order_ref[HALF * core + s], slot_token)
+    slot_ref[...] = slot_token
+    row = lane_ids((8, HD))
+    row_token = jnp.full((8, HD), -1, jnp.int32)
+    for r in range(TOKS):
+        row_token = jnp.where(row == r, order_ref[lax.rem(r + HALF * core, TOKS)], row_token)
+    lane_ref[...] = row_token
     for kv in range(2):
         cols = slice(kv * HD, (kv + 1) * HD)
         stats = jnp.zeros((GROUP, SHARD), f32)
@@ -169,15 +183,15 @@
             for q_ in range(2):
                 i = pair * 2 + q_
                 p = i + 4 * core
-                queries = jnp.concatenate(
-                    [
-                        gath[gather_row(order_ref, p * 8 + j, core), kv * GROUP : (kv + 1) * GROUP, :]
-                        for j in range(8)
-                    ],
-                    axis=0,
-                )
-                keys = jnp.concatenate([k_ref[p, :, cols], k2_ref[p, :, cols]], axis=0)
-                values = jnp.concatenate([v_ref[p, :, cols], v2_ref[p, :, cols]], axis=0)
+                tiles = [
+                    gath[gather_row(order_ref, p * 8 + j, core), kv * GROUP : (kv + 1) * GROUP, :]
+                    for j in range(8)
+                ]
+                for j in range(8):
+                    query_ref[i * 8 + j, kv * GROUP : (kv + 1) * GROUP, :] = tiles[j]
+                queries = jnp.concatenate(tiles, axis=0)
+                keys = jnp.concatenate([k_ref[i, :, cols], k2_ref[p, :, cols]], axis=0)
+                values = jnp.concatenate([v_ref[i, :, cols], v2_ref[p, :, cols]], axis=0)
                 scores = nt_dot(queries, keys) * SCALE
                 visible = position < order_ref[TOKS + p]
                 top = jnp.max(jnp.where(visible, scores, FLOOR), axis=1, keepdims=True)
@@ -212,19 +226,15 @@
             ).astype(bf16)
 
 
-def combine_kernel(order_ref, part_ref, gath, out_ref, gain_ref, stat, turn):
+def combine_kernel(part_ref, query_ref, slot_ref, out_ref, gain_ref, stat, turn):
     kvp = lax.axis_index("kvp")
     core = lax.rem(kvp, 2)
     head = kvp // 2
     kv = head // GROUP
     first = pl.multiple_of(kv * GROUP, GROUP)
-    query_tiles, draft_tiles = [], []
-    slots = row_ids((HALF, HD))
-    slot_token = jnp.zeros((HALF, HD), jnp.int32)
-    for s in range(HALF):
-        slot = HALF * core + s
-        query_tiles.append(gath[gather_row(order_ref, slot, core), pl.ds(first, GROUP), :])
-        slot_token = jnp.where(slots == s, order_ref[slot], slot_token)
+    slot_token = slot_ref[...]
+    query_tiles = [query_ref[s, pl.ds(first, GROUP), :] for s in range(HALF)]
+    draft_tiles = []
     for i in range(PEERS):
         tile = part_ref[i, HALF:ROWS_OUT, :].astype(f32)
         draft_tiles.append(tile)
@@ -273,8 +283,7 @@
         out_ref[i] = attn
 
 
-def project_kernel(order_ref, own_ref, oth_ref, w_ref, stream_ref, out_ref, by_slot, by_token):
-    core = lax.rem(lax.axis_index("kvp"), 2)
+def project_kernel(token_ref, own_ref, oth_ref, w_ref, stream_ref, out_ref, by_token):
     tp = lax.axis_index("tp")
     acc = jnp.zeros((TOKS, COLS), f32)
     for i in range(HEADS // 2):
@@ -286,10 +295,12 @@
             axis=0,
         )
         acc = acc + nn_dot(lhs, w_ref[2 * i * HD : (2 * i + 2) * HD, :])
-    by_slot[...] = acc
-    for r in range(TOKS):
-        t = order_ref[lax.rem(r + HALF * core, TOKS)]
-        by_token[pl.ds(t, 1), :] = by_slot[r : r + 1, :]
+    place = (row_ids((TOKS, HD)) == token_ref[0:1, :]).astype(bf16)[:, :TOKS]
+    high = acc.astype(bf16)
+    rest = acc - high.astype(f32)
+    middle = rest.astype(bf16)
+    low = (rest - middle.astype(f32)).astype(bf16)
+    by_token[...] = nn_dot(place, high) + (nn_dot(place, middle) + nn_dot(place, low))
     mine = pl.ds(pl.multiple_of(tp * 16, 16), 16)
     by_token[mine, :] = by_token[mine, :] + stream_ref[...].astype(f32)
     for y in range(NY):
@@ -301,32 +312,14 @@
 def spread_kernel(in_ref, gain_ref, out_ref, mid_ref, whole):
     mine = lax.axis_index("kvp") // NC
     x = lax.rem(mine, NX)
-    squares = jnp.zeros((16, 1), f32)
     for z in range(NZ):
         parts = [in_ref[z * NY + y].astype(f32) for y in range(NY)]
         middle = (parts[0] + parts[1]) + (parts[2] + parts[3])
         whole[z] = middle
-        squares = squares + jnp.sum(middle * middle, axis=1, keepdims=True)
         scaled = (middle * gain_ref[pl.ds(z * NX + x, 1), :]).astype(bf16)
         for i in range(NX * NY):
             out_ref[i, z * 16 : (z + 1) * 16, :] = scaled
     mid_ref[...] = whole[mine // NX]
-    high = squares.astype(bf16).astype(f32)
-    low = squares - high
-    lanes = lane_ids((16, COLS))
-    tile = jnp.where(lanes == 0, high, jnp.where(lanes == 1, low, 0.0)).astype(bf16)
-    for i in range(NX * NY):
-        out_ref[i, NZ * 16 :, :] = tile
-
-
-def sum_of_squares(src_ref):
-    columns = []
-    for y in range(NY):
-        stats = jnp.zeros((16, HD), f32)
-        for x in range(NX):
-            stats = stats + src_ref[x * NY + y, NZ * 16 :, :HD].astype(f32)
-        columns.append(stats[:, 0:1] + stats[:, 1:2])
-    return jnp.concatenate(columns, axis=0)
 
 
 def token_rows(src_ref, i):
@@ -336,28 +329,32 @@
     )
 
 
-def gate_kernel(rows_ref, gu_ref, gu2_ref, sums_ref):
+def gate_kernel(rows_ref, gain_ref, gu_ref, gu2_ref, sums_ref):
     core = lax.rem(lax.axis_index("kvp"), 2)
-    sums = [jnp.zeros((TOKS, HIDDEN), f32) for _ in range(4)]
-    sums_ref[4] = jnp.broadcast_to(sum_of_squares(rows_ref), (TOKS, HD))
+    sums = [jnp.zeros((TOKS, 2 * HIDDEN), f32) for _ in range(2)]
+    squares = jnp.zeros((TOKS, COLS), f32)
+    inverse = 1.0 / gain_ref[...]
     for i in range(PEERS):
         rows = token_rows(rows_ref, i)
+        middle = rows.astype(f32) * inverse[i : i + 1, :]
+        squares = squares + middle * middle
         cols = pl.ds(pl.multiple_of((2 * i + core) * COLS, COLS), COLS)
         for j, ref in enumerate((gu_ref, gu2_ref)):
-            for k in range(2):
-                sums[2 * j + k] = sums[2 * j + k] + nt_dot(rows, ref[k, :, cols])
-    for j in range(4):
-        sums_ref[j, :, :HIDDEN] = sums[j]
+            both = jnp.concatenate([ref[0, :, cols], ref[1, :, cols]], axis=0)
+            sums[j] = sums[j] + nt_dot(rows, both)
+    for j in range(2):
+        sums_ref[j, :, : 2 * HIDDEN] = sums[j]
+    sums_ref[2] = jnp.broadcast_to(jnp.sum(squares, axis=1, keepdims=True), (TOKS, COLS))
 
 
 def down_kernel(own_ref, oth_ref, down_ref, down2_ref, out_ref):
     core = lax.rem(lax.axis_index("kvp"), 2)
-    squares = own_ref[4][:, 0:1] + oth_ref[4][:, 0:1]
+    squares = own_ref[2][:, 0:1] + oth_ref[2][:, 0:1]
     rscale = lax.rsqrt(squares / D + EPS)
     hidden = []
     for j in range(2):
-        gate = (own_ref[2 * j] + oth_ref[2 - 2 * j])[:, :HIDDEN] * rscale
-        up = (own_ref[2 * j + 1] + oth_ref[3 - 2 * j])[:, :HIDDEN] * rscale
+        total = (own_ref[j] + oth_ref[1 - j]) * rscale
+        gate, up = total[:, :HIDDEN], total[:, HIDDEN : 2 * HIDDEN]
         hidden.append((gate / (1.0 + jnp.exp(-gate)) * up).astype(bf16))
     for i in range(PEERS):
         z, x = i // NX, i % NX
@@ -371,10 +368,11 @@
 VMEM = pl.BlockSpec(memory_space=pltpu.VMEM)
 SMEM = pl.BlockSpec(memory_space=pltpu.SMEM)
 HBM = pl.BlockSpec(memory_space=pltpu.HBM)
+COST = pl.CostEstimate(flops=10**9, bytes_accessed=4 * 10**7, transcendentals=0)
 PARAMS = pltpu.CompilerParams(vmem_limit_bytes=VMEM_LIMIT)
 
 
-def call(kernel, name, in_specs, out_shape, out_specs, scratch=()):
+def call(kernel, name, in_specs, out_shape, out_specs, scratch=(), cost=COST):
     return pl.pallas_call(
         kernel,
         name=name,
@@ -383,6 +381,7 @@
         out_specs=out_specs,
         scratch_shapes=list(scratch),
         compiler_params=PARAMS,
+        cost_estimate=cost,
     )
 
 
@@ -404,7 +403,7 @@
     down_weight,
 ):
     shape = jax.ShapeDtypeStruct
-    cache = shape((PROMPTS, SHARD, 2 * HD), bf16)
+    cache = shape((PROMPTS // 2, SHARD, 2 * HD), bf16)
     key_pair, value_pair = swap_cores(key_cache), swap_cores(value_cache)
     draft_pair = swap_cores(draft_kv)
     block, keys, values, extra, order = call(
@@ -424,6 +423,7 @@
             pltpu.SMEM((PROMPTS,), jnp.int32),
             pltpu.SemaphoreType.DMA((2,)),
         ],
+        None,
     )(
         in_hbm(prompt_of),
         in_hbm(prefix_len),
@@ -438,24 +438,39 @@
     )
     own = swap_plane(block)
     oth = swap_cores(own)
-    part, gath = call(
+    part, queries, slot_token, row_token = call(
         attention_kernel,
         "attention",
         [SMEM] + [VMEM] * 8,
-        [shape((HEADS, ROWS_OUT, HD), bf16), shape((TOKS, HEADS, HD), bf16)],
-        [VMEM, VMEM],
-        [pltpu.VMEM((8, HD), f32)],
-    )(order, own, oth, keys, values, key_pair, value_pair, extra, draft_pair)
+        [
+            shape((HEADS, ROWS_OUT, HD), bf16),
+            shape((HALF, HEADS, HD), bf16),
+            shape((HALF, HD), jnp.int32),
+            shape((8, HD), jnp.int32),
+        ],
+        [VMEM] * 4,
+        [pltpu.VMEM((TOKS, HEADS, HD), bf16), pltpu.VMEM((8, HD), f32)],
+    )(
+        order,
+        own,
+        oth,
+        keys,
+        values,
+        key_pair,
+        value_pair,
+        extra,
+        draft_pair,
+    )
     part, gate_up_sent = lax.optimization_barrier((part, gate_up))
     gate_up_pair = swap_cores(gate_up_sent)
     attn, gains = call(
         combine_kernel,
         "combine",
-        [SMEM, VMEM, VMEM],
+        [VMEM, VMEM, VMEM],
         [shape((PEERS, HALF, HD), bf16), shape((PEERS, COLS), f32)],
         [VMEM, VMEM],
         [pltpu.VMEM((PEERS, HD), f32), pltpu.VMEM((HD, HD), f32)],
-    )(order, swap_plane(part), gath)
+    )(swap_plane(part), queries, slot_token)
     attn, down_sent = lax.optimization_barrier((attn, down_weight))
     down_pair = swap_cores(down_sent)
     attn_own = swap_plane(attn)
@@ -463,17 +478,17 @@
     partial = call(
         project_kernel,
         "project",
-        [SMEM, VMEM, VMEM, VMEM, VMEM],
+        [VMEM] * 5,
         shape((NZ * NY, 16, COLS), bf16),
         VMEM,
-        [pltpu.VMEM((TOKS, COLS), f32), pltpu.VMEM((TOKS, COLS), f32)],
-    )(order, attn_own, attn_oth, out_weight, in_hbm(stream))
+        [pltpu.VMEM((TOKS, COLS), f32)],
+    )(row_token, attn_own, attn_oth, out_weight, in_hbm(stream))
     partial = lax.all_to_all(partial, ("kvp", "tp"), 0, 0, axis_index_groups=G_YZ, tiled=True)
     msg, middle = call(
         spread_kernel,
         "spread",
         [VMEM, VMEM],
-        [shape((NX * NY, NZ * 16 + 16, COLS), bf16), shape((16, COLS), f32)],
+        [shape((NX * NY, NZ * 16, COLS), bf16), shape((16, COLS), f32)],
         [VMEM, VMEM],
         [pltpu.VMEM((NZ, 16, COLS), f32)],
     )(partial, gains)
@@ -481,10 +496,10 @@
     sums = call(
         gate_kernel,
         "gate",
-        [VMEM] * 3,
-        shape((5, TOKS, HD), f32),
+        [VMEM] * 4,
+        shape((3, TOKS, COLS), f32),
         VMEM,
-    )(normed, gate_up, gate_up_pair)
+    )(normed, gains, gate_up, gate_up_pair)
     partial = call(
         down_kernel,
         "down",

time: 150 us -> 147 us (0.980)
  transfers between devices with their start and end apart: 8 -> 8, of which waited for: 3 -> 3; matrix products, arithmetic and copies ran while one was open for 0% -> 0% of each run, Pallas kernels for 6% -> 5%
where the time goes in v5:
time: 147 us
  blocking collectives  130 us (88%)
  Pallas kernels  11 us (7%)
  waiting for transfers between devices  4.5 us (3%)
    all_to_all x3, blocking collectives, swap_plane(): lax.all_to_all(array, 'kvp', 0, 0, axis_index_groups=G_XZ, tiled=True)  60.6 us
    all_to_all x2, blocking collectives, swap_face(): lax.all_to_all(array, ('kvp', 'tp'), 0, 0, axis_index_groups=G_XY, tiled=...  40.8 us
    all_to_all x1, blocking collectives, on_device(): lax.all_to_all(partial, ('kvp', 'tp'), 0, 0, axis_index_groups=G_YZ, tile...  17.1 us
    all_to_all x1, blocking collectives, on_device(): lax.all_to_all(summed, 'kvp', 0, 0, axis_index_groups=G_Z, tiled=True)  11.1 us
    ppermute x8, waiting for transfers between devices, swap_cores(): return lax.ppermute(array, 'kvp', CORE_PAIRS)  4.5 us
    pallas_call x1, Pallas kernels, on_device(): call(attention_kernel, 'attention', [SMEM] + [VMEM] * 8, [shape((HEADS, R...  3.06 us
  transfers between devices with their start and end apart: 8, of which 3 were waited for; matrix products, arithmetic and copies ran while one was open for 0% of the time, Pallas kernels for 5%

profile of v5, /device:TPU:8, one launch (start us, length us, event | category | flops | bytes accessed | tf_op | source)
XLA Modules:
  0.0 146.9 jit_solution(17929370107077116297)
XLA Ops:
  0.0 0.0 collective-permute-start.1
  0.0 0.5 collective-permute-start.2
  0.5 0.0 collective-permute-start
  0.5 2.5 %prepare.1 = (bf16[32,32,128]{2,1,0:T(8,128)(2,1)S(1)}, bf16[4,128,256]{2,1,0:T(8,128)(2,1)S(1)}, bf16[4,128,256]{2,1,0:T(8,128)(2,1)S(1)}, f32[2,8,128]{2,1,0:T(8,128)S(1)}, s32[72]{0:T(128)S(1)}) custom-call(s32[32]{0:T(128)} %prompt_ref.1, s32[8]{0:T(128)} %len_ref.1, bf16[1,4096]{1,0:T(2,128)(2,1)} %query_ref.1, bf16[1,2,256]{2,1,0:T(2,128)(2,1)} %draft_ref.1, ...), custom_call_target="tpu_custom_call" | custom-call | tf_op jit(solution)/shard_map/prepare/pallas_call | solution.py:409
  3.0 0.0 collective-permute-done.draft2_ref
  3.0 0.0 collective-permute-done.1.k2_ref
  3.0 0.0 collective-permute-done.2.v2_ref
  3.0 24.8 %all_to_all.35.own_ref = bf16[32,32,128]{2,1,0:T(8,128)(2,1)S(1)} all-to-all(bf16[32,32,128]{2,1,0:T(8,128)(2,1)S(1)} %get-tuple-element.28), channel_id=1, replica_groups={{0,8,16,24,32,40,48,56,64,72,80,88,96,104,112,120,128,136,144,152,160,1..., dimensions={0} | all-to-all | bytes 524288 | tf_op jit(solution)/shard_map/all_to_all | solution.py:60
  27.8 0.0 collective-permute-start.3
  27.8 1.5 %collective-permute-done.3.oth_ref = bf16[32,32,128]{2,1,0:T(8,128)(2,1)S(1)} collective-permute-done((bf16[32,32,128]{2,1,0:T(8,128)(2,1)S(1)}, bf16[32,32,128]{2,1,0:T(8,128)(2,1)S(1)}, u32[]{:S(2)}, u32[]{:S(2)}) %collective-permute-start.3) | collective-permute-done | bytes 262176 | tf_op jit(solution)/shard_map/ppermute | solution.py:56
  29.4 0.0 copy-start
  29.4 0.0 copy-start.1
  29.4 3.1 %attention.1 = (bf16[32,40,128]{2,1,0:T(8,128)(2,1)S(1)}, bf16[32,32,128]{2,1,0:T(8,128)(2,1)S(1)}, s32[32,128]{1,0:T(8,128)S(1)}, s32[8,128]{1,0:T(8,128)S(1)}) custom-call(s32[72]{0:T(128)S(1)} %get-tuple-element.26.order_ref, bf16[32,32,128]{2,1,0:T(8,128)(2,1)S(1)} %all_to_all.35.own_ref, bf16[32,32,128]{2,1,0:T(8,128)(2,1)S(1)} %collective-permute-done.3.oth_ref, ...), custom_call_target="tpu_custom_call" | custom-call | flops 1000000000 | bytes 40000000 | tf_op jit(solution)/shard_map/attention/pallas_call | solution.py:441
  32.4 0.2 collective-permute-start.5
  32.7 18.4 %all_to_all.36.part_ref = bf16[32,40,128]{2,1,0:T(8,128)(2,1)S(1)} all-to-all(bf16[32,40,128]{2,1,0:T(8,128)(2,1)S(1)} %get-tuple-element.37), channel_id=1, replica_groups={{0,8,16,24,32,40,48,56,64,72,80,88,96,104,112,120,128,136,144,152,160,1..., dimensions={0} | all-to-all | bytes 655360 | tf_op jit(solution)/shard_map/all_to_all | solution.py:60
  51.0 0.0 slice-start
  51.0 0.7 combine.1
  51.8 0.0 copy-done
  51.8 0.1 collective-permute-start.7
  51.9 17.4 %all_to_all.37.own_ref = bf16[32,32,128]{2,1,0:T(8,128)(2,1)S(1)} all-to-all(bf16[32,32,128]{2,1,0:T(8,128)(2,1)S(1)} %get-tuple-element.41), channel_id=1, replica_groups={{0,8,16,24,32,40,48,56,64,72,80,88,96,104,112,120,128,136,144,152,160,1..., dimensions={0} | all-to-all | bytes 524288 | tf_op jit(solution)/shard_map/all_to_all | solution.py:60
  69.3 0.0 collective-permute-start.4
  69.3 1.5 %collective-permute-done.4.oth_ref = bf16[32,32,128]{2,1,0:T(8,128)(2,1)S(1)} collective-permute-done((bf16[32,32,128]{2,1,0:T(8,128)(2,1)S(1)}, bf16[32,32,128]{2,1,0:T(8,128)(2,1)S(1)}, u32[]{:S(2)}, u32[]{:S(2)}) %collective-permute-start.4) | collective-permute-done | bytes 262176 | tf_op jit(solution)/shard_map/ppermute | solution.py:56
  70.8 0.0 copy-done.1
  70.8 0.0 slice-start.1
  70.8 1.6 %project.1 = bf16[32,16,256]{2,1,0:T(8,128)(2,1)S(1)} custom-call(s32[8,128]{1,0:T(8,128)S(1)} %get-tuple-element.35.token_ref, bf16[32,32,128]{2,1,0:T(8,128)(2,1)S(1)} %all_to_all.37.own_ref, bf16[32,32,128]{2,1,0:T(8,128)(2,1)S(1)} %collective-permute-done.4.oth_ref, bf16[4096,256]{1,0:T(8,128)(2,1)S(1)} %copy-done.1, bf16[16,256]{1,0:T(8,128)(2,1)} %stream_ref.1), custom_call_target="tpu_custom_call" | custom-call | flops 1000000000 | bytes 40000000 | tf_op jit(solution)/shard_map/project/pallas_call | solution.py:478
  72.4 17.1 %all_to_all.38.in_ref = bf16[32,16,256]{2,1,0:T(8,128)(2,1)S(1)} all-to-all(bf16[32,16,256]{2,1,0:T(8,128)(2,1)S(1)} %project.1), channel_id=1, replica_groups={{0,1,2,3,32,33,34,35,64,65,66,67,96,97,98,99,128,129,130,131,160,161,16..., dimensions={0} | all-to-all | bytes 524288 | tf_op jit(solution)/shard_map/all_to_all | solution.py:486
  89.4 0.1 spread.1
  89.5 20.1 %all_to_all.39.rows_ref = bf16[16,128,256]{2,1,0:T(8,128)(2,1)S(1)} all-to-all(bf16[16,128,256]{2,1,0:T(8,128)(2,1)S(1)} %get-tuple-element.44), channel_id=1, replica_groups={{0,1,2,3,8,9,10,11,16,17,18,19,24,25,26,27},{4,5,6,7,12,13,14,15,20,21,..., dimensions={0} | all-to-all | bytes 2097152 | tf_op jit(solution)/shard_map/all_to_all | solution.py:64
  109.7 0.0 collective-permute-done.5.gu2_ref
  109.7 0.0 slice-done
  109.7 0.0 slice-done.1
  109.7 2.3 %gate.1.own_ref = f32[3,64,256]{2,1,0:T(8,128)S(1)} custom-call(bf16[16,128,256]{2,1,0:T(8,128)(2,1)S(1)} %all_to_all.39.rows_ref, f32[32,256]{1,0:T(8,128)S(1)} %get-tuple-element.42.gain_ref, bf16[2,104,16384]{2,1,0:T(8,128)(2,1)S(1)} %bitcast.2, bf16[2,104,16384]{2,1,0:T(8,128)(2,1)S(1)} %collective-permute-done.5.gu2_ref), custom_call_target="tpu_custom_call" | custom-call | flops 1000000000 | bytes 40000000 | tf_op jit(solution)/shard_map/gate/pallas_call | solution.py:496
  112.0 0.1 collective-permute-start.6
  112.1 0.0 collective-permute-done.7.down2_ref
  112.1 1.4 collective-permute-done.6.oth_ref
  113.5 0.8 down.1
  114.4 20.7 %all_to_all.40 = bf16[16,128,256]{2,1,0:T(8,128)(2,1)S(1)} all-to-all(bf16[16,128,256]{2,1,0:T(8,128)(2,1)S(1)} %down.1), channel_id=1, replica_groups={{0,1,2,3,8,9,10,11,16,17,18,19,24,25,26,27},{4,5,6,7,12,13,14,15,20,21,..., dimensions={0} | all-to-all | bytes 2097152 | tf_op jit(solution)/shard_map/all_to_all | solution.py:64
  135.0 0.1 reduce_sum.21
  135.2 11.1 %all_to_all.41 = bf16[8,16,256]{2,1,0:T(8,128)(2,1)S(1)} all-to-all(bf16[8,16,256]{2,1,0:T(8,128)(2,1)S(1)} %bitcast.3), channel_id=1, replica_groups={{0,32,64,96,128,160,192,224},{4,36,68,100,132,164,196,228},{8,40,72,104..., dimensions={0} | all-to-all | bytes 131072 | tf_op jit(solution)/shard_map/all_to_all | solution.py:512
  146.3 0.6 add_convert_fusion
  (2 shorter events, 0.0 us)
Async XLA Ops:
  0.0 3.0 %collective-permute-start.1 = (bf16[8,128,256]{2,1,0:T(8,128)(2,1)}, bf16[8,128,256]{2,1,0:T(8,128)(2,1)S(1)}, u32[]{:S(2)}, u32[]{:S(2)}) collective-permute-start(bf16[8,128,256]{2,1,0:T(8,128)(2,1)} %k_ref.1), channel_id=1, source_target_pairs={{0,4},{4,0},{8,12},{12,8},{16,20},{20,16},{24,28},{28,24},{32,36},... | collective-permute-start | bytes 1572872 | tf_op jit(solution)/shard_map/ppermute | solution.py:56
  0.0 3.0 %collective-permute-start.2 = (bf16[8,128,256]{2,1,0:T(8,128)(2,1)}, bf16[8,128,256]{2,1,0:T(8,128)(2,1)S(1)}, u32[]{:S(2)}, u32[]{:S(2)}) collective-permute-start(bf16[8,128,256]{2,1,0:T(8,128)(2,1)} %v_ref.1), channel_id=1, source_target_pairs={{0,4},{4,0},{8,12},{12,8},{16,20},{20,16},{24,28},{28,24},{32,36},... | collective-permute-start | bytes 1572872 | tf_op jit(solution)/shard_map/ppermute | solution.py:56
  0.5 2.5 %collective-permute-start = (bf16[1,2,256]{2,1,0:T(2,128)(2,1)}, bf16[1,2,256]{2,1,0:T(2,128)(2,1)S(1)}, u32[]{:S(2)}, u32[]{:S(2)}) collective-permute-start(bf16[1,2,256]{2,1,0:T(2,128)(2,1)} %draft_ref.1), channel_id=1, source_target_pairs={{0,4},{4,0},{8,12},{12,8},{16,20},{20,16},{24,28},{28,24},{32,36},... | collective-permute-start | bytes 3080 | tf_op jit(solution)/shard_map/ppermute | solution.py:56
  27.8 1.5 %collective-permute-start.3 = (bf16[32,32,128]{2,1,0:T(8,128)(2,1)S(1)}, bf16[32,32,128]{2,1,0:T(8,128)(2,1)S(1)}, u32[]{:S(2)}, u32[]{:S(2)}) collective-permute-start(bf16[32,32,128]{2,1,0:T(8,128)(2,1)S(1)} %all_to_all.35.own_ref), channel_id=1, source_target_pairs={{0,4},{4,0},{8,12},{12,8},{16,20},{20,16},{24,28},{28,24},{32,36},... | collective-permute-start | bytes 786440 | tf_op jit(solution)/shard_map/ppermute | solution.py:56
  29.4 22.4 %copy-start = (bf16[104,16384]{1,0:T(8,128)(2,1)S(1)}, bf16[104,16384]{1,0:T(8,128)(2,1)}, u32[]{:S(2)}) copy-start(bf16[104,16384]{1,0:T(8,128)(2,1)} %down_ref.1) | copy-start | bytes 10223620
  29.4 41.4 %copy-start.1 = (bf16[4096,256]{1,0:T(8,128)(2,1)S(1)}, bf16[4096,256]{1,0:T(8,128)(2,1)}, u32[]{:S(2)}) copy-start(bf16[4096,256]{1,0:T(8,128)(2,1)} %w_ref.1) | copy-start | bytes 6291460
  32.4 77.2 %collective-permute-start.5 = (bf16[2,104,16384]{2,1,0:T(8,128)(2,1)}, bf16[2,104,16384]{2,1,0:T(8,128)(2,1)S(1)}, u32[]{:S(2)}, u32[]{:S(2)}) collective-permute-start(bf16[2,104,16384]{2,1,0:T(8,128)(2,1)} %gu_ref.1), channel_id=1, source_target_pairs={{0,4},{4,0},{8,12},{12,8},{16,20},{20,16},{24,28},{28,24},{32,36},... | collective-permute-start | bytes 20447240 | tf_op jit(solution)/shard_map/ppermute | solution.py:56
  51.0 58.7 %slice-start = ((s8[6815744]{0:T(1024)(128)(4,1)}), s8[4194304]{0:T(1024)(128)(4,1)S(1)}, s32[]{:S(2)}) async-start(s8[6815744]{0:T(1024)(128)(4,1)} %bitcast.1), calls=%async_computation.7 | async-start | bytes 8388608
  51.8 60.3 %collective-permute-start.7 = (bf16[104,16384]{1,0:T(8,128)(2,1)S(1)}, bf16[104,16384]{1,0:T(8,128)(2,1)S(1)}, u32[]{:S(2)}, u32[]{:S(2)}) collective-permute-start(bf16[104,16384]{1,0:T(8,128)(2,1)S(1)} %copy-done), channel_id=1, source_target_pairs={{0,4},{4,0},{8,12},{12,8},{16,20},{20,16},{24,28},{28,24},{32,36},... | collective-permute-start | bytes 10223624 | tf_op jit(solution)/shard_map/ppermute | solution.py:56
  69.3 1.5 %collective-permute-start.4 = (bf16[32,32,128]{2,1,0:T(8,128)(2,1)S(1)}, bf16[32,32,128]{2,1,0:T(8,128)(2,1)S(1)}, u32[]{:S(2)}, u32[]{:S(2)}) collective-permute-start(bf16[32,32,128]{2,1,0:T(8,128)(2,1)S(1)} %all_to_all.37.own_ref), channel_id=1, source_target_pairs={{0,4},{4,0},{8,12},{12,8},{16,20},{20,16},{24,28},{28,24},{32,36},... | collective-permute-start | bytes 786440 | tf_op jit(solution)/shard_map/ppermute | solution.py:56
  70.8 38.9 %slice-start.1 = ((s8[6815744]{0:T(1024)(128)(4,1)}), s8[2621440]{0:T(1024)(128)(4,1)S(1)}, s32[]{:S(2)}) async-start(s8[6815744]{0:T(1024)(128)(4,1)} %bitcast.1), calls=%async_computation.8 | async-start | bytes 5242880
  112.0 1.5 %collective-permute-start.6 = (f32[3,64,256]{2,1,0:T(8,128)S(1)}, f32[3,64,256]{2,1,0:T(8,128)S(1)}, u32[]{:S(2)}, u32[]{:S(2)}) collective-permute-start(f32[3,64,256]{2,1,0:T(8,128)S(1)} %gate.1.own_ref), channel_id=1, source_target_pairs={{0,4},{4,0},{8,12},{12,8},{16,20},{20,16},{24,28},{28,24},{32,36},... | collective-permute-start | bytes 589832 | tf_op jit(solution)/shard_map/ppermute | solution.py:56

commit v6 on v5

--- a/solution.py
+++ b/solution.py
@@ -48,6 +48,12 @@
     [all_index(z, x, c, y) for z in range(NZ) for y in range(NY)]
     for x in range(NX)
     for c in range(NC)
+]
+G_LINE = [[all_index(z, x, 0, y) for x in range(NX)] for z in range(NZ) for y in range(NY)] + [
+    [all_index(z, x, 1, y) for y in range(NY)] for z in range(NZ) for x in range(NX)
+]
+G_REST = [[all_index(z, x, 0, y) for y in range(NY) for z in range(NZ)] for x in range(NX)] + [
+    [all_index(z, x, 1, y) for x in range(NX) for z in range(NZ)] for y in range(NY)
 ]
 CORE_PAIRS = [(i, i ^ 1) for i in range(NZ * NX * NC)]
 
@@ -362,7 +368,11 @@
         part = nn_dot(hidden[0], down_ref[:, cols]) + nn_dot(hidden[1], down2_ref[:, cols])
         part = part.astype(bf16)
         for y in range(NY):
-            out_ref[x * NY + y, z * 16 : (z + 1) * 16, :] = part[16 * y : 16 * y + 16]
+            line = jnp.where(core == 0, x, y)
+            rest = (x + y - line) * NZ + z
+            out_ref[line, pl.ds(pl.multiple_of(rest * 16, 16), 16), :] = part[
+                16 * y : 16 * y + 16
+            ]
 
 
 VMEM = pl.BlockSpec(memory_space=pltpu.VMEM)
@@ -504,12 +514,12 @@
         down_kernel,
         "down",
         [VMEM] * 4,
-        shape((NX * NY, NZ * 16, COLS), bf16),
+        shape((4, 4 * NZ * 16, COLS), bf16),
         VMEM,
     )(sums, swap_cores(sums), down_weight, down_pair)
-    summed = swap_face(partial)
-    summed = jnp.sum(summed.astype(f32), axis=0).astype(bf16).reshape(NZ, 16, COLS)
-    summed = lax.all_to_all(summed, "kvp", 0, 0, axis_index_groups=G_Z, tiled=True)
+    summed = lax.all_to_all(partial, ("kvp", "tp"), 0, 0, axis_index_groups=G_LINE, tiled=True)
+    summed = jnp.sum(summed.astype(f32), axis=0).astype(bf16).reshape(4 * NZ, 16, COLS)
+    summed = lax.all_to_all(summed, ("kvp", "tp"), 0, 0, axis_index_groups=G_REST, tiled=True)
     return (middle + jnp.sum(summed.astype(f32), axis=0)).astype(bf16)
 
 

time: 147 us -> 145 us (0.986); the launches traced: 147 us -> 143 us
  blocking collectives: 130 us -> 126 us
    all_to_all x2 -> x1, blocking collectives: 40.8 us -> 20.1 us  [swap_face(): lax.all_to_all(array, ('kvp', 'tp'), 0, 0, axis_index_groups=G_XY, tiled=...]
    all_to_all x1 -> x2, blocking collectives: 11.1 us -> 28.1 us  [the longest x1 14.8 us: on_device(): lax.all_to_all(summed, ('kvp', 'tp'), 0, 0, axis_index_groups=G_REST, til...]
where the time goes in v6:
time: 145 us; the launch traced here: 143 us
  blocking collectives  126 us (87%)
  Pallas kernels  11 us (8%)
  waiting for transfers between devices  4.5 us (3%)
    all_to_all x3, blocking collectives, swap_plane(): lax.all_to_all(array, 'kvp', 0, 0, axis_index_groups=G_XZ, tiled=True)  60.6 us
    all_to_all x1, blocking collectives, swap_face(): lax.all_to_all(array, ('kvp', 'tp'), 0, 0, axis_index_groups=G_XY, tiled=...  20.1 us
    all_to_all x1, blocking collectives, on_device(): lax.all_to_all(partial, ('kvp', 'tp'), 0, 0, axis_index_groups=G_YZ, tile...  17.1 us
    all_to_all x1, blocking collectives, on_device(): lax.all_to_all(summed, ('kvp', 'tp'), 0, 0, axis_index_groups=G_REST, til...  14.8 us
    all_to_all x1, blocking collectives, on_device(): lax.all_to_all(partial, ('kvp', 'tp'), 0, 0, axis_index_groups=G_LINE, ti...  13.3 us
    ppermute x8, waiting for transfers between devices, swap_cores(): return lax.ppermute(array, 'kvp', CORE_PAIRS)  4.5 us
    pallas_call x1, Pallas kernels, on_device(): call(attention_kernel, 'attention', [SMEM] + [VMEM] * 8, [shape((HEADS, R...  3.06 us
  transfers between devices with their start and end apart: 8, of which 3 were waited for; matrix products, arithmetic and copies ran while one was open for 0% of the time, Pallas kernels for 5%

profile of v6, /device:TPU:8, one launch (start us, length us, event | category | flops | bytes accessed | tf_op | source)
XLA Modules:
  0.0 143.4 jit_solution(1072249907590521013)
XLA Ops:
  0.0 0.0 collective-permute-start.1
  0.0 0.5 collective-permute-start.2
  0.5 0.0 collective-permute-start
  0.5 2.5 %prepare.1 = (bf16[32,32,128]{2,1,0:T(8,128)(2,1)S(1)}, bf16[4,128,256]{2,1,0:T(8,128)(2,1)S(1)}, bf16[4,128,256]{2,1,0:T(8,128)(2,1)S(1)}, f32[2,8,128]{2,1,0:T(8,128)S(1)}, s32[72]{0:T(128)S(1)}) custom-call(s32[32]{0:T(128)} %prompt_ref.1, s32[8]{0:T(128)} %len_ref.1, bf16[1,4096]{1,0:T(2,128)(2,1)} %query_ref.1, bf16[1,2,256]{2,1,0:T(2,128)(2,1)} %draft_ref.1, ...), custom_call_target="tpu_custom_call" | custom-call | tf_op jit(solution)/shard_map/prepare/pallas_call | solution.py:419
  3.0 0.0 collective-permute-done.draft2_ref
  3.0 0.0 collective-permute-done.1.k2_ref
  3.0 0.0 collective-permute-done.2.v2_ref
  3.0 24.8 %all_to_all.35.own_ref = bf16[32,32,128]{2,1,0:T(8,128)(2,1)S(1)} all-to-all(bf16[32,32,128]{2,1,0:T(8,128)(2,1)S(1)} %get-tuple-element.28), channel_id=1, replica_groups={{0,8,16,24,32,40,48,56,64,72,80,88,96,104,112,120,128,136,144,152,160,1..., dimensions={0} | all-to-all | bytes 524288 | tf_op jit(solution)/shard_map/all_to_all | solution.py:66
  27.8 0.0 collective-permute-start.3
  27.8 1.5 %collective-permute-done.3.oth_ref = bf16[32,32,128]{2,1,0:T(8,128)(2,1)S(1)} collective-permute-done((bf16[32,32,128]{2,1,0:T(8,128)(2,1)S(1)}, bf16[32,32,128]{2,1,0:T(8,128)(2,1)S(1)}, u32[]{:S(2)}, u32[]{:S(2)}) %collective-permute-start.3) | collective-permute-done | bytes 262176 | tf_op jit(solution)/shard_map/ppermute | solution.py:62
  29.4 0.0 copy-start
  29.4 0.0 copy-start.1
  29.4 3.1 %attention.1 = (bf16[32,40,128]{2,1,0:T(8,128)(2,1)S(1)}, bf16[32,32,128]{2,1,0:T(8,128)(2,1)S(1)}, s32[32,128]{1,0:T(8,128)S(1)}, s32[8,128]{1,0:T(8,128)S(1)}) custom-call(s32[72]{0:T(128)S(1)} %get-tuple-element.26.order_ref, bf16[32,32,128]{2,1,0:T(8,128)(2,1)S(1)} %all_to_all.35.own_ref, bf16[32,32,128]{2,1,0:T(8,128)(2,1)S(1)} %collective-permute-done.3.oth_ref, ...), custom_call_target="tpu_custom_call" | custom-call | flops 1000000000 | bytes 40000000 | tf_op jit(solution)/shard_map/attention/pallas_call | solution.py:451
  32.4 0.2 collective-permute-start.5
  32.7 18.4 %all_to_all.36.part_ref = bf16[32,40,128]{2,1,0:T(8,128)(2,1)S(1)} all-to-all(bf16[32,40,128]{2,1,0:T(8,128)(2,1)S(1)} %get-tuple-element.37), channel_id=1, replica_groups={{0,8,16,24,32,40,48,56,64,72,80,88,96,104,112,120,128,136,144,152,160,1..., dimensions={0} | all-to-all | bytes 655360 | tf_op jit(solution)/shard_map/all_to_all | solution.py:66
  51.0 0.0 slice-start
  51.0 0.7 combine.1
  51.8 0.0 copy-done
  51.8 0.1 collective-permute-start.7
  51.9 17.4 %all_to_all.37.own_ref = bf16[32,32,128]{2,1,0:T(8,128)(2,1)S(1)} all-to-all(bf16[32,32,128]{2,1,0:T(8,128)(2,1)S(1)} %get-tuple-element.41), channel_id=1, replica_groups={{0,8,16,24,32,40,48,56,64,72,80,88,96,104,112,120,128,136,144,152,160,1..., dimensions={0} | all-to-all | bytes 524288 | tf_op jit(solution)/shard_map/all_to_all | solution.py:66
  69.3 0.0 collective-permute-start.4
  69.3 1.5 %collective-permute-done.4.oth_ref = bf16[32,32,128]{2,1,0:T(8,128)(2,1)S(1)} collective-permute-done((bf16[32,32,128]{2,1,0:T(8,128)(2,1)S(1)}, bf16[32,32,128]{2,1,0:T(8,128)(2,1)S(1)}, u32[]{:S(2)}, u32[]{:S(2)}) %collective-permute-start.4) | collective-permute-done | bytes 262176 | tf_op jit(solution)/shard_map/ppermute | solution.py:62
  70.8 0.0 copy-done.1
  70.8 0.0 slice-start.1
  70.8 1.6 %project.1 = bf16[32,16,256]{2,1,0:T(8,128)(2,1)S(1)} custom-call(s32[8,128]{1,0:T(8,128)S(1)} %get-tuple-element.35.token_ref, bf16[32,32,128]{2,1,0:T(8,128)(2,1)S(1)} %all_to_all.37.own_ref, bf16[32,32,128]{2,1,0:T(8,128)(2,1)S(1)} %collective-permute-done.4.oth_ref, bf16[4096,256]{1,0:T(8,128)(2,1)S(1)} %copy-done.1, bf16[16,256]{1,0:T(8,128)(2,1)} %stream_ref.1), custom_call_target="tpu_custom_call" | custom-call | flops 1000000000 | bytes 40000000 | tf_op jit(solution)/shard_map/project/pallas_call | solution.py:488
  72.4 17.1 %all_to_all.38.in_ref = bf16[32,16,256]{2,1,0:T(8,128)(2,1)S(1)} all-to-all(bf16[32,16,256]{2,1,0:T(8,128)(2,1)S(1)} %project.1), channel_id=1, replica_groups={{0,1,2,3,32,33,34,35,64,65,66,67,96,97,98,99,128,129,130,131,160,161,16..., dimensions={0} | all-to-all | bytes 524288 | tf_op jit(solution)/shard_map/all_to_all | solution.py:496
  89.4 0.1 spread.1
  89.5 20.1 %all_to_all.39.rows_ref = bf16[16,128,256]{2,1,0:T(8,128)(2,1)S(1)} all-to-all(bf16[16,128,256]{2,1,0:T(8,128)(2,1)S(1)} %get-tuple-element.44), channel_id=1, replica_groups={{0,1,2,3,8,9,10,11,16,17,18,19,24,25,26,27},{4,5,6,7,12,13,14,15,20,21,..., dimensions={0} | all-to-all | bytes 2097152 | tf_op jit(solution)/shard_map/all_to_all | solution.py:70
  109.7 0.0 collective-permute-done.5.gu2_ref
  109.7 0.0 slice-done
  109.7 0.0 slice-done.1
  109.7 2.3 %gate.1.own_ref = f32[3,64,256]{2,1,0:T(8,128)S(1)} custom-call(bf16[16,128,256]{2,1,0:T(8,128)(2,1)S(1)} %all_to_all.39.rows_ref, f32[32,256]{1,0:T(8,128)S(1)} %get-tuple-element.42.gain_ref, bf16[2,104,16384]{2,1,0:T(8,128)(2,1)S(1)} %bitcast.2, bf16[2,104,16384]{2,1,0:T(8,128)(2,1)S(1)} %collective-permute-done.5.gu2_ref), custom_call_target="tpu_custom_call" | custom-call | flops 1000000000 | bytes 40000000 | tf_op jit(solution)/shard_map/gate/pallas_call | solution.py:506
  112.0 0.1 collective-permute-start.6
  112.1 0.0 collective-permute-done.7.down2_ref
  112.1 1.4 collective-permute-done.6.oth_ref
  113.5 0.8 down.1
  114.4 13.3 %all_to_all.40 = bf16[4,512,256]{2,1,0:T(8,128)(2,1)S(1)} all-to-all(bf16[4,512,256]{2,1,0:T(8,128)(2,1)S(1)} %down.1), channel_id=1, replica_groups={{0,8,16,24},{1,9,17,25},{2,10,18,26},{3,11,19,27},{32,40,48,56},{33,41,..., dimensions={0} | all-to-all | bytes 2097152 | tf_op jit(solution)/shard_map/all_to_all | solution.py:520
  127.7 0.3 reduce_sum.21
  127.9 14.8 %all_to_all.41 = bf16[32,16,256]{2,1,0:T(8,128)(2,1)S(1)} all-to-all(bf16[32,16,256]{2,1,0:T(8,128)(2,1)S(1)} %bitcast.3), channel_id=1, replica_groups={{0,32,64,96,128,160,192,224,1,33,65,97,129,161,193,225,2,34,66,98,130,1..., dimensions={0} | all-to-all | bytes 524288 | tf_op jit(solution)/shard_map/all_to_all | solution.py:522
  142.8 0.6 add_convert_fusion
  (2 shorter events, 0.0 us)
Async XLA Ops:
  0.0 3.0 %collective-permute-start.1 = (bf16[8,128,256]{2,1,0:T(8,128)(2,1)}, bf16[8,128,256]{2,1,0:T(8,128)(2,1)S(1)}, u32[]{:S(2)}, u32[]{:S(2)}) collective-permute-start(bf16[8,128,256]{2,1,0:T(8,128)(2,1)} %k_ref.1), channel_id=1, source_target_pairs={{0,4},{4,0},{8,12},{12,8},{16,20},{20,16},{24,28},{28,24},{32,36},... | collective-permute-start | bytes 1572872 | tf_op jit(solution)/shard_map/ppermute | solution.py:62
  0.0 3.0 %collective-permute-start.2 = (bf16[8,128,256]{2,1,0:T(8,128)(2,1)}, bf16[8,128,256]{2,1,0:T(8,128)(2,1)S(1)}, u32[]{:S(2)}, u32[]{:S(2)}) collective-permute-start(bf16[8,128,256]{2,1,0:T(8,128)(2,1)} %v_ref.1), channel_id=1, source_target_pairs={{0,4},{4,0},{8,12},{12,8},{16,20},{20,16},{24,28},{28,24},{32,36},... | collective-permute-start | bytes 1572872 | tf_op jit(solution)/shard_map/ppermute | solution.py:62
  0.5 2.5 %collective-permute-start = (bf16[1,2,256]{2,1,0:T(2,128)(2,1)}, bf16[1,2,256]{2,1,0:T(2,128)(2,1)S(1)}, u32[]{:S(2)}, u32[]{:S(2)}) collective-permute-start(bf16[1,2,256]{2,1,0:T(2,128)(2,1)} %draft_ref.1), channel_id=1, source_target_pairs={{0,4},{4,0},{8,12},{12,8},{16,20},{20,16},{24,28},{28,24},{32,36},... | collective-permute-start | bytes 3080 | tf_op jit(solution)/shard_map/ppermute | solution.py:62
  27.8 1.5 %collective-permute-start.3 = (bf16[32,32,128]{2,1,0:T(8,128)(2,1)S(1)}, bf16[32,32,128]{2,1,0:T(8,128)(2,1)S(1)}, u32[]{:S(2)}, u32[]{:S(2)}) collective-permute-start(bf16[32,32,128]{2,1,0:T(8,128)(2,1)S(1)} %all_to_all.35.own_ref), channel_id=1, source_target_pairs={{0,4},{4,0},{8,12},{12,8},{16,20},{20,16},{24,28},{28,24},{32,36},... | collective-permute-start | bytes 786440 | tf_op jit(solution)/shard_map/ppermute | solution.py:62
  29.4 22.4 %copy-start = (bf16[104,16384]{1,0:T(8,128)(2,1)S(1)}, bf16[104,16384]{1,0:T(8,128)(2,1)}, u32[]{:S(2)}) copy-start(bf16[104,16384]{1,0:T(8,128)(2,1)} %down_ref.1) | copy-start | bytes 10223620
  29.4 41.4 %copy-start.1 = (bf16[4096,256]{1,0:T(8,128)(2,1)S(1)}, bf16[4096,256]{1,0:T(8,128)(2,1)}, u32[]{:S(2)}) copy-start(bf16[4096,256]{1,0:T(8,128)(2,1)} %w_ref.1) | copy-start | bytes 6291460
  32.4 77.2 %collective-permute-start.5 = (bf16[2,104,16384]{2,1,0:T(8,128)(2,1)}, bf16[2,104,16384]{2,1,0:T(8,128)(2,1)S(1)}, u32[]{:S(2)}, u32[]{:S(2)}) collective-permute-start(bf16[2,104,16384]{2,1,0:T(8,128)(2,1)} %gu_ref.1), channel_id=1, source_target_pairs={{0,4},{4,0},{8,12},{12,8},{16,20},{20,16},{24,28},{28,24},{32,36},... | collective-permute-start | bytes 20447240 | tf_op jit(solution)/shard_map/ppermute | solution.py:62
  51.0 58.7 %slice-start = ((s8[6815744]{0:T(1024)(128)(4,1)}), s8[4194304]{0:T(1024)(128)(4,1)S(1)}, s32[]{:S(2)}) async-start(s8[6815744]{0:T(1024)(128)(4,1)} %bitcast.1), calls=%async_computation.7 | async-start | bytes 8388608
  51.8 60.3 %collective-permute-start.7 = (bf16[104,16384]{1,0:T(8,128)(2,1)S(1)}, bf16[104,16384]{1,0:T(8,128)(2,1)S(1)}, u32[]{:S(2)}, u32[]{:S(2)}) collective-permute-start(bf16[104,16384]{1,0:T(8,128)(2,1)S(1)} %copy-done), channel_id=1, source_target_pairs={{0,4},{4,0},{8,12},{12,8},{16,20},{20,16},{24,28},{28,24},{32,36},... | collective-permute-start | bytes 10223624 | tf_op jit(solution)/shard_map/ppermute | solution.py:62
  69.3 1.5 %collective-permute-start.4 = (bf16[32,32,128]{2,1,0:T(8,128)(2,1)S(1)}, bf16[32,32,128]{2,1,0:T(8,128)(2,1)S(1)}, u32[]{:S(2)}, u32[]{:S(2)}) collective-permute-start(bf16[32,32,128]{2,1,0:T(8,128)(2,1)S(1)} %all_to_all.37.own_ref), channel_id=1, source_target_pairs={{0,4},{4,0},{8,12},{12,8},{16,20},{20,16},{24,28},{28,24},{32,36},... | collective-permute-start | bytes 786440 | tf_op jit(solution)/shard_map/ppermute | solution.py:62
  70.8 38.9 %slice-start.1 = ((s8[6815744]{0:T(1024)(128)(4,1)}), s8[2621440]{0:T(1024)(128)(4,1)S(1)}, s32[]{:S(2)}) async-start(s8[6815744]{0:T(1024)(128)(4,1)} %bitcast.1), calls=%async_computation.8 | async-start | bytes 5242880
  112.0 1.5 %collective-permute-start.6 = (f32[3,64,256]{2,1,0:T(8,128)S(1)}, f32[3,64,256]{2,1,0:T(8,128)S(1)}, u32[]{:S(2)}, u32[]{:S(2)}) collective-permute-start(f32[3,64,256]{2,1,0:T(8,128)S(1)} %gate.1.own_ref), channel_id=1, source_target_pairs={{0,4},{4,0},{8,12},{12,8},{16,20},{20,16},{24,28},{28,24},{32,36},... | collective-permute-start | bytes 589832 | tf_op jit(solution)/shard_map/ppermute | solution.py:62

commit v7 on v6

--- a/solution.py
+++ b/solution.py
@@ -306,7 +306,8 @@
     rest = acc - high.astype(f32)
     middle = rest.astype(bf16)
     low = (rest - middle.astype(f32)).astype(bf16)
-    by_token[...] = nn_dot(place, high) + (nn_dot(place, middle) + nn_dot(place, low))
+    split = nn_dot(place, jnp.concatenate([high, middle, low], axis=1))
+    by_token[...] = split[:, :COLS] + (split[:, COLS : 2 * COLS] + split[:, 2 * COLS :])
     mine = pl.ds(pl.multiple_of(tp * 16, 16), 16)
     by_token[mine, :] = by_token[mine, :] + stream_ref[...].astype(f32)
     for y in range(NY):
@@ -373,6 +374,13 @@
             out_ref[line, pl.ds(pl.multiple_of(rest * 16, 16), 16), :] = part[
                 16 * y : 16 * y + 16
             ]
+
+
+def finish_kernel(parts_ref, middle_ref, out_ref):
+    total = middle_ref[...]
+    for i in range(4 * NZ):
+        total = total + parts_ref[i].astype(f32)
+    out_ref[...] = total.astype(bf16)
 
 
 VMEM = pl.BlockSpec(memory_space=pltpu.VMEM)
@@ -492,7 +500,7 @@
         shape((NZ * NY, 16, COLS), bf16),
         VMEM,
         [pltpu.VMEM((TOKS, COLS), f32)],
-    )(row_token, attn_own, attn_oth, out_weight, in_hbm(stream))
+    )(row_token, attn_own, attn_oth, out_weight, stream)
     partial = lax.all_to_all(partial, ("kvp", "tp"), 0, 0, axis_index_groups=G_YZ, tiled=True)
     msg, middle = call(
         spread_kernel,
@@ -520,7 +528,9 @@
     summed = lax.all_to_all(partial, ("kvp", "tp"), 0, 0, axis_index_groups=G_LINE, tiled=True)
     summed = jnp.sum(summed.astype(f32), axis=0).astype(bf16).reshape(4 * NZ, 16, COLS)
     summed = lax.all_to_all(summed, ("kvp", "tp"), 0, 0, axis_index_groups=G_REST, tiled=True)
-    return (middle + jnp.sum(summed.astype(f32), axis=0)).astype(bf16)
+    return call(finish_kernel, "finish", [VMEM, VMEM], shape((16, COLS), bf16), VMEM)(
+        summed, middle
+    )
 
 
 def solution(mesh):

time: 145 us -> 144 us (level)
  transfers between devices with their start and end apart: 8 -> 8, of which waited for: 3 -> 3; matrix products, arithmetic and copies ran while one was open for 0% -> 0% of each run, Pallas kernels for 5% -> 4%
where the time goes in v7:
time: 144 us; the launch traced here: 143 us
  blocking collectives  126 us (88%)
  Pallas kernels  10.8 us (8%)
  waiting for transfers between devices  4.5 us (3%)
    all_to_all x3, blocking collectives, swap_plane(): lax.all_to_all(array, 'kvp', 0, 0, axis_index_groups=G_XZ, tiled=True)  60.6 us
    all_to_all x1, blocking collectives, swap_face(): lax.all_to_all(array, ('kvp', 'tp'), 0, 0, axis_index_groups=G_XY, tiled=...  20.1 us
    all_to_all x1, blocking collectives, on_device(): lax.all_to_all(partial, ('kvp', 'tp'), 0, 0, axis_index_groups=G_YZ, tile...  17.2 us
    all_to_all x1, blocking collectives, on_device(): lax.all_to_all(summed, ('kvp', 'tp'), 0, 0, axis_index_groups=G_REST, til...  14.8 us
    all_to_all x1, blocking collectives, on_device(): lax.all_to_all(partial, ('kvp', 'tp'), 0, 0, axis_index_groups=G_LINE, ti...  13.3 us
    ppermute x8, waiting for transfers between devices, swap_cores(): return lax.ppermute(array, 'kvp', CORE_PAIRS)  4.5 us
    pallas_call x1, Pallas kernels, on_device(): call(attention_kernel, 'attention', [SMEM] + [VMEM] * 8, [shape((HEADS, R...  3.07 us
  transfers between devices with their start and end apart: 8, of which 3 were waited for; matrix products, arithmetic and copies ran while one was open for 0% of the time, Pallas kernels for 4%

profile of v7, /device:TPU:8, one launch (start us, length us, event | category | flops | bytes accessed | tf_op | source)
XLA Modules:
  0.0 142.7 jit_solution(4803466782016997978)
XLA Ops:
  0.0 0.0 collective-permute-start.1
  0.0 0.5 collective-permute-start.2
  0.5 0.0 collective-permute-start
  0.5 2.5 %prepare.1 = (bf16[32,32,128]{2,1,0:T(8,128)(2,1)S(1)}, bf16[4,128,256]{2,1,0:T(8,128)(2,1)S(1)}, bf16[4,128,256]{2,1,0:T(8,128)(2,1)S(1)}, f32[2,8,128]{2,1,0:T(8,128)S(1)}, s32[72]{0:T(128)S(1)}) custom-call(s32[32]{0:T(128)} %prompt_ref.1, s32[8]{0:T(128)} %len_ref.1, bf16[1,4096]{1,0:T(2,128)(2,1)} %query_ref.1, bf16[1,2,256]{2,1,0:T(2,128)(2,1)} %draft_ref.1, ...), custom_call_target="tpu_custom_call" | custom-call | tf_op jit(solution)/shard_map/prepare/pallas_call | solution.py:427
  3.0 0.0 collective-permute-done.draft2_ref
  3.0 0.0 collective-permute-done.1.k2_ref
  3.0 0.0 collective-permute-done.2.v2_ref
  3.0 24.8 %all_to_all.35.own_ref = bf16[32,32,128]{2,1,0:T(8,128)(2,1)S(1)} all-to-all(bf16[32,32,128]{2,1,0:T(8,128)(2,1)S(1)} %get-tuple-element.28), channel_id=1, replica_groups={{0,8,16,24,32,40,48,56,64,72,80,88,96,104,112,120,128,136,144,152,160,1..., dimensions={0} | all-to-all | bytes 524288 | tf_op jit(solution)/shard_map/all_to_all | solution.py:66
  27.8 0.0 collective-permute-start.3
  27.8 1.5 %collective-permute-done.3.oth_ref = bf16[32,32,128]{2,1,0:T(8,128)(2,1)S(1)} collective-permute-done((bf16[32,32,128]{2,1,0:T(8,128)(2,1)S(1)}, bf16[32,32,128]{2,1,0:T(8,128)(2,1)S(1)}, u32[]{:S(2)}, u32[]{:S(2)}) %collective-permute-start.3) | collective-permute-done | bytes 262176 | tf_op jit(solution)/shard_map/ppermute | solution.py:62
  29.4 0.0 copy-start
  29.4 0.0 copy-start.1
  29.4 0.0 copy-start.2
  29.4 3.1 %attention.1 = (bf16[32,40,128]{2,1,0:T(8,128)(2,1)S(1)}, bf16[32,32,128]{2,1,0:T(8,128)(2,1)S(1)}, s32[32,128]{1,0:T(8,128)S(1)}, s32[8,128]{1,0:T(8,128)S(1)}) custom-call(s32[72]{0:T(128)S(1)} %get-tuple-element.26.order_ref, bf16[32,32,128]{2,1,0:T(8,128)(2,1)S(1)} %all_to_all.35.own_ref, bf16[32,32,128]{2,1,0:T(8,128)(2,1)S(1)} %collective-permute-done.3.oth_ref, ...), custom_call_target="tpu_custom_call" | custom-call | flops 1000000000 | bytes 40000000 | tf_op jit(solution)/shard_map/attention/pallas_call | solution.py:459
  32.5 0.2 collective-permute-start.5
  32.7 18.4 %all_to_all.36.part_ref = bf16[32,40,128]{2,1,0:T(8,128)(2,1)S(1)} all-to-all(bf16[32,40,128]{2,1,0:T(8,128)(2,1)S(1)} %get-tuple-element.37), channel_id=1, replica_groups={{0,8,16,24,32,40,48,56,64,72,80,88,96,104,112,120,128,136,144,152,160,1..., dimensions={0} | all-to-all | bytes 655360 | tf_op jit(solution)/shard_map/all_to_all | solution.py:66
  51.0 0.0 slice-start
  51.0 0.7 combine.1
  51.8 0.0 copy-done
  51.8 0.1 collective-permute-start.7
  51.9 17.4 %all_to_all.37.own_ref = bf16[32,32,128]{2,1,0:T(8,128)(2,1)S(1)} all-to-all(bf16[32,32,128]{2,1,0:T(8,128)(2,1)S(1)} %get-tuple-element.41), channel_id=1, replica_groups={{0,8,16,24,32,40,48,56,64,72,80,88,96,104,112,120,128,136,144,152,160,1..., dimensions={0} | all-to-all | bytes 524288 | tf_op jit(solution)/shard_map/all_to_all | solution.py:66
  69.3 0.0 collective-permute-start.4
  69.3 1.5 %collective-permute-done.4.oth_ref = bf16[32,32,128]{2,1,0:T(8,128)(2,1)S(1)} collective-permute-done((bf16[32,32,128]{2,1,0:T(8,128)(2,1)S(1)}, bf16[32,32,128]{2,1,0:T(8,128)(2,1)S(1)}, u32[]{:S(2)}, u32[]{:S(2)}) %collective-permute-start.4) | collective-permute-done | bytes 262176 | tf_op jit(solution)/shard_map/ppermute | solution.py:62
  70.8 0.0 copy-done.1
  70.8 0.0 copy-done.2
  70.8 0.0 slice-start.1
  70.8 0.7 project.1
  71.5 17.2 %all_to_all.38.in_ref = bf16[32,16,256]{2,1,0:T(8,128)(2,1)S(1)} all-to-all(bf16[32,16,256]{2,1,0:T(8,128)(2,1)S(1)} %project.1), channel_id=1, replica_groups={{0,1,2,3,32,33,34,35,64,65,66,67,96,97,98,99,128,129,130,131,160,161,16..., dimensions={0} | all-to-all | bytes 524288 | tf_op jit(solution)/shard_map/all_to_all | solution.py:504
  88.7 0.1 spread.1
  88.8 20.1 %all_to_all.39.rows_ref = bf16[16,128,256]{2,1,0:T(8,128)(2,1)S(1)} all-to-all(bf16[16,128,256]{2,1,0:T(8,128)(2,1)S(1)} %get-tuple-element.43), channel_id=1, replica_groups={{0,1,2,3,8,9,10,11,16,17,18,19,24,25,26,27},{4,5,6,7,12,13,14,15,20,21,..., dimensions={0} | all-to-all | bytes 2097152 | tf_op jit(solution)/shard_map/all_to_all | solution.py:70
  109.0 0.0 collective-permute-done.5.gu2_ref
  109.0 0.0 slice-done
  109.0 0.0 slice-done.1
  109.0 2.3 %gate.1.own_ref = f32[3,64,256]{2,1,0:T(8,128)S(1)} custom-call(bf16[16,128,256]{2,1,0:T(8,128)(2,1)S(1)} %all_to_all.39.rows_ref, f32[32,256]{1,0:T(8,128)S(1)} %get-tuple-element.42.gain_ref, bf16[2,104,16384]{2,1,0:T(8,128)(2,1)S(1)} %bitcast.2, bf16[2,104,16384]{2,1,0:T(8,128)(2,1)S(1)} %collective-permute-done.5.gu2_ref), custom_call_target="tpu_custom_call" | custom-call | flops 1000000000 | bytes 40000000 | tf_op jit(solution)/shard_map/gate/pallas_call | solution.py:514
  111.3 0.1 collective-permute-start.6
  111.4 0.0 collective-permute-done.7.down2_ref
  111.4 1.4 collective-permute-done.6.oth_ref
  112.8 0.8 down.1
  113.6 13.3 %all_to_all.40 = bf16[4,512,256]{2,1,0:T(8,128)(2,1)S(1)} all-to-all(bf16[4,512,256]{2,1,0:T(8,128)(2,1)S(1)} %down.1), channel_id=1, replica_groups={{0,8,16,24},{1,9,17,25},{2,10,18,26},{3,11,19,27},{32,40,48,56},{33,41,..., dimensions={0} | all-to-all | bytes 2097152 | tf_op jit(solution)/shard_map/all_to_all | solution.py:528
  127.0 0.3 reduce_sum.12
  127.2 14.8 %all_to_all.41.parts_ref = bf16[32,16,256]{2,1,0:T(8,128)(2,1)S(1)} all-to-all(bf16[32,16,256]{2,1,0:T(8,128)(2,1)S(1)} %bitcast.3), channel_id=1, replica_groups={{0,32,64,96,128,160,192,224,1,33,65,97,129,161,193,225,2,34,66,98,130,1..., dimensions={0} | all-to-all | bytes 524288 | tf_op jit(solution)/shard_map/all_to_all | solution.py:530
  142.0 0.6 finish.1
  (1 shorter events, 0.0 us)
Async XLA Ops:
  0.0 3.0 %collective-permute-start.1 = (bf16[8,128,256]{2,1,0:T(8,128)(2,1)}, bf16[8,128,256]{2,1,0:T(8,128)(2,1)S(1)}, u32[]{:S(2)}, u32[]{:S(2)}) collective-permute-start(bf16[8,128,256]{2,1,0:T(8,128)(2,1)} %k_ref.1), channel_id=1, source_target_pairs={{0,4},{4,0},{8,12},{12,8},{16,20},{20,16},{24,28},{28,24},{32,36},... | collective-permute-start | bytes 1572872 | tf_op jit(solution)/shard_map/ppermute | solution.py:62
  0.0 3.0 %collective-permute-start.2 = (bf16[8,128,256]{2,1,0:T(8,128)(2,1)}, bf16[8,128,256]{2,1,0:T(8,128)(2,1)S(1)}, u32[]{:S(2)}, u32[]{:S(2)}) collective-permute-start(bf16[8,128,256]{2,1,0:T(8,128)(2,1)} %v_ref.1), channel_id=1, source_target_pairs={{0,4},{4,0},{8,12},{12,8},{16,20},{20,16},{24,28},{28,24},{32,36},... | collective-permute-start | bytes 1572872 | tf_op jit(solution)/shard_map/ppermute | solution.py:62
  0.5 2.5 %collective-permute-start = (bf16[1,2,256]{2,1,0:T(2,128)(2,1)}, bf16[1,2,256]{2,1,0:T(2,128)(2,1)S(1)}, u32[]{:S(2)}, u32[]{:S(2)}) collective-permute-start(bf16[1,2,256]{2,1,0:T(2,128)(2,1)} %draft_ref.1), channel_id=1, source_target_pairs={{0,4},{4,0},{8,12},{12,8},{16,20},{20,16},{24,28},{28,24},{32,36},... | collective-permute-start | bytes 3080 | tf_op jit(solution)/shard_map/ppermute | solution.py:62
  27.8 1.5 %collective-permute-start.3 = (bf16[32,32,128]{2,1,0:T(8,128)(2,1)S(1)}, bf16[32,32,128]{2,1,0:T(8,128)(2,1)S(1)}, u32[]{:S(2)}, u32[]{:S(2)}) collective-permute-start(bf16[32,32,128]{2,1,0:T(8,128)(2,1)S(1)} %all_to_all.35.own_ref), channel_id=1, source_target_pairs={{0,4},{4,0},{8,12},{12,8},{16,20},{20,16},{24,28},{28,24},{32,36},... | collective-permute-start | bytes 786440 | tf_op jit(solution)/shard_map/ppermute | solution.py:62
  29.4 22.4 %copy-start = (bf16[104,16384]{1,0:T(8,128)(2,1)S(1)}, bf16[104,16384]{1,0:T(8,128)(2,1)}, u32[]{:S(2)}) copy-start(bf16[104,16384]{1,0:T(8,128)(2,1)} %down_ref.1) | copy-start | bytes 10223620
  29.4 41.4 %copy-start.1 = (bf16[4096,256]{1,0:T(8,128)(2,1)S(1)}, bf16[4096,256]{1,0:T(8,128)(2,1)}, u32[]{:S(2)}) copy-start(bf16[4096,256]{1,0:T(8,128)(2,1)} %w_ref.1) | copy-start | bytes 6291460
  29.4 41.4 %copy-start.2 = (bf16[16,256]{1,0:T(8,128)(2,1)S(1)}, bf16[16,256]{1,0:T(8,128)(2,1)}, u32[]{:S(2)}) copy-start(bf16[16,256]{1,0:T(8,128)(2,1)} %stream_ref.1) | copy-start | bytes 24580
  32.5 76.5 %collective-permute-start.5 = (bf16[2,104,16384]{2,1,0:T(8,128)(2,1)}, bf16[2,104,16384]{2,1,0:T(8,128)(2,1)S(1)}, u32[]{:S(2)}, u32[]{:S(2)}) collective-permute-start(bf16[2,104,16384]{2,1,0:T(8,128)(2,1)} %gu_ref.1), channel_id=1, source_target_pairs={{0,4},{4,0},{8,12},{12,8},{16,20},{20,16},{24,28},{28,24},{32,36},... | collective-permute-start | bytes 20447240 | tf_op jit(solution)/shard_map/ppermute | solution.py:62
  51.0 57.9 %slice-start = ((s8[6815744]{0:T(1024)(128)(4,1)}), s8[4194304]{0:T(1024)(128)(4,1)S(1)}, s32[]{:S(2)}) async-start(s8[6815744]{0:T(1024)(128)(4,1)} %bitcast.1), calls=%async_computation.7 | async-start | bytes 8388608
  51.8 59.6 %collective-permute-start.7 = (bf16[104,16384]{1,0:T(8,128)(2,1)S(1)}, bf16[104,16384]{1,0:T(8,128)(2,1)S(1)}, u32[]{:S(2)}, u32[]{:S(2)}) collective-permute-start(bf16[104,16384]{1,0:T(8,128)(2,1)S(1)} %copy-done), channel_id=1, source_target_pairs={{0,4},{4,0},{8,12},{12,8},{16,20},{20,16},{24,28},{28,24},{32,36},... | collective-permute-start | bytes 10223624 | tf_op jit(solution)/shard_map/ppermute | solution.py:62
  69.3 1.5 %collective-permute-start.4 = (bf16[32,32,128]{2,1,0:T(8,128)(2,1)S(1)}, bf16[32,32,128]{2,1,0:T(8,128)(2,1)S(1)}, u32[]{:S(2)}, u32[]{:S(2)}) collective-permute-start(bf16[32,32,128]{2,1,0:T(8,128)(2,1)S(1)} %all_to_all.37.own_ref), channel_id=1, source_target_pairs={{0,4},{4,0},{8,12},{12,8},{16,20},{20,16},{24,28},{28,24},{32,36},... | collective-permute-start | bytes 786440 | tf_op jit(solution)/shard_map/ppermute | solution.py:62
  70.8 38.2 %slice-start.1 = ((s8[6815744]{0:T(1024)(128)(4,1)}), s8[2621440]{0:T(1024)(128)(4,1)S(1)}, s32[]{:S(2)}) async-start(s8[6815744]{0:T(1024)(128)(4,1)} %bitcast.1), calls=%async_computation.8 | async-start | bytes 5242880
  111.3 1.5 %collective-permute-start.6 = (f32[3,64,256]{2,1,0:T(8,128)S(1)}, f32[3,64,256]{2,1,0:T(8,128)S(1)}, u32[]{:S(2)}, u32[]{:S(2)}) collective-permute-start(f32[3,64,256]{2,1,0:T(8,128)S(1)} %gate.1.own_ref), channel_id=1, source_target_pairs={{0,4},{4,0},{8,12},{12,8},{16,20},{20,16},{24,28},{28,24},{32,36},... | collective-permute-start | bytes 589832 | tf_op jit(solution)/shard_map/ppermute | solution.py:62

commit v8 on v7

--- a/solution.py
+++ b/solution.py
@@ -87,11 +87,11 @@
 
 
 def prepare_kernel(
-    prompt_ref,
-    len_ref,
-    query_ref,
-    draft_ref,
-    gain_ref,
+    prompt_hbm,
+    len_hbm,
+    query_hbm,
+    draft_hbm,
+    gain_hbm,
     k_ref,
     v_ref,
     block_ref,
@@ -101,13 +101,28 @@
     order_ref,
     rows,
     count,
+    prompt_ref,
+    len_ref,
+    query_ref,
+    draft_ref,
+    gain_ref,
     sems,
 ):
     half = pl.ds(lax.rem(lax.axis_index("kvp"), 2) * (PROMPTS // 2), PROMPTS // 2)
-    k_copy = pltpu.make_async_copy(k_ref.at[half], k_out, sems.at[0])
-    v_copy = pltpu.make_async_copy(v_ref.at[half], v_out, sems.at[1])
-    k_copy.start()
-    v_copy.start()
+    pairs = (
+        (prompt_hbm, prompt_ref),
+        (len_hbm, len_ref),
+        (query_hbm, query_ref),
+        (draft_hbm, draft_ref),
+        (gain_hbm, gain_ref),
+        (k_ref.at[half], k_out),
+        (v_ref.at[half], v_out),
+    )
+    copies = [pltpu.make_async_copy(*pair, sems.at[i]) for i, pair in enumerate(pairs)]
+    for copy in copies:
+        copy.start()
+    for copy in copies[:5]:
+        copy.wait()
     query = query_ref[...].astype(f32)
     for h in range(HEADS):
         rows[h : h + 1, :] = query[:, h * HD : (h + 1) * HD]
@@ -130,8 +145,8 @@
         count[p] = seen + 1
         order_ref[p * 8 + seen] = s
         order_ref[p * 8 + 4 + seen] = s + HALF
-    k_copy.wait()
-    v_copy.wait()
+    for copy in copies[5:]:
+        copy.wait()
 
 
 def gather_row(order_ref, slot, core):
@@ -427,7 +442,7 @@
     block, keys, values, extra, order = call(
         prepare_kernel,
         "prepare",
-        [SMEM, SMEM, VMEM, VMEM, VMEM, HBM, HBM],
+        [HBM] * 7,
         [
             shape((PEERS, HEADS, HD), bf16),
             cache,
@@ -439,7 +454,12 @@
         [
             pltpu.VMEM((HEADS, HD), f32),
             pltpu.SMEM((PROMPTS,), jnp.int32),
-            pltpu.SemaphoreType.DMA((2,)),
+            pltpu.SMEM((HALF,), jnp.int32),
+            pltpu.SMEM((PROMPTS,), jnp.int32),
+            pltpu.VMEM((1, HEADS * HD), bf16),
+            pltpu.VMEM((1, 2, 2 * HD), bf16),
+            pltpu.VMEM((COLS,), bf16),
+            pltpu.SemaphoreType.DMA((7,)),
         ],
         None,
     )(
@@ -489,10 +509,10 @@
         [VMEM, VMEM],
         [pltpu.VMEM((PEERS, HD), f32), pltpu.VMEM((HD, HD), f32)],
     )(swap_plane(part), queries, slot_token)
-    attn, down_sent = lax.optimization_barrier((attn, down_weight))
-    down_pair = swap_cores(down_sent)
     attn_own = swap_plane(attn)
     attn_oth = swap_cores(attn_own)
+    attn_oth, down_sent = lax.optimization_barrier((attn_oth, down_weight))
+    down_pair = swap_cores(down_sent)
     partial = call(
         project_kernel,
         "project",

time: 144 us -> 143 us (level)
    all_to_all x3, blocking collectives: 60.6 us -> 59 us  [swap_plane(): lax.all_to_all(array, 'kvp', 0, 0, axis_index_groups=G_XZ, tiled=True)]
  transfers between devices with their start and end apart: 8 -> 8, of which waited for: 3 -> 4; matrix products, arithmetic and copies ran while one was open for 0% -> 0% of each run, Pallas kernels for 4% -> 4%
where the time goes in v8:
time: 143 us; the launch traced here: 141 us
  blocking collectives  125 us (87%)
  Pallas kernels  10.1 us (7%)
  waiting for transfers between devices  5.11 us (4%)
    all_to_all x3, blocking collectives, swap_plane(): lax.all_to_all(array, 'kvp', 0, 0, axis_index_groups=G_XZ, tiled=True)  59 us
    all_to_all x1, blocking collectives, swap_face(): lax.all_to_all(array, ('kvp', 'tp'), 0, 0, axis_index_groups=G_XY, tiled=...  20.5 us
    all_to_all x1, blocking collectives, on_device(): lax.all_to_all(partial, ('kvp', 'tp'), 0, 0, axis_index_groups=G_YZ, tile...  17.3 us
    all_to_all x1, blocking collectives, on_device(): lax.all_to_all(summed, ('kvp', 'tp'), 0, 0, axis_index_groups=G_REST, til...  14.5 us
    all_to_all x1, blocking collectives, on_device(): lax.all_to_all(partial, ('kvp', 'tp'), 0, 0, axis_index_groups=G_LINE, ti...  13.3 us
    ppermute x8, waiting for transfers between devices, swap_cores(): return lax.ppermute(array, 'kvp', CORE_PAIRS)  5.11 us
    pallas_call x1, Pallas kernels, on_device(): call(attention_kernel, 'attention', [SMEM] + [VMEM] * 8, [shape((HEADS, R...  3.07 us
  transfers between devices with their start and end apart: 8, of which 4 were waited for; matrix products, arithmetic and copies ran while one was open for 0% of the time, Pallas kernels for 4%

profile of v8, /device:TPU:8, one launch (start us, length us, event | category | flops | bytes accessed | tf_op | source)
XLA Modules:
  0.0 141.2 jit_solution(1517429452726710609)
XLA Ops:
  0.0 0.0 collective-permute-start.1
  0.0 0.5 collective-permute-start.2
  0.5 0.0 collective-permute-start
  0.5 1.7 %prepare.1 = (bf16[32,32,128]{2,1,0:T(8,128)(2,1)S(1)}, bf16[4,128,256]{2,1,0:T(8,128)(2,1)S(1)}, bf16[4,128,256]{2,1,0:T(8,128)(2,1)S(1)}, f32[2,8,128]{2,1,0:T(8,128)S(1)}, s32[72]{0:T(128)S(1)}) custom-call(s32[32]{0:T(128)} %prompt_hbm.1, s32[8]{0:T(128)} %len_hbm.1, bf16[1,4096]{1,0:T(2,128)(2,1)} %query_hbm.1, bf16[1,2,256]{2,1,0:T(2,128)(2,1)} %draft_hbm.1, ...), custom_call_target="tpu_custom_call" | custom-call | tf_op jit(solution)/shard_map/prepare/pallas_call | solution.py:442
  2.3 0.6 collective-permute-done.draft2_ref
  2.9 0.0 collective-permute-done.1.k2_ref
  2.9 0.0 collective-permute-done.2.v2_ref
  2.9 24.3 %all_to_all.35.own_ref = bf16[32,32,128]{2,1,0:T(8,128)(2,1)S(1)} all-to-all(bf16[32,32,128]{2,1,0:T(8,128)(2,1)S(1)} %get-tuple-element.28), channel_id=1, replica_groups={{0,8,16,24,32,40,48,56,64,72,80,88,96,104,112,120,128,136,144,152,160,1..., dimensions={0} | all-to-all | bytes 524288 | tf_op jit(solution)/shard_map/all_to_all | solution.py:66
  27.2 0.0 collective-permute-start.3
  27.2 1.5 %collective-permute-done.3.oth_ref = bf16[32,32,128]{2,1,0:T(8,128)(2,1)S(1)} collective-permute-done((bf16[32,32,128]{2,1,0:T(8,128)(2,1)S(1)}, bf16[32,32,128]{2,1,0:T(8,128)(2,1)S(1)}, u32[]{:S(2)}, u32[]{:S(2)}) %collective-permute-start.3) | collective-permute-done | bytes 262176 | tf_op jit(solution)/shard_map/ppermute | solution.py:62
  28.8 0.0 copy-start
  28.8 0.0 copy-start.1
  28.8 0.0 copy-start.2
  28.8 3.1 %attention.1 = (bf16[32,40,128]{2,1,0:T(8,128)(2,1)S(1)}, bf16[32,32,128]{2,1,0:T(8,128)(2,1)S(1)}, s32[32,128]{1,0:T(8,128)S(1)}, s32[8,128]{1,0:T(8,128)S(1)}) custom-call(s32[72]{0:T(128)S(1)} %get-tuple-element.26.order_ref, bf16[32,32,128]{2,1,0:T(8,128)(2,1)S(1)} %all_to_all.35.own_ref, bf16[32,32,128]{2,1,0:T(8,128)(2,1)S(1)} %collective-permute-done.3.oth_ref, ...), custom_call_target="tpu_custom_call" | custom-call | flops 1000000000 | bytes 40000000 | tf_op jit(solution)/shard_map/attention/pallas_call | solution.py:479
  31.8 0.2 collective-permute-start.5
  32.1 18.5 %all_to_all.36.part_ref = bf16[32,40,128]{2,1,0:T(8,128)(2,1)S(1)} all-to-all(bf16[32,40,128]{2,1,0:T(8,128)(2,1)S(1)} %get-tuple-element.37), channel_id=1, replica_groups={{0,8,16,24,32,40,48,56,64,72,80,88,96,104,112,120,128,136,144,152,160,1..., dimensions={0} | all-to-all | bytes 655360 | tf_op jit(solution)/shard_map/all_to_all | solution.py:66
  50.5 0.0 slice-start
  50.5 0.7 combine.1
  51.2 16.2 %all_to_all.37.own_ref = bf16[32,32,128]{2,1,0:T(8,128)(2,1)S(1)} all-to-all(bf16[32,32,128]{2,1,0:T(8,128)(2,1)S(1)} %get-tuple-element.40), channel_id=1, replica_groups={{0,8,16,24,32,40,48,56,64,72,80,88,96,104,112,120,128,136,144,152,160,1..., dimensions={0} | all-to-all | bytes 524288 | tf_op jit(solution)/shard_map/all_to_all | solution.py:66
  67.4 0.0 collective-permute-start.4
  67.4 1.5 %collective-permute-done.4.oth_ref = bf16[32,32,128]{2,1,0:T(8,128)(2,1)S(1)} collective-permute-done((bf16[32,32,128]{2,1,0:T(8,128)(2,1)S(1)}, bf16[32,32,128]{2,1,0:T(8,128)(2,1)S(1)}, u32[]{:S(2)}, u32[]{:S(2)}) %collective-permute-start.4) | collective-permute-done | bytes 262176 | tf_op jit(solution)/shard_map/ppermute | solution.py:62
  69.0 0.0 copy-done
  69.0 0.1 collective-permute-start.7
  69.1 0.0 copy-done.1
  69.1 0.0 copy-done.2
  69.1 0.0 slice-start.1
  69.1 0.7 project.1
  69.8 17.3 %all_to_all.38.in_ref = bf16[32,16,256]{2,1,0:T(8,128)(2,1)S(1)} all-to-all(bf16[32,16,256]{2,1,0:T(8,128)(2,1)S(1)} %project.1), channel_id=1, replica_groups={{0,1,2,3,32,33,34,35,64,65,66,67,96,97,98,99,128,129,130,131,160,161,16..., dimensions={0} | all-to-all | bytes 524288 | tf_op jit(solution)/shard_map/all_to_all | solution.py:524
  87.2 0.1 spread.1
  87.3 20.5 %all_to_all.39.rows_ref = bf16[16,128,256]{2,1,0:T(8,128)(2,1)S(1)} all-to-all(bf16[16,128,256]{2,1,0:T(8,128)(2,1)S(1)} %get-tuple-element.43), channel_id=1, replica_groups={{0,1,2,3,8,9,10,11,16,17,18,19,24,25,26,27},{4,5,6,7,12,13,14,15,20,21,..., dimensions={0} | all-to-all | bytes 2097152 | tf_op jit(solution)/shard_map/all_to_all | solution.py:70
  107.8 0.0 collective-permute-done.5.gu2_ref
  107.8 0.0 slice-done
  107.8 0.0 slice-done.1
  107.8 2.3 %gate.1.own_ref = f32[3,64,256]{2,1,0:T(8,128)S(1)} custom-call(bf16[16,128,256]{2,1,0:T(8,128)(2,1)S(1)} %all_to_all.39.rows_ref, f32[32,256]{1,0:T(8,128)S(1)} %get-tuple-element.42.gain_ref, bf16[2,104,16384]{2,1,0:T(8,128)(2,1)S(1)} %bitcast.2, bf16[2,104,16384]{2,1,0:T(8,128)(2,1)S(1)} %collective-permute-done.5.gu2_ref), custom_call_target="tpu_custom_call" | custom-call | flops 1000000000 | bytes 40000000 | tf_op jit(solution)/shard_map/gate/pallas_call | solution.py:534
  110.1 0.1 collective-permute-start.6
  110.2 0.0 collective-permute-done.7.down2_ref
  110.2 1.4 %collective-permute-done.6.oth_ref = f32[3,64,256]{2,1,0:T(8,128)S(1)} collective-permute-done((f32[3,64,256]{2,1,0:T(8,128)S(1)}, f32[3,64,256]{2,1,0:T(8,128)S(1)}, u32[]{:S(2)}, u32[]{:S(2)}) %collective-permute-start.6) | collective-permute-done | bytes 196640 | tf_op jit(solution)/shard_map/ppermute | solution.py:62
  111.7 0.8 down.1
  112.5 13.3 %all_to_all.40 = bf16[4,512,256]{2,1,0:T(8,128)(2,1)S(1)} all-to-all(bf16[4,512,256]{2,1,0:T(8,128)(2,1)S(1)} %down.1), channel_id=1, replica_groups={{0,8,16,24},{1,9,17,25},{2,10,18,26},{3,11,19,27},{32,40,48,56},{33,41,..., dimensions={0} | all-to-all | bytes 2097152 | tf_op jit(solution)/shard_map/all_to_all | solution.py:548
  125.8 0.3 reduce_sum.12
  126.1 14.5 %all_to_all.41.parts_ref = bf16[32,16,256]{2,1,0:T(8,128)(2,1)S(1)} all-to-all(bf16[32,16,256]{2,1,0:T(8,128)(2,1)S(1)} %bitcast.3), channel_id=1, replica_groups={{0,32,64,96,128,160,192,224,1,33,65,97,129,161,193,225,2,34,66,98,130,1..., dimensions={0} | all-to-all | bytes 524288 | tf_op jit(solution)/shard_map/all_to_all | solution.py:550
  140.6 0.6 finish.1
  (1 shorter events, 0.0 us)
Async XLA Ops:
  0.0 2.9 %collective-permute-start.1 = (bf16[8,128,256]{2,1,0:T(8,128)(2,1)}, bf16[8,128,256]{2,1,0:T(8,128)(2,1)S(1)}, u32[]{:S(2)}, u32[]{:S(2)}) collective-permute-start(bf16[8,128,256]{2,1,0:T(8,128)(2,1)} %k_ref.1), channel_id=1, source_target_pairs={{0,4},{4,0},{8,12},{12,8},{16,20},{20,16},{24,28},{28,24},{32,36},... | collective-permute-start | bytes 1572872 | tf_op jit(solution)/shard_map/ppermute | solution.py:62
  0.0 2.9 %collective-permute-start.2 = (bf16[8,128,256]{2,1,0:T(8,128)(2,1)}, bf16[8,128,256]{2,1,0:T(8,128)(2,1)S(1)}, u32[]{:S(2)}, u32[]{:S(2)}) collective-permute-start(bf16[8,128,256]{2,1,0:T(8,128)(2,1)} %v_ref.1), channel_id=1, source_target_pairs={{0,4},{4,0},{8,12},{12,8},{16,20},{20,16},{24,28},{28,24},{32,36},... | collective-permute-start | bytes 1572872 | tf_op jit(solution)/shard_map/ppermute | solution.py:62
  0.5 2.4 %collective-permute-start = (bf16[1,2,256]{2,1,0:T(2,128)(2,1)}, bf16[1,2,256]{2,1,0:T(2,128)(2,1)S(1)}, u32[]{:S(2)}, u32[]{:S(2)}) collective-permute-start(bf16[1,2,256]{2,1,0:T(2,128)(2,1)} %draft_hbm.1), channel_id=1, source_target_pairs={{0,4},{4,0},{8,12},{12,8},{16,20},{20,16},{24,28},{28,24},{32,36},... | collective-permute-start | bytes 3080 | tf_op jit(solution)/shard_map/ppermute | solution.py:62
  27.2 1.5 %collective-permute-start.3 = (bf16[32,32,128]{2,1,0:T(8,128)(2,1)S(1)}, bf16[32,32,128]{2,1,0:T(8,128)(2,1)S(1)}, u32[]{:S(2)}, u32[]{:S(2)}) collective-permute-start(bf16[32,32,128]{2,1,0:T(8,128)(2,1)S(1)} %all_to_all.35.own_ref), channel_id=1, source_target_pairs={{0,4},{4,0},{8,12},{12,8},{16,20},{20,16},{24,28},{28,24},{32,36},... | collective-permute-start | bytes 786440 | tf_op jit(solution)/shard_map/ppermute | solution.py:62
  28.8 40.2 %copy-start = (bf16[104,16384]{1,0:T(8,128)(2,1)S(1)}, bf16[104,16384]{1,0:T(8,128)(2,1)}, u32[]{:S(2)}) copy-start(bf16[104,16384]{1,0:T(8,128)(2,1)} %down_ref.1) | copy-start | bytes 10223620
  28.8 40.3 %copy-start.1 = (bf16[4096,256]{1,0:T(8,128)(2,1)S(1)}, bf16[4096,256]{1,0:T(8,128)(2,1)}, u32[]{:S(2)}) copy-start(bf16[4096,256]{1,0:T(8,128)(2,1)} %w_ref.1) | copy-start | bytes 6291460
  28.8 40.3 %copy-start.2 = (bf16[16,256]{1,0:T(8,128)(2,1)S(1)}, bf16[16,256]{1,0:T(8,128)(2,1)}, u32[]{:S(2)}) copy-start(bf16[16,256]{1,0:T(8,128)(2,1)} %stream_ref.1) | copy-start | bytes 24580
  31.8 76.0 %collective-permute-start.5 = (bf16[2,104,16384]{2,1,0:T(8,128)(2,1)}, bf16[2,104,16384]{2,1,0:T(8,128)(2,1)S(1)}, u32[]{:S(2)}, u32[]{:S(2)}) collective-permute-start(bf16[2,104,16384]{2,1,0:T(8,128)(2,1)} %gu_ref.1), channel_id=1, source_target_pairs={{0,4},{4,0},{8,12},{12,8},{16,20},{20,16},{24,28},{28,24},{32,36},... | collective-permute-start | bytes 20447240 | tf_op jit(solution)/shard_map/ppermute | solution.py:62
  50.5 57.3 %slice-start = ((s8[6815744]{0:T(1024)(128)(4,1)}), s8[4194304]{0:T(1024)(128)(4,1)S(1)}, s32[]{:S(2)}) async-start(s8[6815744]{0:T(1024)(128)(4,1)} %bitcast.1), calls=%async_computation.7 | async-start | bytes 8388608
  67.4 1.5 %collective-permute-start.4 = (bf16[32,32,128]{2,1,0:T(8,128)(2,1)S(1)}, bf16[32,32,128]{2,1,0:T(8,128)(2,1)S(1)}, u32[]{:S(2)}, u32[]{:S(2)}) collective-permute-start(bf16[32,32,128]{2,1,0:T(8,128)(2,1)S(1)} %all_to_all.37.own_ref), channel_id=1, source_target_pairs={{0,4},{4,0},{8,12},{12,8},{16,20},{20,16},{24,28},{28,24},{32,36},... | collective-permute-start | bytes 786440 | tf_op jit(solution)/shard_map/ppermute | solution.py:62
  69.0 41.3 %collective-permute-start.7 = (bf16[104,16384]{1,0:T(8,128)(2,1)S(1)}, bf16[104,16384]{1,0:T(8,128)(2,1)S(1)}, u32[]{:S(2)}, u32[]{:S(2)}) collective-permute-start(bf16[104,16384]{1,0:T(8,128)(2,1)S(1)} %copy-done), channel_id=1, source_target_pairs={{0,4},{4,0},{8,12},{12,8},{16,20},{20,16},{24,28},{28,24},{32,36},... | collective-permute-start | bytes 10223624 | tf_op jit(solution)/shard_map/ppermute | solution.py:62
  69.1 38.7 %slice-start.1 = ((s8[6815744]{0:T(1024)(128)(4,1)}), s8[2621440]{0:T(1024)(128)(4,1)S(1)}, s32[]{:S(2)}) async-start(s8[6815744]{0:T(1024)(128)(4,1)} %bitcast.1), calls=%async_computation.8 | async-start | bytes 5242880
  110.1 1.5 %collective-permute-start.6 = (f32[3,64,256]{2,1,0:T(8,128)S(1)}, f32[3,64,256]{2,1,0:T(8,128)S(1)}, u32[]{:S(2)}, u32[]{:S(2)}) collective-permute-start(f32[3,64,256]{2,1,0:T(8,128)S(1)} %gate.1.own_ref), channel_id=1, source_target_pairs={{0,4},{4,0},{8,12},{12,8},{16,20},{20,16},{24,28},{28,24},{32,36},... | collective-permute-start | bytes 589832 | tf_op jit(solution)/shard_map/ppermute | solution.py:62

commit v9 on v8

--- a/solution.py
+++ b/solution.py
@@ -476,6 +476,8 @@
     )
     own = swap_plane(block)
     oth = swap_cores(own)
+    oth, gate_up_sent = lax.optimization_barrier((oth, gate_up))
+    gate_up_pair = swap_cores(gate_up_sent)
     part, queries, slot_token, row_token = call(
         attention_kernel,
         "attention",
@@ -499,8 +501,6 @@
         extra,
         draft_pair,
     )
-    part, gate_up_sent = lax.optimization_barrier((part, gate_up))
-    gate_up_pair = swap_cores(gate_up_sent)
     attn, gains = call(
         combine_kernel,
         "combine",

time: 143 us -> 143 us (level)
  transfers between devices with their start and end apart: 8 -> 8, of which waited for: 4 -> 4; matrix products, arithmetic and copies ran while one was open for 0% -> 0% of each run, Pallas kernels for 4% -> 6%
where the time goes in v9:
time: 143 us; the launch traced here: 141 us
  blocking collectives  125 us (87%)
  Pallas kernels  10.1 us (7%)
  waiting for transfers between devices  5.11 us (4%)
    all_to_all x3, blocking collectives, swap_plane(): lax.all_to_all(array, 'kvp', 0, 0, axis_index_groups=G_XZ, tiled=True)  59 us
    all_to_all x1, blocking collectives, swap_face(): lax.all_to_all(array, ('kvp', 'tp'), 0, 0, axis_index_groups=G_XY, tiled=...  20.5 us
    all_to_all x1, blocking collectives, on_device(): lax.all_to_all(partial, ('kvp', 'tp'), 0, 0, axis_index_groups=G_YZ, tile...  17.3 us
    all_to_all x1, blocking collectives, on_device(): lax.all_to_all(summed, ('kvp', 'tp'), 0, 0, axis_index_groups=G_REST, til...  14.5 us
    all_to_all x1, blocking collectives, on_device(): lax.all_to_all(partial, ('kvp', 'tp'), 0, 0, axis_index_groups=G_LINE, ti...  13.3 us
    ppermute x8, waiting for transfers between devices, swap_cores(): return lax.ppermute(array, 'kvp', CORE_PAIRS)  5.11 us
    pallas_call x1, Pallas kernels, on_device(): call(attention_kernel, 'attention', [SMEM] + [VMEM] * 8, [shape((HEADS, R...  3.06 us
  transfers between devices with their start and end apart: 8, of which 4 were waited for; matrix products, arithmetic and copies ran while one was open for 0% of the time, Pallas kernels for 6%

profile of v9, /device:TPU:8, one launch (start us, length us, event | category | flops | bytes accessed | tf_op | source)
XLA Modules:
  0.0 141.2 jit_solution(11944590858450767080)
XLA Ops:
  0.0 0.0 collective-permute-start.1
  0.0 0.5 collective-permute-start.2
  0.5 0.0 collective-permute-start
  0.5 1.7 %prepare.1 = (bf16[32,32,128]{2,1,0:T(8,128)(2,1)S(1)}, bf16[4,128,256]{2,1,0:T(8,128)(2,1)S(1)}, bf16[4,128,256]{2,1,0:T(8,128)(2,1)S(1)}, f32[2,8,128]{2,1,0:T(8,128)S(1)}, s32[72]{0:T(128)S(1)}) custom-call(s32[32]{0:T(128)} %prompt_hbm.1, s32[8]{0:T(128)} %len_hbm.1, bf16[1,4096]{1,0:T(2,128)(2,1)} %query_hbm.1, bf16[1,2,256]{2,1,0:T(2,128)(2,1)} %draft_hbm.1, ...), custom_call_target="tpu_custom_call" | custom-call | tf_op jit(solution)/shard_map/prepare/pallas_call | solution.py:442
  2.3 0.6 collective-permute-done.draft2_ref
  2.9 0.0 collective-permute-done.1.k2_ref
  2.9 0.0 collective-permute-done.2.v2_ref
  2.9 24.3 %all_to_all.35.own_ref = bf16[32,32,128]{2,1,0:T(8,128)(2,1)S(1)} all-to-all(bf16[32,32,128]{2,1,0:T(8,128)(2,1)S(1)} %get-tuple-element.28), channel_id=1, replica_groups={{0,8,16,24,32,40,48,56,64,72,80,88,96,104,112,120,128,136,144,152,160,1..., dimensions={0} | all-to-all | bytes 524288 | tf_op jit(solution)/shard_map/all_to_all | solution.py:66
  27.2 0.0 collective-permute-start.3
  27.2 1.5 %collective-permute-done.3.oth_ref = bf16[32,32,128]{2,1,0:T(8,128)(2,1)S(1)} collective-permute-done((bf16[32,32,128]{2,1,0:T(8,128)(2,1)S(1)}, bf16[32,32,128]{2,1,0:T(8,128)(2,1)S(1)}, u32[]{:S(2)}, u32[]{:S(2)}) %collective-permute-start.3) | collective-permute-done | bytes 262176 | tf_op jit(solution)/shard_map/ppermute | solution.py:62
  28.8 0.1 collective-permute-start.5
  28.9 0.0 copy-start
  28.9 0.0 copy-start.1
  28.9 0.0 copy-start.2
  28.9 3.1 %attention.1 = (bf16[32,40,128]{2,1,0:T(8,128)(2,1)S(1)}, bf16[32,32,128]{2,1,0:T(8,128)(2,1)S(1)}, s32[32,128]{1,0:T(8,128)S(1)}, s32[8,128]{1,0:T(8,128)S(1)}) custom-call(s32[72]{0:T(128)S(1)} %get-tuple-element.26.order_ref, bf16[32,32,128]{2,1,0:T(8,128)(2,1)S(1)} %all_to_all.35.own_ref, bf16[32,32,128]{2,1,0:T(8,128)(2,1)S(1)} %collective-permute-done.3.oth_ref, ...), custom_call_target="tpu_custom_call" | custom-call | flops 1000000000 | bytes 40000000 | tf_op jit(solution)/shard_map/attention/pallas_call | solution.py:481
  32.0 18.5 %all_to_all.36.part_ref = bf16[32,40,128]{2,1,0:T(8,128)(2,1)S(1)} all-to-all(bf16[32,40,128]{2,1,0:T(8,128)(2,1)S(1)} %get-tuple-element.37), channel_id=1, replica_groups={{0,8,16,24,32,40,48,56,64,72,80,88,96,104,112,120,128,136,144,152,160,1..., dimensions={0} | all-to-all | bytes 655360 | tf_op jit(solution)/shard_map/all_to_all | solution.py:66
  50.4 0.0 slice-start
  50.4 0.7 combine.1
  51.2 16.2 %all_to_all.37.own_ref = bf16[32,32,128]{2,1,0:T(8,128)(2,1)S(1)} all-to-all(bf16[32,32,128]{2,1,0:T(8,128)(2,1)S(1)} %get-tuple-element.40), channel_id=1, replica_groups={{0,8,16,24,32,40,48,56,64,72,80,88,96,104,112,120,128,136,144,152,160,1..., dimensions={0} | all-to-all | bytes 524288 | tf_op jit(solution)/shard_map/all_to_all | solution.py:66
  67.3 0.0 collective-permute-start.4
  67.3 1.5 %collective-permute-done.4.oth_ref = bf16[32,32,128]{2,1,0:T(8,128)(2,1)S(1)} collective-permute-done((bf16[32,32,128]{2,1,0:T(8,128)(2,1)S(1)}, bf16[32,32,128]{2,1,0:T(8,128)(2,1)S(1)}, u32[]{:S(2)}, u32[]{:S(2)}) %collective-permute-start.4) | collective-permute-done | bytes 262176 | tf_op jit(solution)/shard_map/ppermute | solution.py:62
  68.9 0.0 copy-done
  68.9 0.1 collective-permute-start.7
  69.0 0.0 copy-done.1
  69.0 0.0 copy-done.2
  69.0 0.0 slice-start.1
  69.0 0.7 project.1
  69.8 17.3 %all_to_all.38.in_ref = bf16[32,16,256]{2,1,0:T(8,128)(2,1)S(1)} all-to-all(bf16[32,16,256]{2,1,0:T(8,128)(2,1)S(1)} %project.1), channel_id=1, replica_groups={{0,1,2,3,32,33,34,35,64,65,66,67,96,97,98,99,128,129,130,131,160,161,16..., dimensions={0} | all-to-all | bytes 524288 | tf_op jit(solution)/shard_map/all_to_all | solution.py:524
  87.1 0.1 spread.1
  87.2 20.5 %all_to_all.39.rows_ref = bf16[16,128,256]{2,1,0:T(8,128)(2,1)S(1)} all-to-all(bf16[16,128,256]{2,1,0:T(8,128)(2,1)S(1)} %get-tuple-element.43), channel_id=1, replica_groups={{0,1,2,3,8,9,10,11,16,17,18,19,24,25,26,27},{4,5,6,7,12,13,14,15,20,21,..., dimensions={0} | all-to-all | bytes 2097152 | tf_op jit(solution)/shard_map/all_to_all | solution.py:70
  107.7 0.0 collective-permute-done.5.gu2_ref
  107.7 0.0 slice-done
  107.7 0.0 slice-done.1
  107.8 2.3 %gate.1.own_ref = f32[3,64,256]{2,1,0:T(8,128)S(1)} custom-call(bf16[16,128,256]{2,1,0:T(8,128)(2,1)S(1)} %all_to_all.39.rows_ref, f32[32,256]{1,0:T(8,128)S(1)} %get-tuple-element.42.gain_ref, bf16[2,104,16384]{2,1,0:T(8,128)(2,1)S(1)} %bitcast.2, bf16[2,104,16384]{2,1,0:T(8,128)(2,1)S(1)} %collective-permute-done.5.gu2_ref), custom_call_target="tpu_custom_call" | custom-call | flops 1000000000 | bytes 40000000 | tf_op jit(solution)/shard_map/gate/pallas_call | solution.py:534
  110.0 0.1 collective-permute-start.6
  110.1 0.0 collective-permute-done.7.down2_ref
  110.2 1.4 %collective-permute-done.6.oth_ref = f32[3,64,256]{2,1,0:T(8,128)S(1)} collective-permute-done((f32[3,64,256]{2,1,0:T(8,128)S(1)}, f32[3,64,256]{2,1,0:T(8,128)S(1)}, u32[]{:S(2)}, u32[]{:S(2)}) %collective-permute-start.6) | collective-permute-done | bytes 196640 | tf_op jit(solution)/shard_map/ppermute | solution.py:62
  111.6 0.8 down.1
  112.4 13.3 %all_to_all.40 = bf16[4,512,256]{2,1,0:T(8,128)(2,1)S(1)} all-to-all(bf16[4,512,256]{2,1,0:T(8,128)(2,1)S(1)} %down.1), channel_id=1, replica_groups={{0,8,16,24},{1,9,17,25},{2,10,18,26},{3,11,19,27},{32,40,48,56},{33,41,..., dimensions={0} | all-to-all | bytes 2097152 | tf_op jit(solution)/shard_map/all_to_all | solution.py:548
  125.7 0.3 reduce_sum.12
  126.0 14.5 %all_to_all.41.parts_ref = bf16[32,16,256]{2,1,0:T(8,128)(2,1)S(1)} all-to-all(bf16[32,16,256]{2,1,0:T(8,128)(2,1)S(1)} %bitcast.3), channel_id=1, replica_groups={{0,32,64,96,128,160,192,224,1,33,65,97,129,161,193,225,2,34,66,98,130,1..., dimensions={0} | all-to-all | bytes 524288 | tf_op jit(solution)/shard_map/all_to_all | solution.py:550
  140.5 0.6 finish.1
  (1 shorter events, 0.0 us)
Async XLA Ops:
  0.0 2.9 %collective-permute-start.1 = (bf16[8,128,256]{2,1,0:T(8,128)(2,1)}, bf16[8,128,256]{2,1,0:T(8,128)(2,1)S(1)}, u32[]{:S(2)}, u32[]{:S(2)}) collective-permute-start(bf16[8,128,256]{2,1,0:T(8,128)(2,1)} %k_ref.1), channel_id=1, source_target_pairs={{0,4},{4,0},{8,12},{12,8},{16,20},{20,16},{24,28},{28,24},{32,36},... | collective-permute-start | bytes 1572872 | tf_op jit(solution)/shard_map/ppermute | solution.py:62
  0.0 2.9 %collective-permute-start.2 = (bf16[8,128,256]{2,1,0:T(8,128)(2,1)}, bf16[8,128,256]{2,1,0:T(8,128)(2,1)S(1)}, u32[]{:S(2)}, u32[]{:S(2)}) collective-permute-start(bf16[8,128,256]{2,1,0:T(8,128)(2,1)} %v_ref.1), channel_id=1, source_target_pairs={{0,4},{4,0},{8,12},{12,8},{16,20},{20,16},{24,28},{28,24},{32,36},... | collective-permute-start | bytes 1572872 | tf_op jit(solution)/shard_map/ppermute | solution.py:62
  0.5 2.4 %collective-permute-start = (bf16[1,2,256]{2,1,0:T(2,128)(2,1)}, bf16[1,2,256]{2,1,0:T(2,128)(2,1)S(1)}, u32[]{:S(2)}, u32[]{:S(2)}) collective-permute-start(bf16[1,2,256]{2,1,0:T(2,128)(2,1)} %draft_hbm.1), channel_id=1, source_target_pairs={{0,4},{4,0},{8,12},{12,8},{16,20},{20,16},{24,28},{28,24},{32,36},... | collective-permute-start | bytes 3080 | tf_op jit(solution)/shard_map/ppermute | solution.py:62
  27.2 1.5 %collective-permute-start.3 = (bf16[32,32,128]{2,1,0:T(8,128)(2,1)S(1)}, bf16[32,32,128]{2,1,0:T(8,128)(2,1)S(1)}, u32[]{:S(2)}, u32[]{:S(2)}) collective-permute-start(bf16[32,32,128]{2,1,0:T(8,128)(2,1)S(1)} %all_to_all.35.own_ref), channel_id=1, source_target_pairs={{0,4},{4,0},{8,12},{12,8},{16,20},{20,16},{24,28},{28,24},{32,36},... | collective-permute-start | bytes 786440 | tf_op jit(solution)/shard_map/ppermute | solution.py:62
  28.8 79.0 %collective-permute-start.5 = (bf16[2,104,16384]{2,1,0:T(8,128)(2,1)}, bf16[2,104,16384]{2,1,0:T(8,128)(2,1)S(1)}, u32[]{:S(2)}, u32[]{:S(2)}) collective-permute-start(bf16[2,104,16384]{2,1,0:T(8,128)(2,1)} %gu_ref.1), channel_id=1, source_target_pairs={{0,4},{4,0},{8,12},{12,8},{16,20},{20,16},{24,28},{28,24},{32,36},... | collective-permute-start | bytes 20447240 | tf_op jit(solution)/shard_map/ppermute | solution.py:62
  28.9 40.0 %copy-start = (bf16[104,16384]{1,0:T(8,128)(2,1)S(1)}, bf16[104,16384]{1,0:T(8,128)(2,1)}, u32[]{:S(2)}) copy-start(bf16[104,16384]{1,0:T(8,128)(2,1)} %down_ref.1) | copy-start | bytes 10223620
  28.9 40.1 %copy-start.1 = (bf16[4096,256]{1,0:T(8,128)(2,1)S(1)}, bf16[4096,256]{1,0:T(8,128)(2,1)}, u32[]{:S(2)}) copy-start(bf16[4096,256]{1,0:T(8,128)(2,1)} %w_ref.1) | copy-start | bytes 6291460
  28.9 40.1 %copy-start.2 = (bf16[16,256]{1,0:T(8,128)(2,1)S(1)}, bf16[16,256]{1,0:T(8,128)(2,1)}, u32[]{:S(2)}) copy-start(bf16[16,256]{1,0:T(8,128)(2,1)} %stream_ref.1) | copy-start | bytes 24580
  50.4 57.3 %slice-start = ((s8[6815744]{0:T(1024)(128)(4,1)}), s8[4194304]{0:T(1024)(128)(4,1)S(1)}, s32[]{:S(2)}) async-start(s8[6815744]{0:T(1024)(128)(4,1)} %bitcast.1), calls=%async_computation.7 | async-start | bytes 8388608
  67.3 1.5 %collective-permute-start.4 = (bf16[32,32,128]{2,1,0:T(8,128)(2,1)S(1)}, bf16[32,32,128]{2,1,0:T(8,128)(2,1)S(1)}, u32[]{:S(2)}, u32[]{:S(2)}) collective-permute-start(bf16[32,32,128]{2,1,0:T(8,128)(2,1)S(1)} %all_to_all.37.own_ref), channel_id=1, source_target_pairs={{0,4},{4,0},{8,12},{12,8},{16,20},{20,16},{24,28},{28,24},{32,36},... | collective-permute-start | bytes 786440 | tf_op jit(solution)/shard_map/ppermute | solution.py:62
  68.9 41.3 %collective-permute-start.7 = (bf16[104,16384]{1,0:T(8,128)(2,1)S(1)}, bf16[104,16384]{1,0:T(8,128)(2,1)S(1)}, u32[]{:S(2)}, u32[]{:S(2)}) collective-permute-start(bf16[104,16384]{1,0:T(8,128)(2,1)S(1)} %copy-done), channel_id=1, source_target_pairs={{0,4},{4,0},{8,12},{12,8},{16,20},{20,16},{24,28},{28,24},{32,36},... | collective-permute-start | bytes 10223624 | tf_op jit(solution)/shard_map/ppermute | solution.py:62
  69.0 38.7 %slice-start.1 = ((s8[6815744]{0:T(1024)(128)(4,1)}), s8[2621440]{0:T(1024)(128)(4,1)S(1)}, s32[]{:S(2)}) async-start(s8[6815744]{0:T(1024)(128)(4,1)} %bitcast.1), calls=%async_computation.8 | async-start | bytes 5242880
  110.0 1.5 %collective-permute-start.6 = (f32[3,64,256]{2,1,0:T(8,128)S(1)}, f32[3,64,256]{2,1,0:T(8,128)S(1)}, u32[]{:S(2)}, u32[]{:S(2)}) collective-permute-start(f32[3,64,256]{2,1,0:T(8,128)S(1)} %gate.1.own_ref), channel_id=1, source_target_pairs={{0,4},{4,0},{8,12},{12,8},{16,20},{20,16},{24,28},{28,24},{32,36},... | collective-permute-start | bytes 589832 | tf_op jit(solution)/shard_map/ppermute | solution.py:62
